TPU v7x, 32 devices: a whole 2x2x4 slice. The times are simulated.
32 devices in a mesh: dp: 8 (over y, x, core), state: 4 (over z).
Axes of the slice: x: 2, y: 2, z: 4, core: 2. Of those that a mesh axis runs over, the one named last changes fastest.
Arguments:
- tokens: bfloat16 [8, 2, 512, 1024], P('dp', None, 'state'), may hold values from -32 to 32
- carried_state: float32 [8, 512, 1024], P('dp', 'state'), may hold values from -6 to 6
- past_keys: bfloat16 [8, 512, 2, 1024], P('dp', None, None, 'state'), may hold values from -6 to 6
- fresh_start: int32 [8], P('dp'), may hold values 0 or 1
- valid_count: int32 [8], P('dp'), may hold values from 128 to 1024, as said below
- bucket_ids: int32 [512], replicated, may hold values from 0 to 31
- grad_output: bfloat16 [8, 2, 512, 1024], P('dp', None, 'state'), may hold values from -6 to 6
- grad_state: float32 [8, 512, 1024], P('dp', 'state'), may hold values from -6 to 6
- norm_gains: float32 [3, 1024], replicated, may hold values from 0.5 to 1.5
- token_qkv: bfloat16 [1024, 3, 1024], P('dp', None, 'state'), may hold values from -0.1875 to 0.1875
- token_out: bfloat16 [1024, 1024], P('dp', 'state'), may hold values from -3 to 3
- bias_table: float32 [32, 8], P(None, 'state'), may hold values from -4 to 4
- mlp_up: bfloat16 [1024, 4096], P('dp', 'state'), may hold values from -0.1875 to 0.1875
- mlp_down: bfloat16 [1024, 4096], P('dp', 'state'), may hold values from -0.09375 to 0.09375
- state_qkv: bfloat16 [1024, 3, 1024], P('dp', None, 'state'), may hold values from -0.1875 to 0.1875
- state_gates: bfloat16 [1024, 3, 1024], P('dp'), may hold values from -3 to 3
- initial_state: bfloat16 [512, 1024], P('state', 'dp'), may hold values from -6 to 6
Outputs:
- block_out: bfloat16 [8, 2, 512, 1024], P('dp', None, 'state')
- state_out: float32 [8, 512, 1024], P('dp', 'state')
- rms_stats: float32 [3], replicated
- tokens_grad: bfloat16 [8, 2, 512, 1024], P('dp', None, 'state')
- carried_grad: float32 [8, 512, 1024], P('dp', 'state')
- past_grad: float32 [8, 512, 2, 1024], P('dp', None, None, 'state')
- gains_grad: float32 [3, 1024], P(None, ('dp', 'state'))
- token_qkv_grad: float32 [1024, 3, 1024], P('dp', None, 'state')
- token_out_grad: float32 [1024, 1024], P('dp', 'state')
- table_grad: float32 [32, 8], P('dp', 'state')
- mlp_up_grad: float32 [1024, 4096], P('dp', 'state')
- mlp_down_grad: float32 [1024, 4096], P('dp', 'state')
- state_qkv_grad: float32 [1024, 3, 1024], P('dp', None, 'state')
- state_gates_grad: float32 [1024, 3, 1024], P(('dp', 'state'))
- initial_grad: float32 [512, 1024], P('state', 'dp')
Inputs may be any that keep to these rules, and one draw needn't show every extreme that they name: `fresh_start`: 1 marks an item that begins a segment: it starts from initial_state and has no valid previous keys. `valid_count`: some item is wholly valid and some item has 128 valid tokens. `bucket_ids`: bucket of each distance from 0 to 511.
All inputs are finite; a program needn't handle non-finite values. No bound on the sum of `fresh_start` on one device may be relied on, other than what follows from the above.
Results may differ from a plain program's by a relative error of at most 0.04.
Values may be sent and summed in bfloat16 or wider, within the bound.
A program may use at most 576 MiB of HBM per device.

v0:
```python
import math

import jax
import jax.numpy as jnp
from jax import lax
from jax.sharding import PartitionSpec as P

DH = 128


EPS = 1e-06
NEGATIVE = -1e30
HIGHEST = lax.Precision.HIGHEST


def rms_norm(tensor, gains_row):
    return tensor * lax.rsqrt(jnp.mean(tensor * tensor, axis=-1, keepdims=True) + EPS) * gains_row


def norm_back(tensor, gains_row, cotangent):
    return jax.vjp(rms_norm, tensor, gains_row)[1](cotangent)


def smooth_gelu(tensor):
    return jax.nn.gelu(tensor, approximate=True)


def renew_state(state_now, gate_values):
    return state_now * jax.nn.sigmoid(gate_values[2] + 1.0) + jnp.tanh(
        gate_values[0]
    ) * jax.nn.sigmoid(gate_values[1] - 1.0)


def split_heads(tensor):
    return tensor.reshape(tensor.shape[0], tensor.shape[1], tensor.shape[2] // DH, DH)


def merge_heads(tensor):
    return tensor.reshape(tensor.shape[0], tensor.shape[1], tensor.shape[2] * DH)


def score_grid(queries, key_rows, bias_add, allowed):
    scores = jnp.einsum(
        "iqhd,ikhd->ihqk", queries, key_rows, preferred_element_type=jnp.float32
    ) / math.sqrt(DH)
    if bias_add is not None:
        scores = scores + bias_add[None]
    return jnp.where(allowed[:, None], scores, NEGATIVE)


def attend_forward(queries, key_rows, values, bias_add, allowed):
    scores = score_grid(queries, key_rows, bias_add, allowed)
    row_max = jnp.max(scores, axis=-1, keepdims=True)
    weights = jnp.exp(scores - row_max)
    row_total = jnp.sum(weights, axis=-1, keepdims=True)
    attn_probs = (weights / row_total).astype(jnp.bfloat16)
    mixed_heads = jnp.einsum(
        "ihqk,ikhd->iqhd", attn_probs, values, preferred_element_type=jnp.float32
    )
    return (merge_heads(mixed_heads.astype(jnp.bfloat16)), row_max + jnp.log(row_total))


def attention_backward_pass(queries, key_rows, values, bias_add, allowed, log_total, grad_mixed):
    scores = score_grid(queries, key_rows, bias_add, allowed)
    attn_probs = jnp.exp(scores - log_total)
    probs_grad = jnp.einsum(
        "iqhd,ikhd->ihqk", grad_mixed, values, preferred_element_type=jnp.float32
    )
    scores_grad = attn_probs * (
        probs_grad - jnp.sum(attn_probs * probs_grad, axis=-1, keepdims=True)
    )
    scores_grad = scores_grad.astype(jnp.bfloat16)
    values_grad = jnp.einsum(
        "ihqk,iqhd->ikhd",
        attn_probs.astype(jnp.bfloat16),
        grad_mixed,
        preferred_element_type=jnp.float32,
    )
    queries_grad = jnp.einsum(
        "ihqk,ikhd->iqhd", scores_grad, key_rows, preferred_element_type=jnp.float32
    ) / math.sqrt(DH)
    keys_grad = jnp.einsum(
        "ihqk,iqhd->ikhd", scores_grad, queries, preferred_element_type=jnp.float32
    ) / math.sqrt(DH)
    return (
        merge_heads(queries_grad),
        merge_heads(keys_grad),
        merge_heads(values_grad),
        scores_grad,
    )


def diagonal_sums(grid_values):
    num_heads, num_rows, num_cols = grid_values.shape
    flipped = grid_values[:, :, ::-1]
    padded = jnp.pad(flipped, ((0, 0), (0, 0), (0, 1)))
    sheared = padded.reshape(num_heads, num_rows * (num_cols + 1))[:, : num_rows * num_cols]
    sheared = sheared.reshape(num_heads, num_rows, num_cols)
    return jnp.sum(sheared, axis=1)[:, num_rows - 1 : num_cols - 1]


def sum_rows(partial_value):
    return lax.psum_scatter(
        partial_value.astype(jnp.bfloat16), "state", scatter_dimension=1, tiled=True
    ).astype(jnp.float32)


def whole_rows(partial_value):
    return lax.all_gather(partial_value, "state", axis=1, tiled=True)


def shards(
    tokens,
    carried_state,
    past_keys,
    fresh_start,
    valid_count,
    bucket_ids,
    grad_output,
    grad_state,
    norm_gains,
    token_qkv,
    token_out,
    bias_table,
    mlp_up,
    mlp_down,
    state_qkv,
    state_gates,
    initial_state,
):
    item_count, blocks, share_rows, model_width = tokens.shape
    groups = lax.axis_size("state")
    state_rank = lax.axis_index("state")
    window_width = share_rows * groups
    vector_rows = carried_state.shape[1] * groups
    local_width = token_qkv.shape[2]
    qkv_full, out_full, up_full, down_full, sqkv_full, gates_full, initial_full = (
        lax.all_gather(token_qkv, "dp", axis=0, tiled=True),
        lax.all_gather(token_out, "dp", axis=0, tiled=True),
        lax.all_gather(mlp_up, "dp", axis=0, tiled=True),
        lax.all_gather(mlp_down, "dp", axis=0, tiled=True),
        lax.all_gather(state_qkv, "dp", axis=0, tiled=True),
        lax.all_gather(state_gates, "dp", axis=0, tiled=True),
        lax.all_gather(initial_state, "dp", axis=1, tiled=True),
    )
    gates_used = lax.dynamic_slice_in_dim(gates_full, state_rank * local_width, local_width, 2)
    one_hot = (bucket_ids[:, None] == jnp.arange(bias_table.shape[0])[None, :]).astype(jnp.float32)
    per_offset = jnp.dot(one_hot, bias_table, precision=HIGHEST)
    query_pos = jnp.arange(window_width)[:, None]
    key_pos = jnp.arange(2 * window_width)[None, :]
    offset = window_width + query_pos - key_pos
    inside = (offset >= 0) & (offset < window_width)
    bias_grid = jnp.transpose(
        jnp.take(per_offset, jnp.clip(offset, 0, window_width - 1), axis=0), (2, 0, 1)
    )
    token_bias = jnp.pad(bias_grid, ((0, 0), (0, 0), (0, vector_rows)))
    is_fresh = fresh_start == 1
    state_now = jnp.where(
        is_fresh[:, None, None], initial_full.astype(jnp.float32)[None], carried_state
    )
    past_key = past_keys[:, :, 0]
    past_value = past_keys[:, :, 1]
    past_ok = jnp.broadcast_to(~is_fresh[:, None], (item_count, window_width))
    gains_token, gains_middle, gains_state = (norm_gains[0], norm_gains[1], norm_gains[2])
    share_pos = state_rank * share_rows + jnp.arange(share_rows)
    square_sums = jnp.zeros((3,), jnp.float32)
    valid_total = jnp.zeros((), jnp.float32)
    kept_values = []
    results = []
    for block_at in range(blocks):
        token_ok = (
            block_at * window_width + jnp.arange(window_width)[None, :] < valid_count[:, None]
        )
        inputs = tokens[:, block_at].astype(jnp.float32)
        normed, state_normed = (
            lax.all_gather(
                rms_norm(inputs, gains_token).astype(jnp.bfloat16), "state", axis=1, tiled=True
            ),
            lax.all_gather(
                rms_norm(state_now, gains_state).astype(jnp.bfloat16), "state", axis=1, tiled=True
            ),
        )
        project = jnp.einsum(
            "iwd,dch->ciwh", normed, qkv_full, preferred_element_type=jnp.float32
        ).astype(jnp.bfloat16)
        state_project = jnp.einsum(
            "ind,dch->cinh", state_normed, sqkv_full, preferred_element_type=jnp.float32
        ).astype(jnp.bfloat16)
        token_keys = jnp.concatenate([past_key, project[1], state_project[1]], axis=1)
        token_values = jnp.concatenate([past_value, project[2], state_project[2]], axis=1)
        window_ok = inside[None] & jnp.concatenate([past_ok, token_ok], axis=1)[:, None, :]
        token_allowed = jnp.concatenate(
            [window_ok, jnp.ones((item_count, window_width, vector_rows), jnp.bool_)], axis=2
        )
        mixed_heads, token_total = attend_forward(
            split_heads(project[0]),
            split_heads(token_keys),
            split_heads(token_values),
            token_bias,
            token_allowed,
        )
        branch = sum_rows(
            jnp.einsum("iwh,dh->iwd", mixed_heads, out_full, preferred_element_type=jnp.float32)
        )
        middle = inputs + branch
        middle_normed = lax.all_gather(
            rms_norm(middle, gains_middle).astype(jnp.bfloat16), "state", axis=1, tiled=True
        )
        up_values = jnp.einsum(
            "iwd,df->iwf", middle_normed, up_full, preferred_element_type=jnp.float32
        )
        hidden = smooth_gelu(up_values).astype(jnp.bfloat16)
        feed_out = sum_rows(
            jnp.einsum("iwf,df->iwd", hidden, down_full, preferred_element_type=jnp.float32)
        )
        result = middle + feed_out
        results.append(result.astype(jnp.bfloat16))
        share_ok = (block_at * window_width + share_pos[None, :] < valid_count[:, None]).astype(
            jnp.float32
        )[:, :, None]
        square_sums = square_sums + jnp.stack(
            [
                jnp.sum(share_ok * result * result),
                jnp.sum(share_ok * branch * branch),
                jnp.sum(share_ok * feed_out * feed_out),
            ]
        )
        valid_total = valid_total + jnp.sum(share_ok)
        state_keys = jnp.concatenate([state_project[1], project[1]], axis=1)
        state_values = jnp.concatenate([state_project[2], project[2]], axis=1)
        state_allowed = jnp.concatenate(
            [
                jnp.ones((item_count, vector_rows, vector_rows), jnp.bool_),
                jnp.broadcast_to(token_ok[:, None, :], (item_count, vector_rows, window_width)),
            ],
            axis=2,
        )
        state_mixed, state_total = attend_forward(
            split_heads(state_project[0]),
            split_heads(state_keys),
            split_heads(state_values),
            None,
            state_allowed,
        )
        gate_source = state_mixed
        gate_values = lax.psum_scatter(
            jnp.einsum(
                "inh,dch->cind", state_mixed, gates_used, preferred_element_type=jnp.float32
            ).astype(jnp.bfloat16),
            "state",
            scatter_dimension=2,
            tiled=True,
        ).astype(jnp.float32)
        kept_values.append(
            (
                inputs,
                normed,
                state_normed,
                project,
                state_project,
                token_keys,
                token_values,
                token_allowed,
                mixed_heads,
                token_total,
                middle,
                middle_normed,
                up_values,
                hidden,
                state_keys,
                state_values,
                state_allowed,
                state_total,
                gate_source,
                gate_values,
                state_now,
            )
        )
        state_now = renew_state(state_now, gate_values)
        past_key, past_value, past_ok = (project[1], project[2], token_ok)
    square_sums, valid_total = lax.psum((square_sums, valid_total), ("dp", "state"))
    rms_stats = jnp.sqrt(square_sums / valid_total)
    qkv_grad = jnp.zeros(qkv_full.shape, jnp.float32)
    out_grad = jnp.zeros(out_full.shape, jnp.float32)
    up_grad = jnp.zeros(up_full.shape, jnp.float32)
    down_grad = jnp.zeros(down_full.shape, jnp.float32)
    sqkv_grad = jnp.zeros(sqkv_full.shape, jnp.float32)
    gate_grad = jnp.zeros(gates_used.shape, jnp.float32)
    bias_grad = jnp.zeros(bias_grid.shape, jnp.float32)
    gain_token_grad = jnp.zeros((model_width,), jnp.float32)
    gain_middle_grad = jnp.zeros((model_width,), jnp.float32)
    gain_state_grad = jnp.zeros((model_width,), jnp.float32)
    state_grad = grad_state
    carried_key_rows = jnp.zeros(past_keys[:, :, 0].shape, jnp.float32)
    carry_value = jnp.zeros(past_keys[:, :, 0].shape, jnp.float32)
    token_grads = [None] * blocks
    for block_at in reversed(range(blocks)):
        (
            inputs,
            normed,
            state_normed,
            project,
            state_project,
            token_keys,
            token_values,
            token_allowed,
            mixed_heads,
            token_total,
            middle,
            middle_normed,
            up_values,
            hidden,
            state_keys,
            state_values,
            state_allowed,
            state_total,
            gate_source,
            gate_values,
            state_before,
        ) = kept_values[block_at]
        direct_grad, gates_grad = jax.vjp(renew_state, state_before, gate_values)[1](state_grad)
        gates_low = gates_grad.astype(jnp.bfloat16)
        gates_rows = lax.all_gather(gates_low, "state", axis=2, tiled=True)
        state_mixed_grad = jnp.einsum(
            "cind,dch->inh", gates_rows, gates_used, preferred_element_type=jnp.float32
        ).astype(jnp.bfloat16)
        gate_grad = gate_grad + jnp.einsum(
            "inh,cind->dch", gate_source, gates_rows, preferred_element_type=jnp.float32
        )
        state_query_gradient, state_keys_gradient, state_values_gradient, discarded_output = (
            attention_backward_pass(
                split_heads(state_project[0]),
                split_heads(state_keys),
                split_heads(state_values),
                None,
                state_allowed,
                state_total,
                split_heads(state_mixed_grad),
            )
        )
        out_share = grad_output[:, block_at]
        out_whole = whole_rows(out_share)
        down_grad = down_grad + jnp.einsum(
            "iwf,iwd->df", hidden, out_whole, preferred_element_type=jnp.float32
        )
        hidden_grad = jnp.einsum(
            "iwd,df->iwf", out_whole, down_full, preferred_element_type=jnp.float32
        )
        up_values_grad = jax.vjp(smooth_gelu, up_values)[1](hidden_grad)[0].astype(jnp.bfloat16)
        up_grad = up_grad + jnp.einsum(
            "iwd,iwf->df", middle_normed, up_values_grad, preferred_element_type=jnp.float32
        )
        middle_normed_grad = lax.psum_scatter(
            jnp.einsum(
                "iwf,df->iwd", up_values_grad, up_full, preferred_element_type=jnp.float32
            ).astype(jnp.bfloat16),
            "state",
            scatter_dimension=1,
            tiled=True,
        ).astype(jnp.float32)
        middle_grad, gain_part = norm_back(middle, gains_middle, middle_normed_grad)
        middle_grad = out_share.astype(jnp.float32) + middle_grad
        gain_middle_grad = gain_middle_grad + gain_part
        branch_whole = whole_rows(middle_grad.astype(jnp.bfloat16))
        out_grad = out_grad + jnp.einsum(
            "iwh,iwd->dh", mixed_heads, branch_whole, preferred_element_type=jnp.float32
        )
        mixed_grad = jnp.einsum(
            "iwd,dh->iwh", branch_whole, out_full, preferred_element_type=jnp.float32
        ).astype(jnp.bfloat16)
        query_grad, token_keys_gradient, tvalues_grad, scores_grad = attention_backward_pass(
            split_heads(project[0]),
            split_heads(token_keys),
            split_heads(token_values),
            token_bias,
            token_allowed,
            token_total,
            split_heads(mixed_grad),
        )
        bias_grad = bias_grad + jnp.sum(
            scores_grad[:, :, :, : 2 * window_width].astype(jnp.float32), axis=0
        )
        key_gradient_rows = (
            token_keys_gradient[:, window_width : 2 * window_width]
            + state_keys_gradient[:, vector_rows:]
            + carried_key_rows
        )
        value_grad = (
            tvalues_grad[:, window_width : 2 * window_width]
            + state_values_gradient[:, vector_rows:]
            + carry_value
        )
        state_key_gradient = (
            token_keys_gradient[:, 2 * window_width :] + state_keys_gradient[:, :vector_rows]
        )
        state_value_gradient = (
            tvalues_grad[:, 2 * window_width :] + state_values_gradient[:, :vector_rows]
        )
        project_grad = jnp.stack([query_grad, key_gradient_rows, value_grad]).astype(jnp.bfloat16)
        state_projection_gradient = jnp.stack(
            [state_query_gradient, state_key_gradient, state_value_gradient]
        ).astype(jnp.bfloat16)
        qkv_grad = qkv_grad + jnp.einsum(
            "iwd,ciwh->dch", normed, project_grad, preferred_element_type=jnp.float32
        )
        sqkv_grad = sqkv_grad + jnp.einsum(
            "ind,cinh->dch",
            state_normed,
            state_projection_gradient,
            preferred_element_type=jnp.float32,
        )
        normed_grad, state_normed_grad = (
            lax.psum_scatter(
                jnp.einsum(
                    "ciwh,dch->iwd", project_grad, qkv_full, preferred_element_type=jnp.float32
                ).astype(jnp.bfloat16),
                "state",
                scatter_dimension=1,
                tiled=True,
            ).astype(jnp.float32),
            lax.psum_scatter(
                jnp.einsum(
                    "cinh,dch->ind",
                    state_projection_gradient,
                    sqkv_full,
                    preferred_element_type=jnp.float32,
                ).astype(jnp.bfloat16),
                "state",
                scatter_dimension=1,
                tiled=True,
            ).astype(jnp.float32),
        )
        input_grad, gain_part = norm_back(inputs, gains_token, normed_grad)
        gain_token_grad = gain_token_grad + gain_part
        token_grads[block_at] = (middle_grad + input_grad).astype(jnp.bfloat16)
        state_norm_grad, gain_part = norm_back(state_before, gains_state, state_normed_grad)
        gain_state_grad = gain_state_grad + gain_part
        state_grad = direct_grad + state_norm_grad
        carried_key_rows = token_keys_gradient[:, :window_width]
        carry_value = tvalues_grad[:, :window_width]
    carried_grad = jnp.where(is_fresh[:, None, None], 0.0, state_grad)
    initial_part = jnp.sum(jnp.where(is_fresh[:, None, None], state_grad, 0.0), axis=0)
    past_grad = jnp.stack([carried_key_rows, carry_value], axis=2)
    table_part = jnp.dot(one_hot.T, diagonal_sums(bias_grad).T, precision=HIGHEST)
    gain_columns = jnp.stack([gain_token_grad, gain_middle_grad, gain_state_grad], axis=1)
    summed = (
        lax.psum_scatter(
            qkv_grad.astype(jnp.bfloat16), "dp", scatter_dimension=0, tiled=True
        ).astype(jnp.float32),
        lax.psum_scatter(
            out_grad.astype(jnp.bfloat16), "dp", scatter_dimension=0, tiled=True
        ).astype(jnp.float32),
        lax.psum_scatter(
            table_part.astype(jnp.bfloat16), "dp", scatter_dimension=0, tiled=True
        ).astype(jnp.float32),
        lax.psum_scatter(
            up_grad.astype(jnp.bfloat16), "dp", scatter_dimension=0, tiled=True
        ).astype(jnp.float32),
        lax.psum_scatter(
            down_grad.astype(jnp.bfloat16), "dp", scatter_dimension=0, tiled=True
        ).astype(jnp.float32),
        lax.psum_scatter(
            sqkv_grad.astype(jnp.bfloat16), "dp", scatter_dimension=0, tiled=True
        ).astype(jnp.float32),
        lax.psum_scatter(
            initial_part.astype(jnp.bfloat16), "dp", scatter_dimension=1, tiled=True
        ).astype(jnp.float32),
        lax.psum_scatter(
            gate_grad.astype(jnp.bfloat16), "dp", scatter_dimension=0, tiled=True
        ).astype(jnp.float32),
        lax.psum_scatter(
            gain_columns.astype(jnp.bfloat16), "dp", scatter_dimension=0, tiled=True
        ).astype(jnp.float32),
    )
    gate_pieces, gain_pieces = (
        lax.all_to_all(
            summed[7][:, :, None, :].astype(jnp.bfloat16),
            "state",
            split_axis=0,
            concat_axis=2,
            tiled=True,
        ).astype(jnp.float32),
        lax.all_to_all(
            summed[8][:, :, None, None].astype(jnp.bfloat16),
            "state",
            split_axis=0,
            concat_axis=2,
            tiled=True,
        ).astype(jnp.float32),
    )
    gains_grad = jnp.sum(gain_pieces, axis=(2, 3)).T
    gates_grad_out = gate_pieces.reshape(
        gate_pieces.shape[0], gate_pieces.shape[1], gate_pieces.shape[2] * gate_pieces.shape[3]
    )
    return (
        jnp.stack(results, axis=1),
        state_now,
        rms_stats,
        jnp.stack(token_grads, axis=1),
        carried_grad,
        past_grad,
        gains_grad,
        summed[0],
        summed[1],
        summed[2],
        summed[3],
        summed[4],
        summed[5],
        gates_grad_out,
        summed[6],
    )


def solution(mesh):
    in_specs = (
        P("dp", None, "state", None),
        P("dp", "state", None),
        P("dp", None, None, "state"),
        P("dp"),
        P("dp"),
        P(),
        P("dp", None, "state", None),
        P("dp", "state", None),
        P(),
        P("dp", None, "state"),
        P("dp", "state"),
        P(None, "state"),
        P("dp", "state"),
        P("dp", "state"),
        P("dp", None, "state"),
        P("dp", None, None),
        P("state", "dp"),
    )
    out_specs = (
        P("dp", None, "state", None),
        P("dp", "state", None),
        P(),
        P("dp", None, "state", None),
        P("dp", "state", None),
        P("dp", None, None, "state"),
        P(None, ("dp", "state")),
        P("dp", None, "state"),
        P("dp", "state"),
        P("dp", "state"),
        P("dp", "state"),
        P("dp", "state"),
        P("dp", None, "state"),
        P(("dp", "state"), None, None),
        P("state", "dp"),
    )
    return jax.shard_map(shards, mesh=mesh, in_specs=in_specs, out_specs=out_specs, check_vma=False)
```

profile of v0, /device:TPU:0, one launch (start us, length us, event | category | flops | bytes accessed | tf_op | source)
XLA Modules:
  0.0 3353.0 jit_solution(8843623085748592164)
XLA Ops:
  43.3 27.9 all-gather.22.cloned.1.call-done
  74.8 26.5 all-gather.24.cloned.1.call-done
  101.3 27.7 all-gather.26.cloned.1.call-done
  137.3 39.0 %all-gather.36.cloned.1.call-done = bf16[1024,3,1024]{2,0,1:T(8,128)(2,1)} async-done(((bf16[128,3,1024]{2,0,1:T(8,128)(2,1)}), bf16[1024,3,1024]{2,0,1:T(8,128)(2,1)}) %all-gather.36.cloned.1.call-update) | async-done | bytes 6291472 | tf_op jit(solution)/shard_map/all_gather | solution.py:143
  182.4 1889.1 %gather_fusion = f32[524288,2]{1,0:T(8,128)} fusion(f32[512,2]{1,0:T(8,128)S(1)} %fusion.246, s32[524288]{0:T(1024)} %broadcast_clamp_fusion), kind=kCustom, calls=%fused_computation | custom fusion | bytes 10485760 | tf_op jit(solution)/shard_map/jit(_take)/gather | solution.py:154
  2071.5 139.5 %copy.476 = f32[512,1024,2]{1,0,2:T(8,128)} copy(f32[512,1024,2]{2,1,0:T(8,128)} %bitcast.32) | data formatting | bytes 8388608 | tf_op jit(solution)/shard_map/jit(_take)/gather | solution.py:154
  2300.4 28.0 reduce-scatter.34.cloned.1.call-done
  2356.9 30.0 all-gather.40.cloned.1.call-done
  2391.4 25.1 all-gather.52.cloned.1.call-done
  2416.5 29.2 all-gather.32.cloned.1.call-done
  2534.4 28.1 reduce-scatter.36.cloned.1.call-done
  2562.5 28.1 reduce-scatter.30.cloned.1.call-done
  2590.6 28.1 reduce-scatter.40.cloned.1.call-done
  2623.5 56.4 %reduce-scatter.38.cloned.1.call-done = bf16[3,1,128,1024]{3,2,1,0:T(8,128)(2,1)} async-done(((bf16[3,1,512,1024]{3,2,1,0:T(8,128)(2,1)}), bf16[3,1,128,1024]{3,2,1,0:T(8,128)(2,1)}) %reduce-scatter.38.cloned.1.call-update) | async-done | bytes 786448 | tf_op jit(solution)/shard_map/reduce_scatter | solution.py:246
  2730.2 45.0 %all-gather.44.cloned.1.call-done = bf16[3,1,512,1024]{3,2,1,0:T(8,128)(2,1)} async-done(((bf16[3,1,128,1024]{3,2,1,0:T(8,128)(2,1)}), bf16[3,1,512,1024]{3,2,1,0:T(8,128)(2,1)}) %all-gather.44.cloned.1.call-update) | async-done | bytes 3145744 | tf_op jit(solution)/shard_map/all_gather | solution.py:323
  2797.9 24.8 reduce-scatter.44.cloned.1.call-done
  2870.3 45.7 %all-gather.48.cloned.1.call-done = bf16[3,1,512,1024]{3,2,1,0:T(8,128)(2,1)} async-done(((bf16[3,1,128,1024]{3,2,1,0:T(8,128)(2,1)}), bf16[3,1,512,1024]{3,2,1,0:T(8,128)(2,1)}) %all-gather.48.cloned.1.call-update) | async-done | bytes 3145744 | tf_op jit(solution)/shard_map/all_gather | solution.py:323
  2989.3 28.2 reduce-scatter.46.cloned.1.call-done
  3041.6 39.3 %all-reduce.14 = (f32[3]{0:T(128)S(1)}, f32[]{:T(128)}) all-reduce(f32[3]{0:T(128)S(1)} %maximum_add_fusion, f32[]{:T(128)S(6)} %add.638), channel_id=1, replica_groups=mesh['dp'=8,'state'=4] {'dp','state'}, use_global_device_ids=true, to_apply=%region_26.27 | all-reduce | flops 4 | bytes 32 | tf_op jit(solution)/shard_map/psum | solution.py:281
  3113.8 34.4 %rev.3 = f32[2,512,1024]{2,1,0:T(8,128)} reverse(f32[2,512,1024]{2,1,0:T(8,128)} %add_bitcast_fusion), dimensions={2} | reverse | bytes 8388608 | tf_op jit(solution)/shard_map/rev | solution.py:95
  3194.9 28.2 reduce-scatter.60.cloned.1.call-done
  3232.0 32.9 reduce-scatter.52.cloned.1.call-done
  3266.6 39.9 %reduce-scatter.58.cloned.1.call-done = bf16[128,3,256]{2,0,1:T(8,128)(2,1)} async-done(((bf16[1024,3,256]{2,0,1:T(8,128)(2,1)}), bf16[128,3,256]{2,0,1:T(8,128)(2,1)}) %reduce-scatter.58.cloned.1.call-update) | async-done | bytes 196624 | tf_op jit(solution)/shard_map/reduce_scatter | solution.py:462
  3308.2 34.8 %reduce-scatter.66.cloned.1.call-done = bf16[128,128]{1,0:T(8,128)(2,1)} async-done(((bf16[1024,128]{1,0:T(8,128)(2,1)}), bf16[128,128]{1,0:T(8,128)(2,1)}) %reduce-scatter.66.cloned.1.call-update) | async-done | bytes 32784
  (676 shorter events, 576.7 us)
Async XLA Ops:
  28.6 147.7 %all-gather.36.cloned.1.call-start = ((), (), s32[]{:S(2)}) async-start(), calls=%async_computation.32 | async-start | bytes 7077888 | tf_op jit(solution)/shard_map/all_gather | solution.py:143
  29.2 2199.9 %all-gather.34.cloned.1.call-start = ((), (), s32[]{:S(2)}) async-start(), calls=%async_computation.31 | async-start | bytes 1310720 | tf_op jit(solution)/shard_map/all_gather | solution.py:176
  29.8 2209.1 %reduce-scatter.32.cloned.1.call-start = ((), (), s32[]{:S(2)}) async-start(), calls=%async_computation.33 | async-start | bytes 3932160 | tf_op jit(solution)/shard_map/reduce_scatter | solution.py:246
  180.4 2090.4 %all-gather.38.cloned.1.call-start = ((), (), s32[]{:S(2)}) async-start(), calls=%async_computation.34 | async-start | bytes 1310720 | tf_op jit(solution)/shard_map/all_gather | solution.py:179
  2333.3 142.3 %all-gather.28.cloned.1.call-start = ((), (), s32[]{:S(2)}) async-start(), calls=%async_computation.27 | async-start | bytes 1310720 | tf_op jit(solution)/shard_map/all_gather | solution.py:206
  2333.8 171.2 %all-gather.50.cloned.1.call-start = ((), (), s32[]{:S(2)}) async-start(), calls=%async_computation.54 | async-start | bytes 1310720 | tf_op jit(solution)/shard_map/all_gather | solution.py:109
  2334.4 200.0 %reduce-scatter.42.cloned.1.call-start = ((), (), s32[]{:S(2)}) async-start(), calls=%async_computation.42 | async-start | bytes 1310720 | tf_op jit(solution)/shard_map/reduce_scatter | solution.py:353
  2458.8 131.8 %reduce-scatter.30.cloned.1.call-start = ((), (), s32[]{:S(2)}) async-start(), calls=%async_computation.30 | async-start | bytes 1310720 | tf_op jit(solution)/shard_map/reduce_scatter | solution.py:103
  2482.7 136.0 %reduce-scatter.40.cloned.1.call-start = ((), (), s32[]{:S(2)}) async-start(), calls=%async_computation.39 | async-start | bytes 1310720 | tf_op jit(solution)/shard_map/reduce_scatter | solution.py:353
  2513.3 166.6 %reduce-scatter.38.cloned.1.call-start = ((), (), s32[]{:S(2)}) async-start(), calls=%async_computation.38 | async-start | bytes 3932160 | tf_op jit(solution)/shard_map/reduce_scatter | solution.py:246
  2522.3 187.7 %all-gather.46.cloned.1.call-start = ((), (), s32[]{:S(2)}) async-start(), calls=%async_computation.43 | async-start | bytes 1310720 | tf_op jit(solution)/shard_map/all_gather | solution.py:109
  2623.5 151.7 %all-gather.44.cloned.1.call-start = ((), (), s32[]{:S(2)}) async-start(), calls=%async_computation.41 | async-start | bytes 3932160 | tf_op jit(solution)/shard_map/all_gather | solution.py:323
  2684.2 138.5 %reduce-scatter.44.cloned.1.call-start = ((), (), s32[]{:S(2)}) async-start(), calls=%async_computation.44 | async-start | bytes 1310720 | tf_op jit(solution)/shard_map/reduce_scatter | solution.py:421
  2797.5 118.6 %all-gather.48.cloned.1.call-start = ((), (), s32[]{:S(2)}) async-start(), calls=%async_computation.45 | async-start | bytes 3932160 | tf_op jit(solution)/shard_map/all_gather | solution.py:323
  2828.7 156.6 %reduce-scatter.50.cloned.1.call-start = ((), (), s32[]{:S(2)}) async-start(), calls=%async_computation.48 | async-start | bytes 1310720 | tf_op jit(solution)/shard_map/reduce_scatter | solution.py:421
  2962.5 120.5 %reduce-scatter.64.cloned.1.call-start = ((), (), s32[]{:S(2)}) async-start(), calls=%async_computation.57 | async-start | bytes 2359296
  2970.0 136.0 %reduce-scatter.56.cloned.1.call-start = ((), (), s32[]{:S(2)}) async-start(), calls=%async_computation.51 | async-start | bytes 2359296 | tf_op jit(solution)/shard_map/reduce_scatter | solution.py:456
  2976.6 205.4 %reduce-scatter.54.cloned.1.call-start = ((), (), s32[]{:S(2)}) async-start(), calls=%async_computation.50 | async-start | bytes 589824 | tf_op jit(solution)/shard_map/reduce_scatter | solution.py:450
  2980.7 207.6 %reduce-scatter.62.cloned.1.call-start = ((), (), s32[]{:S(2)}) async-start(), calls=%async_computation.56 | async-start | bytes 294912
  3020.1 203.0 %reduce-scatter.60.cloned.1.call-start = ((), (), s32[]{:S(2)}) async-start(), calls=%async_computation.53 | async-start | bytes 1769472 | tf_op jit(solution)/shard_map/reduce_scatter | solution.py:468
  3025.4 239.5 %reduce-scatter.52.cloned.1.call-start = ((), (), s32[]{:S(2)}) async-start(), calls=%async_computation.49 | async-start | bytes 1769472 | tf_op jit(solution)/shard_map/reduce_scatter | solution.py:447
  3030.3 276.2 %reduce-scatter.58.cloned.1.call-start = ((), (), s32[]{:S(2)}) async-start(), calls=%async_computation.52 | async-start | bytes 1769472 | tf_op jit(solution)/shard_map/reduce_scatter | solution.py:462
  3037.0 305.9 %reduce-scatter.66.cloned.1.call-start = ((), (), s32[]{:S(2)}) async-start(), calls=%async_computation.58 | async-start | bytes 294912
  3224.9 119.6 %all-to-all-start.1 = ((bf16[128,3,1,256]{3,1,2,0:T(4,128)(2,1)}), bf16[128,3,1,256]{3,1,2,0:T(4,128)(2,1)S(1)}, u32[]{:S(2)}, u32[]{:S(2)}) async-start(bf16[128,3,1,256]{3,1,2,0:T(4,128)(2,1)} %copy.442), calls=%async_computation.18 | async-start | bytes 524288 | tf_op jit(solution)/shard_map/all_to_all | solution.py:476
  (190 other events, 4775.3 us)
Sparse Core Ops, SparseCore 0:
  12.6 30.6 all-gather.19
  73.3 27.9 all-gather.23
  130.7 45.5 all-gather.35
  178.3 27.9 all-gather.33
  208.6 59.7 reduce-scatter.31
  2242.8 27.9 all-gather.37
  2273.7 26.6 reduce-scatter.27
  2358.9 27.9 all-gather.39
  2389.0 27.4 all-gather.51
  2418.2 27.3 all-gather.31
  2447.6 27.9 all-gather.27
  2477.6 27.4 all-gather.49
  2621.0 58.8 reduce-scatter.37
  2682.1 27.9 all-gather.45
  2712.2 62.9 all-gather.43
  2853.1 62.9 all-gather.47
  3020.7 40.4 reduce-scatter.63
  3064.8 41.0 reduce-scatter.55
  3109.7 34.2 reduce-scatter.53
  3147.6 33.5 reduce-scatter.61
  3184.6 38.4 reduce-scatter.59
  3226.4 38.4 reduce-scatter.51
  3268.0 38.4 reduce-scatter.57
  3309.3 33.5 reduce-scatter.65
  (13 shorter events, 336.1 us)
where the time goes:
time: 3410 us; the launch traced here: 3350 us
  local copies, waits for them, and re-layouts  2170 us (64%)
  waiting for transfers between devices  839 us (25%)
  matrix products  158 us (5%)
  other arithmetic  77.6 us (2%)
  blocking collectives  72.9 us (2%)
    gather x2, local copies, waits for them, and re-layouts, shards(): jnp.take(per_offset, jnp.clip(offset, 0, window_width - 1), axis=0)  2030 us
    reduce_scatter x4, waiting for transfers between devices, sum_rows(): lax.psum_scatter(partial_value.astype(jnp.bfloat16), 'state', scatter_dim...  98.8 us
    all_gather x2, waiting for transfers between devices, shards(): gates_rows = lax.all_gather(gates_low, 'state', axis=2, tiled=True)  90.7 us
    all_gather x4, waiting for transfers between devices, whole_rows(): return lax.all_gather(partial_value, 'state', axis=1, tiled=True)  89.9 us
  transfers between devices with their start and end apart: 39, of which 31 were waited for; matrix products, arithmetic and copies ran while one was open for 70% of the time, Pallas kernels for 0%

commit v1 on v0

--- a/solution.py
+++ b/solution.py
@@ -92,11 +92,17 @@
 
 def diagonal_sums(grid_values):
     num_heads, num_rows, num_cols = grid_values.shape
-    flipped = grid_values[:, :, ::-1]
-    padded = jnp.pad(flipped, ((0, 0), (0, 0), (0, 1)))
-    sheared = padded.reshape(num_heads, num_rows * (num_cols + 1))[:, : num_rows * num_cols]
-    sheared = sheared.reshape(num_heads, num_rows, num_cols)
-    return jnp.sum(sheared, axis=1)[:, num_rows - 1 : num_cols - 1]
+    flat = grid_values.reshape(num_heads, num_rows * num_cols)
+    flat = jnp.pad(flat, ((0, 0), (0, num_rows)))
+    sums = jnp.sum(flat.reshape(num_heads, num_rows, num_cols + 1), axis=1)
+    return sums[:, num_rows:0:-1]
+
+
+def toeplitz_grid(per_offset, num_rows):
+    num_cols = 2 * num_rows
+    line = jnp.pad(per_offset[::-1].T, ((0, 0), (1, num_cols - num_rows)))
+    flat = jnp.tile(line, (1, num_rows))[:, : num_rows * num_cols]
+    return flat.reshape(-1, num_rows, num_cols)
 
 
 def sum_rows(partial_value):
@@ -150,9 +156,7 @@
     key_pos = jnp.arange(2 * window_width)[None, :]
     offset = window_width + query_pos - key_pos
     inside = (offset >= 0) & (offset < window_width)
-    bias_grid = jnp.transpose(
-        jnp.take(per_offset, jnp.clip(offset, 0, window_width - 1), axis=0), (2, 0, 1)
-    )
+    bias_grid = toeplitz_grid(per_offset, window_width)
     token_bias = jnp.pad(bias_grid, ((0, 0), (0, 0), (0, vector_rows)))
     is_fresh = fresh_start == 1
     state_now = jnp.where(

time: 3410 us -> 1370 us (0.40); the launches traced: 3350 us -> 1360 us
  local copies, waits for them, and re-layouts: 2170 us -> 128 us
  waiting for transfers between devices: 839 us -> 889 us
    gather x2 -> x0, local copies, waits for them, and re-layouts: 2030 us -> none  [shards(): jnp.take(per_offset, jnp.clip(offset, 0, window_width - 1), axis=0)]
    reduce_scatter x2, waiting for transfers between devices: 56.4 us -> 99.5 us  [shards(): lax.psum_scatter(jnp.einsum('inh,dch->cind', state_mixed, gates_used, pre...]
  transfers between devices with their start and end apart: 39 -> 39, of which waited for: 31 -> 32; matrix products, arithmetic and copies ran while one was open for 70% -> 24% of each run, Pallas kernels for 0% -> 0%
where the time goes in v1:
time: 1370 us; the launch traced here: 1360 us
  waiting for transfers between devices  889 us (65%)
  matrix products  164 us (12%)
  local copies, waits for them, and re-layouts  128 us (9%)
  other arithmetic  77.9 us (6%)
  blocking collectives  72.7 us (5%)
  between operations  20.2 us (1%)
    reduce_scatter x4, waiting for transfers between devices, sum_rows(): lax.psum_scatter(partial_value.astype(jnp.bfloat16), 'state', scatter_dim...  99.5 us
    reduce_scatter x2, waiting for transfers between devices, shards(): lax.psum_scatter(jnp.einsum('inh,dch->cind', state_mixed, gates_used, pre...  99.5 us
    all_gather x4, waiting for transfers between devices, whole_rows(): return lax.all_gather(partial_value, 'state', axis=1, tiled=True)  92.4 us
    all_gather x2, waiting for transfers between devices, shards(): gates_rows = lax.all_gather(gates_low, 'state', axis=2, tiled=True)  74.9 us
    unnamed x358, local copies, waits for them, and re-layouts  65.5 us
    unnamed x40, waiting for transfers between devices  63.1 us
    all_gather x2, waiting for transfers between devices, shards(): lax.all_gather(rms_norm(middle, gains_middle).astype(jnp.bfloat16), 'stat...  46.5 us
    all_gather x2, waiting for transfers between devices, shards(): lax.all_gather(rms_norm(state_now, gains_state).astype(jnp.bfloat16), 'st...  44 us
  transfers between devices with their start and end apart: 39, of which 32 were waited for; matrix products, arithmetic and copies ran while one was open for 24% of the time, Pallas kernels for 0%

profile of v1, /device:TPU:0, one launch (start us, length us, event | category | flops | bytes accessed | tf_op | source)
XLA Modules:
  0.0 1364.1 jit_solution(5027674022482023214)
XLA Ops:
  42.3 27.9 %all-gather.22.cloned.1.call-done = bf16[1024,3,256]{0,2,1:T(8,128)(2,1)} async-done(((bf16[128,3,256]{0,2,1:T(8,128)(2,1)}), bf16[1024,3,256]{0,2,1:T(8,128)(2,1)}) %all-gather.22.cloned.1.call-update) | async-done | bytes 1572880 | tf_op jit(solution)/shard_map/all_gather | solution.py:144
  73.0 27.3 %all-gather.24.cloned.1.call-done = bf16[1,512,1024]{2,1,0:T(8,128)(2,1)} async-done(((bf16[1,128,1024]{2,1,0:T(8,128)(2,1)}), bf16[1,512,1024]{2,1,0:T(8,128)(2,1)}) %all-gather.24.cloned.1.call-update) | async-done | bytes 1048592 | tf_op jit(solution)/shard_map/all_gather | solution.py:183
  100.3 27.7 %all-gather.26.cloned.1.call-done = bf16[1024,3,256]{0,2,1:T(8,128)(2,1)} async-done(((bf16[128,3,256]{0,2,1:T(8,128)(2,1)}), bf16[1024,3,256]{0,2,1:T(8,128)(2,1)}) %all-gather.26.cloned.1.call-update) | async-done | bytes 1572880 | tf_op jit(solution)/shard_map/all_gather | solution.py:148
  135.2 40.1 %all-gather.36.cloned.1.call-done = bf16[1024,3,1024]{2,0,1:T(8,128)(2,1)} async-done(((bf16[128,3,1024]{2,0,1:T(8,128)(2,1)}), bf16[1024,3,1024]{2,0,1:T(8,128)(2,1)}) %all-gather.36.cloned.1.call-update) | async-done | bytes 6291472 | tf_op jit(solution)/shard_map/all_gather | solution.py:149
  224.3 43.1 %reduce-scatter.32.cloned.1.call-done = bf16[3,1,128,1024]{3,2,1,0:T(8,128)(2,1)} async-done(((bf16[3,1,512,1024]{3,2,1,0:T(8,128)(2,1)}), bf16[3,1,128,1024]{3,2,1,0:T(8,128)(2,1)}) %reduce-scatter.32.cloned.1.call-update) | async-done | bytes 786448 | tf_op jit(solution)/shard_map/reduce_scatter | solution.py:250
  328.8 28.0 %reduce-scatter.34.cloned.1.call-done = bf16[1,128,1024]{2,1,0:T(8,128)(2,1)} async-done(((bf16[1,512,1024]{2,1,0:T(8,128)(2,1)}), bf16[1,128,1024]{2,1,0:T(8,128)(2,1)}) %reduce-scatter.34.cloned.1.call-update) | async-done | bytes 262160 | tf_op jit(solution)/shard_map/reduce_scatter | solution.py:109
  362.9 22.4 %all-gather.30.cloned.1.call-done = bf16[1024,1024]{1,0:T(8,128)(2,1)} async-done(((bf16[128,1024]{1,0:T(8,128)(2,1)}), bf16[1024,1024]{1,0:T(8,128)(2,1)}) %all-gather.30.cloned.1.call-update) | async-done | bytes 2097168 | tf_op jit(solution)/shard_map/all_gather | solution.py:146
  385.3 30.0 %all-gather.40.cloned.1.call-done = bf16[1,512,1024]{2,1,0:T(8,128)(2,1)} async-done(((bf16[1,128,1024]{2,1,0:T(8,128)(2,1)}), bf16[1,512,1024]{2,1,0:T(8,128)(2,1)}) %all-gather.40.cloned.1.call-update) | async-done | bytes 1048592 | tf_op jit(solution)/shard_map/all_gather | solution.py:210
  419.8 25.1 %all-gather.52.cloned.1.call-done = bf16[1,1,512,1024]{3,2,1,0:T(8,128)(2,1)} async-done(((bf16[1,1,128,1024]{3,2,1,0:T(8,128)(2,1)}), bf16[1,1,512,1024]{3,2,1,0:T(8,128)(2,1)}) %all-gather.52.cloned.1.call-update) | async-done | bytes 1048592 | tf_op jit(solution)/shard_map/all_gather | solution.py:115
  444.9 29.2 %all-gather.32.cloned.1.call-done = bf16[1024,1024]{1,0:T(8,128)(2,1)} async-done(((bf16[128,1024]{1,0:T(8,128)(2,1)}), bf16[1024,1024]{1,0:T(8,128)(2,1)}) %all-gather.32.cloned.1.call-update) | async-done | bytes 2097168 | tf_op jit(solution)/shard_map/all_gather | solution.py:147
  508.5 25.0 %all-gather.50.cloned.1.call-done = bf16[1,1,512,1024]{3,2,1,0:T(8,128)(2,1)} async-done(((bf16[1,1,128,1024]{3,2,1,0:T(8,128)(2,1)}), bf16[1,1,512,1024]{3,2,1,0:T(8,128)(2,1)}) %all-gather.50.cloned.1.call-update) | async-done | bytes 1048592 | tf_op jit(solution)/shard_map/all_gather | solution.py:115
  562.9 28.0 %reduce-scatter.36.cloned.1.call-done = bf16[1,128,1024]{2,1,0:T(8,128)(2,1)} async-done(((bf16[1,512,1024]{2,1,0:T(8,128)(2,1)}), bf16[1,128,1024]{2,1,0:T(8,128)(2,1)}) %reduce-scatter.36.cloned.1.call-update) | async-done | bytes 262160 | tf_op jit(solution)/shard_map/reduce_scatter | solution.py:109
  590.9 28.1 %reduce-scatter.40.cloned.1.call-done = bf16[1,128,1024]{2,1,0:T(8,128)(2,1)} async-done(((bf16[1,512,1024]{2,1,0:T(8,128)(2,1)}), bf16[1,128,1024]{2,1,0:T(8,128)(2,1)}) %reduce-scatter.40.cloned.1.call-update) | async-done | bytes 262160 | tf_op jit(solution)/shard_map/reduce_scatter | solution.py:357
  619.0 28.1 %reduce-scatter.30.cloned.1.call-done = bf16[1,128,1024]{2,1,0:T(8,128)(2,1)} async-done(((bf16[1,512,1024]{2,1,0:T(8,128)(2,1)}), bf16[1,128,1024]{2,1,0:T(8,128)(2,1)}) %reduce-scatter.30.cloned.1.call-update) | async-done | bytes 262160 | tf_op jit(solution)/shard_map/reduce_scatter | solution.py:109
  651.9 56.4 %reduce-scatter.38.cloned.1.call-done = bf16[3,1,128,1024]{3,2,1,0:T(8,128)(2,1)} async-done(((bf16[3,1,512,1024]{3,2,1,0:T(8,128)(2,1)}), bf16[3,1,128,1024]{3,2,1,0:T(8,128)(2,1)}) %reduce-scatter.38.cloned.1.call-update) | async-done | bytes 786448 | tf_op jit(solution)/shard_map/reduce_scatter | solution.py:250
  758.6 45.1 %all-gather.44.cloned.1.call-done = bf16[3,1,512,1024]{3,2,1,0:T(8,128)(2,1)} async-done(((bf16[3,1,128,1024]{3,2,1,0:T(8,128)(2,1)}), bf16[3,1,512,1024]{3,2,1,0:T(8,128)(2,1)}) %all-gather.44.cloned.1.call-update) | async-done | bytes 3145744 | tf_op jit(solution)/shard_map/all_gather | solution.py:327
  914.5 29.9 %all-gather.48.cloned.1.call-done = bf16[3,1,512,1024]{3,2,1,0:T(8,128)(2,1)} async-done(((bf16[3,1,128,1024]{3,2,1,0:T(8,128)(2,1)}), bf16[3,1,512,1024]{3,2,1,0:T(8,128)(2,1)}) %all-gather.48.cloned.1.call-update) | async-done | bytes 3145744 | tf_op jit(solution)/shard_map/all_gather | solution.py:327
  1007.0 22.4 %reduce-scatter.50.cloned.1.call-done = bf16[1,128,1024]{2,1,0:T(8,128)(2,1)} async-done(((bf16[1,512,1024]{2,1,0:T(8,128)(2,1)}), bf16[1,128,1024]{2,1,0:T(8,128)(2,1)}) %reduce-scatter.50.cloned.1.call-update) | async-done | bytes 262160 | tf_op jit(solution)/shard_map/reduce_scatter | solution.py:425
  1053.0 39.1 %all-reduce.15 = (f32[3]{0:T(128)S(1)}, f32[]{:T(128)}) all-reduce(f32[3]{0:T(128)S(1)} %maximum_add_fusion, f32[]{:T(128)S(6)} %add.618), channel_id=1, replica_groups=mesh['dp'=8,'state'=4] {'dp','state'}, use_global_device_ids=true, to_apply=%region_26.27 | all-reduce | flops 4 | bytes 32 | tf_op jit(solution)/shard_map/psum | solution.py:285
  1168.7 23.7 %reduce-scatter.62.cloned.1.call-done = bf16[128,3]{1,0:T(8,128)(2,1)} async-done(((bf16[1024,3]{1,0:T(8,128)(2,1)}), bf16[128,3]{1,0:T(8,128)(2,1)}) %reduce-scatter.62.cloned.1.call-update) | async-done | bytes 784
  1199.1 35.2 %reduce-scatter.60.cloned.1.call-done = bf16[128,3,256]{2,0,1:T(8,128)(2,1)} async-done(((bf16[1024,3,256]{2,0,1:T(8,128)(2,1)}), bf16[128,3,256]{2,0,1:T(8,128)(2,1)}) %reduce-scatter.60.cloned.1.call-update) | async-done | bytes 196624 | tf_op jit(solution)/shard_map/reduce_scatter | solution.py:472
  1243.2 32.9 %reduce-scatter.52.cloned.1.call-done = bf16[128,3,256]{2,0,1:T(8,128)(2,1)} async-done(((bf16[1024,3,256]{2,0,1:T(8,128)(2,1)}), bf16[128,3,256]{2,0,1:T(8,128)(2,1)}) %reduce-scatter.52.cloned.1.call-update) | async-done | bytes 196624 | tf_op jit(solution)/shard_map/reduce_scatter | solution.py:451
  1277.8 39.9 %reduce-scatter.58.cloned.1.call-done = bf16[128,3,256]{2,0,1:T(8,128)(2,1)} async-done(((bf16[1024,3,256]{2,0,1:T(8,128)(2,1)}), bf16[128,3,256]{2,0,1:T(8,128)(2,1)}) %reduce-scatter.58.cloned.1.call-update) | async-done | bytes 196624 | tf_op jit(solution)/shard_map/reduce_scatter | solution.py:466
  1319.4 34.8 %reduce-scatter.66.cloned.1.call-done = bf16[128,128]{1,0:T(8,128)(2,1)} async-done(((bf16[1024,128]{1,0:T(8,128)(2,1)}), bf16[128,128]{1,0:T(8,128)(2,1)}) %reduce-scatter.66.cloned.1.call-update) | async-done | bytes 32784
  (650 shorter events, 574.5 us)
Async XLA Ops:
  26.8 148.5 %all-gather.36.cloned.1.call-start = ((), (), s32[]{:S(2)}) async-start(), calls=%async_computation.32 | async-start | bytes 7077888 | tf_op jit(solution)/shard_map/all_gather | solution.py:149
  27.4 187.2 %all-gather.34.cloned.1.call-start = ((), (), s32[]{:S(2)}) async-start(), calls=%async_computation.31 | async-start | bytes 1310720 | tf_op jit(solution)/shard_map/all_gather | solution.py:180
  28.0 239.4 %reduce-scatter.32.cloned.1.call-start = ((), (), s32[]{:S(2)}) async-start(), calls=%async_computation.33 | async-start | bytes 3932160 | tf_op jit(solution)/shard_map/reduce_scatter | solution.py:250
  179.5 119.8 %all-gather.38.cloned.1.call-start = ((), (), s32[]{:S(2)}) async-start(), calls=%async_computation.34 | async-start | bytes 1310720 | tf_op jit(solution)/shard_map/all_gather | solution.py:183
  361.1 113.0 %all-gather.32.cloned.1.call-start = ((), (), s32[]{:S(2)}) async-start(), calls=%async_computation.29 | async-start | bytes 2359296 | tf_op jit(solution)/shard_map/all_gather | solution.py:147
  361.7 142.3 %all-gather.28.cloned.1.call-start = ((), (), s32[]{:S(2)}) async-start(), calls=%async_computation.27 | async-start | bytes 1310720 | tf_op jit(solution)/shard_map/all_gather | solution.py:210
  362.3 171.2 %all-gather.50.cloned.1.call-start = ((), (), s32[]{:S(2)}) async-start(), calls=%async_computation.54 | async-start | bytes 1310720 | tf_op jit(solution)/shard_map/all_gather | solution.py:115
  362.9 200.0 %reduce-scatter.42.cloned.1.call-start = ((), (), s32[]{:S(2)}) async-start(), calls=%async_computation.42 | async-start | bytes 1310720 | tf_op jit(solution)/shard_map/reduce_scatter | solution.py:357
  487.3 131.8 %reduce-scatter.40.cloned.1.call-start = ((), (), s32[]{:S(2)}) async-start(), calls=%async_computation.39 | async-start | bytes 1310720 | tf_op jit(solution)/shard_map/reduce_scatter | solution.py:357
  546.5 161.9 %reduce-scatter.38.cloned.1.call-start = ((), (), s32[]{:S(2)}) async-start(), calls=%async_computation.38 | async-start | bytes 3932160 | tf_op jit(solution)/shard_map/reduce_scatter | solution.py:250
  555.4 183.1 %all-gather.46.cloned.1.call-start = ((), (), s32[]{:S(2)}) async-start(), calls=%async_computation.43 | async-start | bytes 1310720 | tf_op jit(solution)/shard_map/all_gather | solution.py:115
  651.9 151.8 %all-gather.44.cloned.1.call-start = ((), (), s32[]{:S(2)}) async-start(), calls=%async_computation.41 | async-start | bytes 3932160 | tf_op jit(solution)/shard_map/all_gather | solution.py:327
  712.6 139.0 %reduce-scatter.44.cloned.1.call-start = ((), (), s32[]{:S(2)}) async-start(), calls=%async_computation.44 | async-start | bytes 1310720 | tf_op jit(solution)/shard_map/reduce_scatter | solution.py:425
  826.4 118.0 %all-gather.48.cloned.1.call-start = ((), (), s32[]{:S(2)}) async-start(), calls=%async_computation.45 | async-start | bytes 3932160 | tf_op jit(solution)/shard_map/all_gather | solution.py:327
  857.6 147.8 %reduce-scatter.48.cloned.1.call-start = ((), (), s32[]{:S(2)}) async-start(), calls=%async_computation.47 | async-start | bytes 1310720 | tf_op jit(solution)/shard_map/reduce_scatter | solution.py:417
  982.6 111.6 %reduce-scatter.64.cloned.1.call-start = ((), (), s32[]{:S(2)}) async-start(), calls=%async_computation.57 | async-start | bytes 2359296
  990.1 127.7 %reduce-scatter.56.cloned.1.call-start = ((), (), s32[]{:S(2)}) async-start(), calls=%async_computation.51 | async-start | bytes 2359296 | tf_op jit(solution)/shard_map/reduce_scatter | solution.py:460
  996.7 164.8 %reduce-scatter.54.cloned.1.call-start = ((), (), s32[]{:S(2)}) async-start(), calls=%async_computation.50 | async-start | bytes 589824 | tf_op jit(solution)/shard_map/reduce_scatter | solution.py:454
  1000.7 191.8 %reduce-scatter.62.cloned.1.call-start = ((), (), s32[]{:S(2)}) async-start(), calls=%async_computation.56 | async-start | bytes 294912
  1031.5 202.8 %reduce-scatter.60.cloned.1.call-start = ((), (), s32[]{:S(2)}) async-start(), calls=%async_computation.53 | async-start | bytes 1769472 | tf_op jit(solution)/shard_map/reduce_scatter | solution.py:472
  1036.7 239.3 %reduce-scatter.52.cloned.1.call-start = ((), (), s32[]{:S(2)}) async-start(), calls=%async_computation.49 | async-start | bytes 1769472 | tf_op jit(solution)/shard_map/reduce_scatter | solution.py:451
  1041.6 276.1 %reduce-scatter.58.cloned.1.call-start = ((), (), s32[]{:S(2)}) async-start(), calls=%async_computation.52 | async-start | bytes 1769472 | tf_op jit(solution)/shard_map/reduce_scatter | solution.py:466
  1046.5 307.7 %reduce-scatter.66.cloned.1.call-start = ((), (), s32[]{:S(2)}) async-start(), calls=%async_computation.58 | async-start | bytes 294912
  1236.1 119.7 %all-to-all-start.1 = ((bf16[128,3,1,256]{3,1,2,0:T(4,128)(2,1)}), bf16[128,3,1,256]{3,1,2,0:T(4,128)(2,1)S(1)}, u32[]{:S(2)}, u32[]{:S(2)}) async-start(bf16[128,3,1,256]{3,1,2,0:T(4,128)(2,1)} %copy.432), calls=%async_computation.18 | async-start | bytes 524288 | tf_op jit(solution)/shard_map/all_to_all | solution.py:480
  (178 other events, 5226.1 us)
Sparse Core Ops, SparseCore 0:
  11.6 30.6 all-gather.19
  72.3 27.9 all-gather.23
  129.7 45.5 all-gather.35
  177.3 27.9 all-gather.33
  207.6 59.7 reduce-scatter.31
  271.3 27.9 all-gather.37
  302.1 26.6 reduce-scatter.27
  387.3 27.9 all-gather.39
  417.4 27.4 all-gather.51
  446.6 27.3 all-gather.31
  476.1 27.9 all-gather.27
  506.0 27.4 all-gather.49
  649.4 58.8 reduce-scatter.37
  710.5 27.9 all-gather.45
  740.6 62.9 all-gather.43
  881.4 62.9 all-gather.47
  1032.5 40.3 reduce-scatter.63
  1076.6 41.1 reduce-scatter.55
  1120.9 34.1 reduce-scatter.53
  1158.8 33.5 reduce-scatter.61
  1195.8 38.4 reduce-scatter.59
  1237.6 38.4 reduce-scatter.51
  1279.2 38.4 reduce-scatter.57
  1320.6 33.6 reduce-scatter.65
  (13 shorter events, 336.1 us)

commit v2 on v1

--- a/solution.py
+++ b/solution.py
@@ -3,6 +3,8 @@
 import jax
 import jax.numpy as jnp
 from jax import lax
+from jax.experimental import pallas as pl
+from jax.experimental.pallas import tpu as pltpu
 from jax.sharding import PartitionSpec as P
 
 DH = 128
@@ -515,6 +517,994 @@
     )
 
 
+MESH = pl.DeviceIdType.MESH
+NN = (((1,), (0,)), ((), ()))
+NT = (((1,), (1,)), ((), ()))
+TN = (((0,), (0,)), ((), ()))
+VMEM_BYTES = 62 * 2**20
+
+
+def place():
+    chip_core = lax.axis_index("dp")
+    level = lax.axis_index("state")
+    core, low = lax.rem(chip_core, 2), lax.rem(level, 2)
+    x, y = lax.rem(chip_core // 2, 2), chip_core // 4
+    flip = lambda bit: 1 - 2 * bit
+    return {
+        "rank": 2 * low + core,
+        "ranks": [2 * low + core, 2 * low + 1 - core, 2 * (1 - low) + core, 2 * (1 - low) + 1 - core],
+        "mates": [
+            None,
+            (chip_core + flip(core), level),
+            (chip_core, level + flip(low)),
+            (chip_core + flip(core), level + flip(low)),
+        ],
+        "plane": 2 * y + x,
+        "planes": [2 * y + x, 2 * y + 1 - x, 2 * (1 - y) + x, 2 * (1 - y) + 1 - x],
+        "plane_mates": [
+            None,
+            (chip_core + 2 * flip(x), level),
+            (chip_core + 4 * flip(y), level),
+            (chip_core + 2 * flip(x) + 4 * flip(y), level),
+        ],
+        "core": core,
+        "dp": chip_core,
+    }
+
+
+def rows_at(start, size, step=128):
+    return pl.ds(pl.multiple_of(start, step), size)
+
+
+class Links:
+    def __init__(self, send_sems, recv_sems):
+        self.send_sems, self.recv_sems = send_sems, recv_sems
+        self.used = 0
+        self.open_sends = []
+
+    def copy(self, source, target, device):
+        at = self.used
+        self.used += 1
+        moved = pltpu.make_async_remote_copy(
+            src_ref=source,
+            dst_ref=target,
+            send_sem=self.send_sems.at[at],
+            recv_sem=self.recv_sems.at[at],
+            device_id=device,
+            device_id_type=MESH,
+        )
+        moved.start()
+        self.open_sends.append(moved)
+        return moved
+
+    def close(self):
+        for moved in self.open_sends:
+            moved.wait_send()
+        self.open_sends = []
+
+
+def greet(devices):
+    barrier = pltpu.get_barrier_semaphore()
+    for device in devices:
+        pl.semaphore_signal(barrier, inc=1, device_id=device, device_id_type=MESH)
+    pl.semaphore_wait(barrier, len(devices))
+
+
+class RowGather:
+    def __init__(self, links, here, ref, base, rows):
+        self.links, self.here, self.ref, self.base, self.rows = links, here, ref, base, rows
+
+    def part(self, k):
+        return self.ref.at[rows_at(self.base + self.here["ranks"][k] * self.rows, self.rows)]
+
+    def start(self):
+        own, mates = self.part(0), self.here["mates"]
+        self.far = self.links.copy(own, own, mates[2])
+        self.near = self.links.copy(own, own, mates[1])
+        return self
+
+    def ready(self, k):
+        if k == 1:
+            self.near.wait_recv()
+        elif k == 2:
+            self.far.wait_recv()
+            block = self.part(2)
+            self.last = self.links.copy(block, block, self.here["mates"][1])
+        elif k == 3:
+            self.last.wait_recv()
+
+
+class RowSum:
+    def __init__(self, links, here, stage, near_in, far_out, far_in, rows):
+        self.links, self.here, self.rows = links, here, rows
+        self.stage, self.near_in, self.far_out, self.far_in = stage, near_in, far_out, far_in
+
+    def part(self, k):
+        return self.stage.at[rows_at(self.here["ranks"][k] * self.rows, self.rows)]
+
+    def fill(self, make_rows):
+        sibling = self.here["mates"][1]
+        for k, slot in ((3, 0), (1, 1)):
+            self.part(k)[...] = make_rows(self.here["ranks"][k]).astype(jnp.bfloat16)
+            moved = self.links.copy(self.part(k), self.near_in.at[slot], sibling)
+            if slot == 0:
+                self.near_far = moved
+            else:
+                self.near_own = moved
+        for k in (2, 0):
+            self.part(k)[...] = make_rows(self.here["ranks"][k]).astype(jnp.bfloat16)
+        return self
+
+    def forward(self):
+        self.near_far.wait_recv()
+        summed = self.part(2)[...].astype(jnp.float32) + self.near_in[0].astype(jnp.float32)
+        self.far_out[...] = summed.astype(jnp.bfloat16)
+        self.far = self.links.copy(self.far_out, self.far_in, self.here["mates"][2])
+        return self
+
+    def finish(self):
+        self.near_own.wait_recv()
+        self.far.wait_recv()
+        return (
+            self.part(0)[...].astype(jnp.float32)
+            + self.near_in[1].astype(jnp.float32)
+            + self.far_in[...].astype(jnp.float32)
+        )
+
+
+def row_sum_scratch(rows, width):
+    return [
+        pltpu.VMEM((4 * rows, width), jnp.bfloat16),
+        pltpu.VMEM((2, rows, width), jnp.bfloat16),
+        pltpu.VMEM((rows, width), jnp.bfloat16),
+        pltpu.VMEM((rows, width), jnp.bfloat16),
+    ]
+
+
+def dot(left, right, dims):
+    return lax.dot_general(left, right, dims, preferred_element_type=jnp.float32)
+
+
+def scale_of(tensor):
+    return lax.rsqrt(jnp.mean(tensor * tensor, axis=-1, keepdims=True) + EPS)
+
+
+def rms_back(tensor, gains_row, cotangent):
+    scale = scale_of(tensor)
+    weighted = cotangent * gains_row
+    inner = jnp.mean(tensor * weighted, axis=-1, keepdims=True)
+    straight = scale * weighted - tensor * (scale * scale * scale * inner)
+    return straight, jnp.sum(cotangent * tensor * scale, axis=0, keepdims=True)
+
+
+def column_heads(head):
+    return pl.ds(head * DH, DH)
+
+
+def bias_tiles(lines_ref, tiles_ref, heads, width):
+    for head in range(heads):
+        line = lines_ref[head : head + 1, :]
+        spread = jnp.broadcast_to(line, (tiles_ref.shape[1], line.shape[1]))
+        tiles_ref[head] = pltpu.roll(spread, 0, 1, stride=1, stride_axis=0)[:, :width]
+
+
+def softmax_pair(first, second):
+    top = jnp.maximum(
+        jnp.max(first, axis=-1, keepdims=True), jnp.max(second, axis=-1, keepdims=True)
+    )
+    first, second = jnp.exp(first - top), jnp.exp(second - top)
+    total = jnp.sum(first, axis=-1, keepdims=True) + jnp.sum(second, axis=-1, keepdims=True)
+    share = 1.0 / total
+    return (
+        (first * share).astype(jnp.bfloat16),
+        (second * share).astype(jnp.bfloat16),
+        top + jnp.log(total),
+    )
+
+
+TILE = 256
+ROOT = 1.0 / math.sqrt(DH)
+
+
+def attention_kernel(
+    x_ref, s0_ref, past_ref, mask_ref, rowmask_ref, lines_ref, gains_ref,
+    wst_in, wtok_in, wout_in, gates_in, wup_in, wdn_in,
+    normed, snormed, queries, keys, values, state_qkv, lse_token, lse_state, mixed, smixed,
+    middle, gate_values, s1_ref, s2_ref, branch_sum, wst, wtok, wout, gates, wup, wdn,
+    tiles, a2a_0, a2a_1, *rest,
+):
+    rs = [rest[0:4], rest[4:8]]
+    links = Links(rest[8], rest[9])
+    here = place()
+    rank, ranks, mates = here["rank"], here["ranks"], here["mates"]
+    planes, plane_mates = here["planes"], here["plane_mates"]
+    rows = s0_ref.shape[0]
+    window = 4 * rows
+    width = queries.shape[1]
+    heads = width // DH
+    greet(mates[1:] + plane_mates[1:])
+
+    def spread(local, full):
+        size = local.shape[0]
+        target = full.at[rows_at(planes[0] * size, size)]
+        return [links.copy(local, target, plane_mates[k]) for k in (1, 2, 3)]
+
+    def own_rows(local, full):
+        size = local.shape[0]
+        full[rows_at(planes[0] * size, size), :] = local[...]
+
+    def arrived(copies):
+        for moved in copies:
+            moved.wait_recv()
+
+    s0 = s0_ref[...]
+    snormed[rows_at(rank * rows, rows), :] = (s0 * scale_of(s0) * gains_ref[2:3, :]).astype(jnp.bfloat16)
+    gather_s0 = RowGather(links, here, snormed, 0, rows).start()
+    wst_moves = spread(wst_in, wst)
+    gather_x = []
+    for block in range(2):
+        x = x_ref[block * rows : (block + 1) * rows, :].astype(jnp.float32)
+        normed[rows_at(block * window + rank * rows, rows), :] = (
+            x * scale_of(x) * gains_ref[0:1, :]
+        ).astype(jnp.bfloat16)
+        gather_x.append(RowGather(links, here, normed, block * window, rows).start())
+        if block == 0:
+            wtok_moves = spread(wtok_in, wtok)
+    wout_moves = spread(wout_in, wout)
+    gate_rows = gates_in.shape[0]
+    gate_target = gates.at[rows_at(here["dp"] * gate_rows, gate_rows)]
+    gate_moves = [links.copy(gates_in, gate_target, plane_mates[k]) for k in (1, 2, 3)]
+    gate_near = links.copy(gates_in, gate_target, mates[1])
+    wup_moves = spread(wup_in, wup)
+    wdn_moves = spread(wdn_in, wdn)
+    own_rows(wst_in, wst)
+    own_rows(wtok_in, wtok)
+    own_rows(wout_in, wout)
+    own_rows(wup_in, wup)
+    own_rows(wdn_in, wdn)
+    gates[rows_at(here["dp"] * gate_rows, gate_rows), :] = gates_in[...]
+    keys[0:window, :] = past_ref[0]
+    values[0:window, :] = past_ref[1]
+    bias_tiles(lines_ref, tiles, heads, 3 * TILE)
+
+    def project_state(block, gather):
+        for k in range(4):
+            gather.ready(k)
+            at = rows_at(block * window + ranks[k] * rows, rows)
+            state_qkv[at, :] = dot(snormed[at, :], wst[...], NN).astype(jnp.bfloat16)
+
+    def project_token(block, gather):
+        for k in range(4):
+            gather.ready(k)
+            at = rows_at(block * window + ranks[k] * rows, rows)
+            later = rows_at((block + 1) * window + ranks[k] * rows, rows)
+            out = dot(normed[at, :], wtok[...], NN).astype(jnp.bfloat16)
+            queries[at, :] = out[:, :width]
+            keys[later, :] = out[:, width : 2 * width]
+            values[later, :] = out[:, 2 * width :]
+
+    def state_attention(block):
+        base = block * window
+        own = pl.ds((block + 1) * window, window)
+        whole = pl.ds(base, window)
+        own_mask = mask_ref[0:1, (block + 1) * window : (block + 2) * window]
+        for head in range(heads):
+            at = head * DH
+            for tile in range(window // TILE):
+                here_rows = pl.ds(base + tile * TILE, TILE)
+                query = state_qkv[here_rows, at : at + DH]
+                first = dot(query, state_qkv[whole, width + at : width + at + DH], NT) * ROOT
+                second = dot(query, keys[own, at : at + DH], NT) * ROOT + own_mask
+                first, second, lse = softmax_pair(first, second)
+                out = dot(first, state_qkv[whole, 2 * width + at : 2 * width + at + DH], NN)
+                out = out + dot(second, values[own, at : at + DH], NN)
+                smixed[here_rows, at : at + DH] = out.astype(jnp.bfloat16)
+                lse_state[here_rows, head : head + 1] = lse
+
+    def token_attention(block):
+        base = block * window
+        whole = pl.ds(base, window)
+        for head in range(heads):
+            at = head * DH
+            for tile in range(window // TILE):
+                here_rows = pl.ds(base + tile * TILE, TILE)
+                near = pl.ds(base + tile * TILE, 3 * TILE)
+                query = queries[here_rows, at : at + DH]
+                first = dot(query, keys[near, at : at + DH], NT) * ROOT + tiles[head]
+                first = first + mask_ref[0:1, base + tile * TILE : base + tile * TILE + 3 * TILE]
+                second = dot(query, state_qkv[whole, width + at : width + at + DH], NT) * ROOT
+                first, second, lse = softmax_pair(first, second)
+                out = dot(first, values[near, at : at + DH], NN)
+                out = out + dot(second, state_qkv[whole, 2 * width + at : 2 * width + at + DH], NN)
+                mixed[here_rows, at : at + DH] = out.astype(jnp.bfloat16)
+                lse_token[here_rows, head : head + 1] = lse
+
+    def spread_state(block, buffer):
+        moves = []
+        columns = pl.ds(pl.multiple_of(rank * width, width), width)
+        for k in (2, 3, 1):
+            source = smixed.at[rows_at(block * window + ranks[k] * rows, rows)]
+            moves.append(links.copy(source, buffer.at[:, columns], mates[k]))
+        buffer[:, columns] = smixed[rows_at(block * window + rank * rows, rows), :]
+        return moves
+
+    def renew(block, buffer, state_now):
+        size = state_now.shape[1]
+        source = buffer[...]
+        parts = []
+        for c in range(3):
+            part = dot(source, gates[:, c * size : (c + 1) * size], NT)
+            gate_values[block * rows : (block + 1) * rows, c * size : (c + 1) * size] = part
+            parts.append(part)
+        return state_now * jax.nn.sigmoid(parts[2] + 1.0) + jnp.tanh(parts[0]) * jax.nn.sigmoid(
+            parts[1] - 1.0
+        )
+
+    def branch_rows(block):
+        def make(which):
+            return dot(mixed[rows_at(block * window + which * rows, rows), :], wout[...], NT)
+
+        return make
+
+    sums = [RowSum(links, here, *rs[block], rows) for block in range(2)]
+
+    def finish_branch(block):
+        branch = sums[block].finish()
+        at = slice(block * rows, (block + 1) * rows)
+        middle[at, :] = x_ref[at, :].astype(jnp.float32) + branch
+        return jnp.sum(branch * branch * rowmask_ref[at, :], axis=0, keepdims=True)
+
+    arrived(wst_moves)
+    project_state(0, gather_s0)
+    arrived(wtok_moves)
+    project_token(0, gather_x[0])
+    state_attention(0)
+    moves_0 = spread_state(0, a2a_0)
+    project_token(1, gather_x[1])
+    arrived(gate_moves)
+    gate_forward = []
+    for k in (1, 2, 3):
+        block_at = gates.at[rows_at((2 * planes[k] + here["core"]) * gate_rows, gate_rows)]
+        gate_forward.append(links.copy(block_at, block_at, mates[1]))
+    token_attention(0)
+    arrived(wout_moves)
+    sums[0].fill(branch_rows(0))
+    arrived(moves_0)
+    gate_near.wait_recv()
+    arrived(gate_forward)
+    s1 = renew(0, a2a_0, s0_ref[...])
+    s1_ref[...] = s1
+    snormed[rows_at(window + rank * rows, rows), :] = (s1 * scale_of(s1) * gains_ref[2:3, :]).astype(
+        jnp.bfloat16
+    )
+    gather_s1 = RowGather(links, here, snormed, window, rows).start()
+    sums[0].forward()
+    project_state(1, gather_s1)
+    state_attention(1)
+    moves_1 = spread_state(1, a2a_1)
+    token_attention(1)
+    sums[1].fill(branch_rows(1))
+    total = finish_branch(0)
+    arrived(moves_1)
+    sums[1].forward()
+    s2_ref[...] = renew(1, a2a_1, s1_ref[...])
+    total = total + finish_branch(1)
+    branch_sum[...] = jnp.broadcast_to(total, branch_sum.shape)
+    arrived(wup_moves)
+    arrived(wdn_moves)
+    links.close()
+
+
+def feed_kernel(
+    middle_ref, gout_ref, gains_ref, rowmask_ref, wup, wdn,
+    block_out, middle_grad, wup_grad, wdn_grad, gain_grad, sums_out,
+    normed, gout, up, hidden, up_grad, *rest,
+):
+    rs = [rest[4 * k : 4 * k + 4] for k in range(4)]
+    links = Links(rest[16], rest[17])
+    here = place()
+    rank, ranks, mates = here["rank"], here["ranks"], here["mates"]
+    rows = middle_ref.shape[0] // 2
+    window = 4 * rows
+    greet(mates[1:])
+    gathers, gout_gathers = [], []
+    for block in range(2):
+        at = slice(block * rows, (block + 1) * rows)
+        middle = middle_ref[at, :]
+        spot = rows_at(block * window + rank * rows, rows)
+        normed[spot, :] = (middle * scale_of(middle) * gains_ref[1:2, :]).astype(jnp.bfloat16)
+        gathers.append(RowGather(links, here, normed, block * window, rows).start())
+    for block in range(2):
+        at = slice(block * rows, (block + 1) * rows)
+        gout[rows_at(block * window + rank * rows, rows), :] = gout_ref[at, :]
+        gout_gathers.append(RowGather(links, here, gout, block * window, rows).start())
+    feeds = [RowSum(links, here, *rs[k], rows) for k in range(2)]
+    backs = [RowSum(links, here, *rs[2 + k], rows) for k in range(2)]
+
+    def rise(block):
+        for k in range(4):
+            gathers[block].ready(k)
+            at = rows_at(block * window + ranks[k] * rows, rows)
+            value = dot(normed[at, :], wup[...], NN)
+            up[at, :] = value
+            hidden[at, :] = jax.nn.gelu(value, approximate=True).astype(jnp.bfloat16)
+        feeds[block].fill(
+            lambda which: dot(hidden[rows_at(block * window + which * rows, rows), :], wdn[...], NT)
+        )
+
+    def back(block):
+        for k in range(4):
+            gout_gathers[block].ready(k)
+            at = rows_at(block * window + ranks[k] * rows, rows)
+            hidden_grad = dot(gout[at, :], wdn[...], NN)
+            value = up[at, :]
+            square = value * value
+            root = math.sqrt(2.0 / math.pi)
+            bend = jnp.tanh(root * value * (1.0 + 0.044715 * square))
+            slope = 0.5 * (1.0 + bend) + 0.5 * value * (1.0 - bend * bend) * (
+                root * (1.0 + 3.0 * 0.044715 * square)
+            )
+            up_grad[at, :] = (hidden_grad * slope).astype(jnp.bfloat16)
+        backs[block].fill(
+            lambda which: dot(up_grad[rows_at(block * window + which * rows, rows), :], wup[...], NT)
+        )
+
+    rise(0)
+    rise(1)
+    feeds[0].forward()
+    back(0)
+    feeds[1].forward()
+    back(1)
+    backs[0].forward()
+    tile = 256
+    size = wdn_grad.shape[0]
+    for part in range(size // tile):
+        at = slice(part * tile, (part + 1) * tile)
+        wdn_grad[at, :] = dot(gout[:, at], hidden[...], TN).astype(jnp.bfloat16)
+    backs[1].forward()
+    for part in range(size // tile):
+        at = slice(part * tile, (part + 1) * tile)
+        wup_grad[at, :] = dot(normed[:, at], up_grad[...], TN).astype(jnp.bfloat16)
+    feed_total, result_total, gain_total = 0.0, 0.0, 0.0
+    for block in range(2):
+        at = slice(block * rows, (block + 1) * rows)
+        feed = feeds[block].finish()
+        result = middle_ref[at, :] + feed
+        block_out[at, :] = result.astype(jnp.bfloat16)
+        share = rowmask_ref[at, :]
+        feed_total = feed_total + jnp.sum(feed * feed * share, axis=0, keepdims=True)
+        result_total = result_total + jnp.sum(result * result * share, axis=0, keepdims=True)
+    sums_out[...] = jnp.concatenate(
+        [result_total, feed_total, jnp.zeros((6, result_total.shape[1]), jnp.float32)], axis=0
+    )
+    for block in range(2):
+        at = slice(block * rows, (block + 1) * rows)
+        straight, gain = rms_back(middle_ref[at, :], gains_ref[1:2, :], backs[block].finish())
+        middle_grad[at, :] = gout_ref[at, :].astype(jnp.float32) + straight
+        gain_total = gain_total + gain
+    gain_grad[...] = jnp.broadcast_to(gain_total, gain_grad.shape)
+    links.close()
+
+
+def cotangent_kernel(
+    middle_grad, gstate_ref, x_ref, s0_ref, s1_ref, gate_values, gains_ref, mask_ref, lines_ref,
+    normed, snormed, queries, keys, values, state_qkv, lse_token, lse_state, mixed, smixed,
+    wst, wtok, wout, gates,
+    tokens_grad, carried, past_grad, gain_grad, line_grad, wst_grad, wtok_grad, wout_grad, gates_grad,
+    tiles, tile_grads, branch_grad, mixed_grad, gate_rows, state_mixed_grad, key_grad, value_grad,
+    skey_grad, svalue_grad, query_grad, squery_grad, token_cot, state_cot, *rest,
+):
+    rs = [rest[4 * k : 4 * k + 4] for k in range(4)]
+    links = Links(rest[16], rest[17])
+    here = place()
+    rank, ranks, mates = here["rank"], here["ranks"], here["mates"]
+    rows = s0_ref.shape[0]
+    window = 4 * rows
+    width = queries.shape[1]
+    heads = width // DH
+    size = s0_ref.shape[1]
+    greet(mates[1:])
+    branch_gathers = []
+    for block in (1, 0):
+        at = slice(block * rows, (block + 1) * rows)
+        branch_grad[rows_at(block * window + rank * rows, rows), :] = middle_grad[at, :].astype(
+            jnp.bfloat16
+        )
+
+    def gates_back(block, state, state_grad):
+        at = slice(block * rows, (block + 1) * rows)
+        spot = rows_at(block * window + rank * rows, rows)
+        keep = jax.nn.sigmoid(gate_values[at, 2 * size : 3 * size] + 1.0)
+        fresh = jnp.tanh(gate_values[at, 0:size])
+        let_in = jax.nn.sigmoid(gate_values[at, size : 2 * size] - 1.0)
+        gate_rows[spot, 0:size] = (state_grad * let_in * (1.0 - fresh * fresh)).astype(jnp.bfloat16)
+        gate_rows[spot, size : 2 * size] = (
+            state_grad * fresh * let_in * (1.0 - let_in)
+        ).astype(jnp.bfloat16)
+        gate_rows[spot, 2 * size : 3 * size] = (
+            state_grad * state * keep * (1.0 - keep)
+        ).astype(jnp.bfloat16)
+        out = dot(gate_rows[spot, 0:size], gates[:, 0:size], NN)
+        out = out + dot(gate_rows[spot, size : 2 * size], gates[:, size : 2 * size], NN)
+        out = out + dot(gate_rows[spot, 2 * size : 3 * size], gates[:, 2 * size : 3 * size], NN)
+        sending = rest[18 + block]
+        sending[...] = out.astype(jnp.bfloat16)
+        moves = []
+        for k in (2, 3, 1):
+            columns = pl.ds(pl.multiple_of(ranks[k] * width, width), width)
+            moves.append(links.copy(sending.at[:, columns], state_mixed_grad.at[spot], mates[k]))
+        columns = pl.ds(pl.multiple_of(rank * width, width), width)
+        state_mixed_grad[spot, :] = sending[:, columns]
+        return state_grad * keep, moves
+
+    def pair_back(first, second, lse, first_grad, second_grad):
+        first, second = jnp.exp(first - lse), jnp.exp(second - lse)
+        inner = jnp.sum(first * first_grad, axis=-1, keepdims=True) + jnp.sum(
+            second * second_grad, axis=-1, keepdims=True
+        )
+        return (
+            first.astype(jnp.bfloat16),
+            second.astype(jnp.bfloat16),
+            (first * (first_grad - inner)).astype(jnp.bfloat16),
+            (second * (second_grad - inner)).astype(jnp.bfloat16),
+        )
+
+    def token_back(block):
+        base = block * window
+        whole = pl.ds(base, window)
+        for head in range(heads):
+            at = head * DH
+            lanes = slice(at, at + DH)
+            skey_lanes = slice(width + at, width + at + DH)
+            svalue_lanes = slice(2 * width + at, 2 * width + at + DH)
+            for tile in range(window // TILE):
+                here_rows = pl.ds(base + tile * TILE, TILE)
+                near = pl.ds(base + tile * TILE, 3 * TILE)
+                query = queries[here_rows, lanes]
+                out_grad = mixed_grad[here_rows, lanes]
+                first = dot(query, keys[near, lanes], NT) * ROOT + tiles[head]
+                first = first + mask_ref[0:1, base + tile * TILE : base + tile * TILE + 3 * TILE]
+                second = dot(query, state_qkv[whole, skey_lanes], NT) * ROOT
+                first, second, first_grad, second_grad = pair_back(
+                    first,
+                    second,
+                    lse_token[here_rows, head : head + 1],
+                    dot(out_grad, values[near, lanes], NT),
+                    dot(out_grad, state_qkv[whole, svalue_lanes], NT),
+                )
+                value_grad[near, lanes] += dot(first, out_grad, TN)
+                svalue_grad[whole, lanes] += dot(second, out_grad, TN)
+                part = dot(first_grad, keys[near, lanes], NN) + dot(
+                    second_grad, state_qkv[whole, skey_lanes], NN
+                )
+                query_grad[pl.ds(tile * TILE, TILE), lanes] = part * ROOT
+                key_grad[near, lanes] += dot(first_grad, query, TN) * ROOT
+                skey_grad[whole, lanes] += dot(second_grad, query, TN) * ROOT
+                tile_grads[head, :, 0 : 3 * TILE] += first_grad.astype(jnp.float32)
+        token_cot[whole, 0:width] = query_grad[...].astype(jnp.bfloat16)
+
+    def state_back(block):
+        base = block * window
+        whole = pl.ds(base, window)
+        own = pl.ds(base + window, window)
+        own_mask = mask_ref[0:1, base + window : base + 2 * window]
+        for head in range(heads):
+            at = head * DH
+            lanes = slice(at, at + DH)
+            skey_lanes = slice(width + at, width + at + DH)
+            svalue_lanes = slice(2 * width + at, 2 * width + at + DH)
+            for tile in range(window // TILE):
+                here_rows = pl.ds(base + tile * TILE, TILE)
+                query = state_qkv[here_rows, lanes]
+                out_grad = state_mixed_grad[here_rows, lanes]
+                first = dot(query, state_qkv[whole, skey_lanes], NT) * ROOT
+                second = dot(query, keys[own, lanes], NT) * ROOT + own_mask
+                first, second, first_grad, second_grad = pair_back(
+                    first,
+                    second,
+                    lse_state[here_rows, head : head + 1],
+                    dot(out_grad, state_qkv[whole, svalue_lanes], NT),
+                    dot(out_grad, values[own, lanes], NT),
+                )
+                svalue_grad[whole, lanes] += dot(first, out_grad, TN)
+                value_grad[own, lanes] += dot(second, out_grad, TN)
+                part = dot(first_grad, state_qkv[whole, skey_lanes], NN) + dot(
+                    second_grad, keys[own, lanes], NN
+                )
+                squery_grad[pl.ds(tile * TILE, TILE), lanes] = part * ROOT
+                skey_grad[whole, lanes] += dot(first_grad, query, TN) * ROOT
+                key_grad[own, lanes] += dot(second_grad, query, TN) * ROOT
+
+    def gather_cot(block):
+        whole = pl.ds(block * window, window)
+        own = pl.ds(block * window + window, window)
+        token_cot[whole, width : 2 * width] = key_grad[own, :].astype(jnp.bfloat16)
+        token_cot[whole, 2 * width : 3 * width] = value_grad[own, :].astype(jnp.bfloat16)
+        state_cot[whole, 0:width] = squery_grad[...].astype(jnp.bfloat16)
+        state_cot[whole, width : 2 * width] = skey_grad[whole, :].astype(jnp.bfloat16)
+        state_cot[whole, 2 * width : 3 * width] = svalue_grad[whole, :].astype(jnp.bfloat16)
+
+    sums = [RowSum(links, here, *rs[k], rows) for k in range(4)]
+
+    def send_state(block):
+        sums[block].fill(
+            lambda which: dot(state_cot[rows_at(block * window + which * rows, rows), :], wst[...], NT)
+        )
+
+    def send_token(block):
+        sums[2 + block].fill(
+            lambda which: dot(token_cot[rows_at(block * window + which * rows, rows), :], wtok[...], NT)
+        )
+
+    def mix_back(block):
+        for k in range(4):
+            branch_gathers[1 - block].ready(k)
+            at = rows_at(block * window + ranks[k] * rows, rows)
+            mixed_grad[at, :] = dot(branch_grad[at, :], wout[...], NN).astype(jnp.bfloat16)
+
+    direct_1, moves_1 = gates_back(1, s1_ref[...], gstate_ref[...])
+    for block in (1, 0):
+        branch_gathers.append(RowGather(links, here, branch_grad, block * window, rows).start())
+    gate_gather_1 = RowGather(links, here, gate_rows, window, rows).start()
+    for ref in (tile_grads, key_grad, value_grad, skey_grad, svalue_grad):
+        ref[...] = jnp.zeros(ref.shape, ref.dtype)
+    bias_tiles(lines_ref, tiles, heads, 3 * TILE)
+    mix_back(1)
+    token_back(1)
+    for moved in moves_1:
+        moved.wait_recv()
+    state_back(1)
+    gather_cot(1)
+    send_state(1)
+    send_token(1)
+    sums[1].forward()
+    mix_back(0)
+    state_norm_grad, gain_2 = rms_back(s1_ref[...], gains_ref[2:3, :], sums[1].finish())
+    direct_0, moves_0 = gates_back(0, s0_ref[...], direct_1 + state_norm_grad)
+    sums[3].forward()
+    for k in range(1, 4):
+        gate_gather_1.ready(k)
+    gate_gather_0 = RowGather(links, here, gate_rows, 0, rows).start()
+    token_back(0)
+    for moved in moves_0:
+        moved.wait_recv()
+    state_back(0)
+    gather_cot(0)
+    send_state(0)
+    send_token(0)
+    past_grad[0] = key_grad[0:window, :].astype(past_grad.dtype)
+    past_grad[1] = value_grad[0:window, :].astype(past_grad.dtype)
+    sums[0].forward()
+    sums[2].forward()
+    wst_grad[...] = dot(snormed[...], state_cot[...], TN).astype(jnp.bfloat16)
+    wtok_grad[...] = dot(normed[...], token_cot[...], TN).astype(jnp.bfloat16)
+    wout_grad[...] = dot(branch_grad[...], mixed[...], TN).astype(jnp.bfloat16)
+    for k in range(1, 4):
+        gate_gather_0.ready(k)
+    for c in range(3):
+        gates_grad[:, c * width : (c + 1) * width] = dot(
+            gate_rows[:, c * size : (c + 1) * size], smixed[...], TN
+        ).astype(jnp.bfloat16)
+    for head in range(heads):
+        lines = tile_grads[head, 0:8, :]
+        span = lines.shape[1]
+        for group in range(1, TILE // 8):
+            lines = lines + pltpu.roll(tile_grads[head, 8 * group : 8 * group + 8, :], span - 8 * group, 1)
+        total = lines[0:1]
+        for line in range(1, 8):
+            total = total + pltpu.roll(lines[line : line + 1], span - line, 1)
+        line_grad[head : head + 1, :] = total
+    state_norm_grad, gain = rms_back(s0_ref[...], gains_ref[2:3, :], sums[0].finish())
+    carried[...] = direct_0 + state_norm_grad
+    gain_2 = gain_2 + gain
+    gain_0 = 0.0
+    for block in (1, 0):
+        at = slice(block * rows, (block + 1) * rows)
+        straight, gain = rms_back(
+            x_ref[at, :].astype(jnp.float32), gains_ref[0:1, :], sums[2 + block].finish()
+        )
+        tokens_grad[at, :] = (middle_grad[at, :] + straight).astype(jnp.bfloat16)
+        gain_0 = gain_0 + gain
+    gain_grad[...] = jnp.concatenate(
+        [gain_0, gain_2, jnp.zeros((6, gain_0.shape[1]), jnp.float32)], axis=0
+    )
+    links.close()
+
+
+def run_kernel(body, outs, scratch, copies, collective, name, *operands):
+    vmem = pl.BlockSpec(memory_space=pltpu.VMEM)
+    return pl.pallas_call(
+        body,
+        out_shape=outs,
+        in_specs=[vmem] * len(operands),
+        out_specs=[vmem] * len(outs),
+        scratch_shapes=scratch,
+        compiler_params=pltpu.CompilerParams(
+            collective_id=collective, has_side_effects=True, vmem_limit_bytes=VMEM_BYTES
+        ),
+        name=name,
+    )(*operands)
+
+
+def plane_kernel(*refs):
+    count = (len(refs) - 2) // 3
+    locals_, outs, inbox = refs[:count], refs[count : 2 * count], refs[2 * count : 3 * count]
+    links = Links(refs[-2], refs[-1])
+    here = place()
+    planes, mates = here["planes"], here["plane_mates"]
+    greet(mates[1:])
+    moves = []
+    for local, slots in zip(locals_, inbox):
+        size = slots.shape[1]
+        moves.append(
+            [
+                links.copy(local.at[rows_at(planes[k] * size, size)], slots.at[k - 1], mates[k])
+                for k in (3, 1, 2)
+            ]
+        )
+    for local, out, slots, copies in zip(locals_, outs, inbox, moves):
+        for moved in copies:
+            moved.wait_recv()
+        size = slots.shape[1]
+        total = local[rows_at(planes[0] * size, size), :].astype(jnp.float32)
+        for k in range(3):
+            total = total + slots[k].astype(jnp.float32)
+        out[...] = total.astype(out.dtype)
+    links.close()
+
+
+def sems(count):
+    return [pltpu.SemaphoreType.DMA((count,)), pltpu.SemaphoreType.DMA((count,))]
+
+
+def turned(dp_size, levels, other):
+    pairs = []
+    for dp in range(dp_size):
+        for level in range(levels):
+            core = dp % 2
+            half = 1 - core if other else core
+            target = (dp - core + level % 2) * levels + 2 * half + level // 2
+            pairs.append((dp * levels + level, target))
+    return pairs
+
+
+def grouped(
+    tokens, carried_state, past_keys, fresh_start, valid_count, bucket_ids, grad_output, grad_state,
+    norm_gains, token_qkv, token_out, bias_table, mlp_up, mlp_down, state_qkv, state_gates, initial_state,
+):
+    axes = ("dp", "state")
+    dp_size, levels = lax.axis_size("dp"), lax.axis_size("state")
+    there, across = turned(dp_size, levels, False), turned(dp_size, levels, True)
+    back, back_across = [(b, a) for a, b in there], [(b, a) for a, b in across]
+    go = lambda tensor: lax.ppermute(tensor, axes, there)
+    go_across = lambda tensor: lax.ppermute(tensor, axes, across)
+    home = lambda tensor: lax.ppermute(tensor, axes, back)
+    home_across = lambda tensor: lax.ppermute(tensor, axes, back_across)
+    core, level = lax.rem(lax.axis_index("dp"), 2), lax.axis_index("state")
+    half = level // 2
+    rank = 2 * lax.rem(level, 2) + core
+    _, blocks, rows, size = tokens.shape
+    window = rows * levels
+    width = token_qkv.shape[2]
+    heads = width // DH
+    units = mlp_up.shape[1]
+    model_rows = token_qkv.shape[0]
+    low, full = jnp.bfloat16, jnp.float32
+
+    initial_rows = lax.all_gather(initial_state, "dp", axis=1, tiled=True).astype(full)
+    is_fresh = fresh_start[0] == 1
+    s0 = go(jnp.where(is_fresh, initial_rows, carried_state[0]))
+    facts = go(jnp.concatenate([fresh_start, valid_count]))
+    item_fresh, item_valid = facts[0] == 1, facts[1]
+
+    def column(weight):
+        first, second = go(weight), go_across(weight)
+        return jnp.where(
+            half == 0, jnp.concatenate([first, second]), jnp.concatenate([second, first])
+        )
+
+    wst = column(state_qkv.reshape(model_rows, 3 * width))
+    x = go(tokens[0].reshape(blocks * rows, size))
+    wtok = column(token_qkv.reshape(model_rows, 3 * width))
+    past = go(jnp.swapaxes(past_keys[0], 0, 1))
+    table = go(bias_table)
+    wout = column(token_out)
+    wup = column(mlp_up)
+    wdn = column(mlp_down)
+    gates = state_gates.reshape(model_rows, 3 * size)
+    gout = go(grad_output[0].reshape(blocks * rows, size))
+    gstate = go(grad_state[0])
+
+    one_hot = (bucket_ids[:, None] == jnp.arange(table.shape[0])[None, :]).astype(full)
+    per_offset = jnp.dot(one_hot, table, precision=HIGHEST)
+    lines = jnp.pad(
+        per_offset[::-1].T, ((0, 0), (1, window - 1)), constant_values=NEGATIVE
+    )
+    places = jnp.arange(window)
+    valid = jnp.concatenate(
+        [jnp.broadcast_to(~item_fresh, (window,)), places < item_valid, window + places < item_valid]
+    )
+    mask = jnp.where(valid, 0.0, NEGATIVE).astype(full)[None, :]
+    own_places = rank * rows + jnp.arange(rows)
+    rowmask = jnp.concatenate([own_places < item_valid, window + own_places < item_valid])
+    rowmask = rowmask.astype(full)[:, None]
+
+    shape = jax.ShapeDtypeStruct
+    vmem = pltpu.VMEM
+    rs = row_sum_scratch(rows, size)
+    lanes = 4 * window // 2
+    (
+        normed, snormed, queries, keys, values, sqkv, lse_token, lse_state, mixed, smixed,
+        middle, gate_values, s1, s2, branch_sum, wst_all, wtok_all, wout_all, gates_all, wup_all, wdn_all,
+    ) = run_kernel(
+        attention_kernel,
+        [
+            shape((2 * window, size), low),
+            shape((2 * window, size), low),
+            shape((2 * window, width), low),
+            shape((3 * window, width), low),
+            shape((3 * window, width), low),
+            shape((2 * window, 3 * width), low),
+            shape((2 * window, heads), full),
+            shape((2 * window, heads), full),
+            shape((2 * window, width), low),
+            shape((2 * window, width), low),
+            shape((2 * rows, size), full),
+            shape((2 * rows, 3 * size), full),
+            shape((rows, size), full),
+            shape((rows, size), full),
+            shape((8, size), full),
+            shape((size, 3 * width), low),
+            shape((size, 3 * width), low),
+            shape((size, width), low),
+            shape((size, 3 * size), low),
+            shape((size, units), low),
+            shape((size, units), low),
+        ],
+        [vmem((heads, TILE, 3 * TILE), full), vmem((rows, size), low), vmem((rows, size), low)]
+        + rs * 2
+        + sems(64),
+        0,
+        0,
+        "attention",
+        x, s0, past, mask, rowmask, lines, norm_gains, wst, wtok, wout, gates, wup, wdn,
+    )
+    block_out, middle_grad, wup_grad, wdn_grad, gain_middle, feed_sums = run_kernel(
+        feed_kernel,
+        [
+            shape((2 * rows, size), low),
+            shape((2 * rows, size), full),
+            shape((size, units), low),
+            shape((size, units), low),
+            shape((8, size), full),
+            shape((8, size), full),
+        ],
+        [
+            vmem((2 * window, size), low),
+            vmem((2 * window, size), low),
+            vmem((2 * window, units), full),
+            vmem((2 * window, units), low),
+            vmem((2 * window, units), low),
+        ]
+        + rs * 4
+        + sems(32),
+        0,
+        1,
+        "feed",
+        middle, gout, norm_gains, rowmask, wup_all, wdn_all,
+    )
+    (
+        tokens_grad, carried, past_grad, gain_ends, line_grad, wst_grad, wtok_grad, wout_grad, gates_grad,
+    ) = run_kernel(
+        cotangent_kernel,
+        [
+            shape((2 * rows, size), low),
+            shape((rows, size), full),
+            shape((2, window, width), low),
+            shape((8, size), full),
+            shape((heads, 4 * TILE), full),
+            shape((size, 3 * width), low),
+            shape((size, 3 * width), low),
+            shape((size, width), low),
+            shape((size, 3 * width), low),
+        ],
+        [
+            vmem((heads, TILE, 3 * TILE), full),
+            vmem((heads, TILE, 4 * TILE), full),
+            vmem((2 * window, size), low),
+            vmem((2 * window, width), low),
+            vmem((2 * window, 3 * size), low),
+            vmem((2 * window, width), low),
+            vmem((3 * window, width), full),
+            vmem((3 * window, width), full),
+            vmem((2 * window, width), full),
+            vmem((2 * window, width), full),
+            vmem((window, width), full),
+            vmem((window, width), full),
+            vmem((2 * window, 3 * width), low),
+            vmem((2 * window, 3 * width), low),
+        ]
+        + rs * 4
+        + sems(48)
+        + [vmem((rows, size), low), vmem((rows, size), low)],
+        0,
+        2,
+        "cotangent",
+        middle_grad, gstate, x, s0, s1, gate_values, norm_gains, mask, lines,
+        normed, snormed, queries, keys, values, sqkv, lse_token, lse_state, mixed, smixed,
+        wst_all, wtok_all, wout_all, gates_all,
+    )
+    partials = [wup_grad, wdn_grad, wtok_grad, wst_grad, gates_grad, wout_grad]
+    quarter = size // 4
+    plane_sums = run_kernel(
+        plane_kernel,
+        [shape((quarter, part.shape[1]), low) for part in partials],
+        [vmem((3, quarter, part.shape[1]), low) for part in partials] + sems(3 * len(partials)),
+        0,
+        3,
+        "plane",
+        *partials,
+    )
+
+    def settle(part):
+        first, second = part[:model_rows], part[model_rows:]
+        straight = home(jnp.where(half == 0, first, second))
+        crossed = home_across(jnp.where(half == 0, second, first))
+        return straight.astype(full) + crossed.astype(full)
+
+    up_out, down_out, qkv_out, sqkv_out, gates_out, out_out = [settle(part) for part in plane_sums]
+    gates_out = lax.all_to_all(
+        gates_out.reshape(model_rows, 3, 1, width).astype(low), "state", split_axis=0, concat_axis=2, tiled=True
+    ).astype(full)
+    gates_out = gates_out.reshape(model_rows // levels, 3, size)
+
+    table_part = jnp.dot(one_hot.T, line_grad[:, 1 : window + 1][:, ::-1].T, precision=HIGHEST)
+    in_place = (jnp.arange(levels) == rank).astype(full)
+    table_wide = (table_part[:, None, :] * in_place[None, :, None]).reshape(-1)
+    sums = jnp.stack(
+        [jnp.sum(feed_sums[0]), jnp.sum(branch_sum[0]), jnp.sum(feed_sums[1]), jnp.sum(rowmask)]
+    )
+    packed = jnp.concatenate(
+        [gain_ends[0], gain_middle[0], gain_ends[1], table_wide, sums, jnp.zeros((124,), full)]
+    )
+    packed = lax.psum(packed, axes)
+    gains_all = packed[: 3 * size].reshape(3, size)
+    share = size // (dp_size * levels)
+    dp_at = lax.axis_index("dp")
+    gains_out = lax.dynamic_slice_in_dim(gains_all, (dp_at * levels + level) * share, share, 1)
+    table_all = packed[3 * size : 3 * size + table_wide.shape[0]].reshape(-1, levels * heads)
+    table_rows = table_all.shape[0] // dp_size
+    table_out = lax.dynamic_slice(table_all, (dp_at * table_rows, level * heads), (table_rows, heads))
+    sums = packed[3 * size + table_wide.shape[0] :][:4]
+    rms_stats = jnp.sqrt(sums[:3] / sums[3])
+
+    state_out = home(s2.astype(low)).astype(full)
+    carried_home = home(carried.astype(low)).astype(full)
+    block_home = home(block_out).reshape(1, blocks, rows, size)
+    tokens_home = home(tokens_grad).reshape(1, blocks, rows, size)
+    past_home = jnp.swapaxes(home(past_grad).astype(full), 0, 1)
+    carried_grad = jnp.where(is_fresh, 0.0, carried_home)
+    initial_part = jnp.where(is_fresh, carried_home, 0.0).astype(low)
+    initial_grad = lax.psum_scatter(initial_part, "dp", scatter_dimension=1, tiled=True).astype(full)
+    return (
+        block_home,
+        state_out[None],
+        rms_stats,
+        tokens_home,
+        carried_grad[None],
+        past_home[None],
+        gains_out,
+        qkv_out.reshape(model_rows, 3, width),
+        out_out,
+        table_out,
+        up_out,
+        down_out,
+        sqkv_out.reshape(model_rows, 3, width),
+        gates_out,
+        initial_grad,
+    )
+
+
 def solution(mesh):
     in_specs = (
         P("dp", None, "state", None),
@@ -552,4 +1542,5 @@
         P(("dp", "state"), None, None),
         P("state", "dp"),
     )
-    return jax.shard_map(shards, mesh=mesh, in_specs=in_specs, out_specs=out_specs, check_vma=False)
+    body = grouped if dict(mesh.shape) == {"dp": 8, "state": 4} else shards
+    return jax.shard_map(body, mesh=mesh, in_specs=in_specs, out_specs=out_specs, check_vma=False)

time: 1370 us -> 690 us (0.50)
  the two profiles are of different devices: /device:TPU:0 before, /device:TPU:1 now
where the time goes in v2:
time: 690 us; the launch traced here: 685 us
  Pallas kernels  416 us (60%)
  starting transfers between devices  99.2 us (14%)
  waiting for transfers between devices  50.6 us (7%)
  blocking collectives  48.6 us (7%)
  local copies, waits for them, and re-layouts  27.7 us (4%)
  other arithmetic  24.7 us (4%)
  between operations  17.2 us (2%)
    pallas_call x4, Pallas kernels, run_kernel(): pl.pallas_call(body, out_shape=outs, in_specs=[vmem] * len(operands), out...  416 us
    ppermute x12, starting transfers between devices, grouped(): go = lambda tensor: lax.ppermute(tensor, axes, there)  56 us
    ppermute x11, waiting for transfers between devices, grouped(): home = lambda tensor: lax.ppermute(tensor, axes, back)  49.3 us
    psum x1, blocking collectives, grouped(): packed = lax.psum(packed, axes)  39.4 us
    ppermute x11, starting transfers between devices, grouped(): home = lambda tensor: lax.ppermute(tensor, axes, back)  32 us
    unnamed x52, local copies, waits for them, and re-layouts  14.9 us
  transfers between devices with their start and end apart: 36, of which 7 were waited for; matrix products, arithmetic and copies ran while one was open for 5% of the time, Pallas kernels for 31%

profile of v2, /device:TPU:1, one launch (start us, length us, event | category | flops | bytes accessed | tf_op | source)
XLA Modules:
  0.0 684.6 jit_solution(3720404534818756332)
XLA Ops:
  7.3 7.1 %collective-permute-start.9 = (bf16[128,256]{1,0:T(8,128)(2,1)}, bf16[128,256]{1,0:T(8,128)(2,1)}, u32[]{:S(2)}, u32[]{:S(2)}) collective-permute-start(bf16[128,256]{1,0:T(8,128)(2,1)} %param.27), channel_id=1, source_target_pairs={{0,0},{1,4},{2,1},{3,5},{4,2},{5,6},{6,3},{7,7},{8,8},{9,12},{10,9... | collective-permute-start | bytes 196616 | tf_op jit(solution)/shard_map/ppermute | solution.py:1279
  19.2 3.6 collective-permute-start.3
  24.1 9.3 %all_gather.3 = bf16[128,1024]{1,0:T(8,128)(2,1)S(1)} all-gather(bf16[128,128]{1,0:T(8,128)(2,1)} %param.33), channel_id=1, replica_groups=mesh['dp'=8,'state'=4] {'dp'}, dimensions={1}, use_global_device_ids=true | all-gather | bytes 294912 | tf_op jit(solution)/shard_map/all_gather | solution.py:1294
  35.9 4.2 collective-permute-start.4
  47.9 5.3 collective-permute-start.7
  58.4 15.4 %collective-permute-start.2 = (bf16[2,512,256]{2,1,0:T(8,128)(2,1)}, bf16[2,512,256]{2,1,0:T(8,128)(2,1)S(1)}, u32[]{:S(2)}, u32[]{:S(2)}) collective-permute-start(bf16[2,512,256]{2,1,0:T(8,128)(2,1)} %bitcast.52), channel_id=1, source_target_pairs={{0,0},{1,4},{2,1},{3,5},{4,2},{5,6},{6,3},{7,7},{8,8},{9,12},{10,9... | collective-permute-start | bytes 1572872 | tf_op jit(solution)/shard_map/ppermute | solution.py:1279
  73.8 4.4 collective-permute-start.1
  85.1 5.0 collective-permute-start.18
  98.1 159.5 %attention.1 = (bf16[1024,1024]{1,0:T(8,128)(2,1)}, bf16[1024,1024]{1,0:T(8,128)(2,1)}, bf16[1024,256]{1,0:T(8,128)(2,1)}, bf16[1536,256]{1,0:T(8,128)(2,1)}, bf...) custom-call(bf16[256,1024]{1,0:T(8,128)(2,1)} %copy-done.1, ...), custom_call_target="tpu_custom_call" | custom-call | tf_op jit(solution)/shard_map/attention/pallas_call | solution.py:1216
  257.6 54.5 %feed.1 = (bf16[256,1024]{1,0:T(8,128)(2,1)}, f32[256,1024]{1,0:T(8,128)}, bf16[1024,1024]{1,0:T(8,128)(2,1)}, bf16[1024,1024]{1,0:T(8,128)(2,1)}, f32[8,1024]{1,0:T(8,128)}, /*index=5*/f32[8,1024]{1,0:T(8,128)}) custom-call(f32[256,1024]{1,0:T(8,128)} %get-tuple-element.57.middle_ref, bf16[256,1024]{1,0:T(8,128)(2,1)} %collective-permute-done.15.gout_ref, ...), custom_call_target="tpu_custom_call" | custom-call | tf_op jit(solution)/shard_map/feed/pallas_call | solution.py:1216
  314.3 91.7 %cotangent.1 = (bf16[256,1024]{1,0:T(8,128)(2,1)}, f32[128,1024]{1,0:T(8,128)}, bf16[2,512,256]{2,1,0:T(8,128)(2,1)}, f32[8,1024]{1,0:T(8,128)}, f32[2,1024]{1,0...) custom-call(f32[256,1024]{1,0:T(8,128)} %get-tuple-element.62.middle, ...), custom_call_target="tpu_custom_call" | custom-call | tf_op jit(solution)/shard_map/cotangent/pallas_call | solution.py:1216
  413.4 39.4 %psum.7 = f32[3456]{0:T(1024)S(1)} all-reduce(f32[3456]{0:T(1024)S(1)} %concatenate.81), channel_id=1, replica_groups=mesh['dp'=8,'state'=4] {'dp','state'}, use_global_device_ids=true, to_apply=%region_4.5 | all-reduce | flops 3456 | bytes 27648 | tf_op jit(solution)/shard_map/psum | solution.py:1470
  453.4 110.2 %plane.1 = (bf16[256,1024]{1,0:T(8,128)(2,1)}, bf16[256,1024]{1,0:T(8,128)(2,1)}, bf16[256,768]{1,0:T(8,128)(2,1)}, bf16[256,768]{1,0:T(8,128)(2,1)}, bf16[256,7...) custom-call(bf16[1024,1024]{1,0:T(8,128)(2,1)} %get-tuple-element.87.refs_0_, bf16[1024,1024]{1,0:T(8,128)(2,1)} %get-tuple-element.88.refs_1_, ...), custom_call_target="tpu_custom_call" | custom-call | tf_op jit(solution)/shard_map/plane/pallas_call | solution.py:1216
  582.6 4.1 collective-permute-start.30
  590.0 11.6 %collective-permute-done.30 = bf16[128,768]{1,0:T(8,128)(2,1)S(1)} collective-permute-done((bf16[128,768]{1,0:T(8,128)(2,1)S(1)}, bf16[128,768]{1,0:T(8,128)(2,1)S(1)}, u32[]{:S(2)}, u32[]{:S(2)}) %collective-permute-start.30) | collective-permute-done | bytes 196640 | tf_op jit(solution)/shard_map/ppermute | solution.py:1281
  601.6 3.4 collective-permute-start.26
  605.1 4.9 collective-permute-done.32
  610.0 3.4 collective-permute-start.28
  616.7 4.6 all-to-all-start
  624.6 3.6 collective-permute-start.19
  628.2 3.5 collective-permute-start.21
  639.9 13.6 %collective-permute-done.19 = bf16[256,1024]{1,0:T(8,128)(2,1)S(1)} collective-permute-done((bf16[256,1024]{1,0:T(8,128)(2,1)}, bf16[256,1024]{1,0:T(8,128)(2,1)S(1)}, u32[]{:S(2)}, u32[]{:S(2)}) %collective-permute-start.19) | collective-permute-done | bytes 524320 | tf_op jit(solution)/shard_map/ppermute | solution.py:1281
  653.5 11.2 %collective-permute-done.21 = bf16[2,512,256]{2,1,0:T(8,128)(2,1)S(1)} collective-permute-done((bf16[2,512,256]{2,1,0:T(8,128)(2,1)}, bf16[2,512,256]{2,1,0:T(8,128)(2,1)S(1)}, u32[]{:S(2)}, u32[]{:S(2)}) %collective-permute-start.21) | collective-permute-done | bytes 524320 | tf_op jit(solution)/shard_map/ppermute | solution.py:1281
  666.6 7.6 %collective-permute-done.16 = bf16[256,1024]{1,0:T(8,128)(2,1)S(1)} collective-permute-done((bf16[256,1024]{1,0:T(8,128)(2,1)S(1)}, bf16[256,1024]{1,0:T(8,128)(2,1)S(1)}, u32[]{:S(2)}, u32[]{:S(2)}) %collective-permute-start.16) | collective-permute-done | bytes 524320 | tf_op jit(solution)/shard_map/ppermute | solution.py:1281
  (178 shorter events, 86.3 us)
Async XLA Ops:
  7.2 36.3 %collective-permute-start.10 = (bf16[128,256]{1,0:T(8,128)(2,1)}, bf16[128,256]{1,0:T(8,128)(2,1)S(1)}, u32[]{:S(2)}, u32[]{:S(2)}) collective-permute-start(bf16[128,256]{1,0:T(8,128)(2,1)} %param.27), channel_id=1, source_target_pairs={{0,2},{1,6},{2,3},{3,7},{4,0},{5,4},{6,1},{7,5},{8,10},{9,14},{10,... | collective-permute-start | bytes 196616 | tf_op jit(solution)/shard_map/ppermute | solution.py:1280
  7.3 37.3 %collective-permute-start.9 = (bf16[128,256]{1,0:T(8,128)(2,1)}, bf16[128,256]{1,0:T(8,128)(2,1)}, u32[]{:S(2)}, u32[]{:S(2)}) collective-permute-start(bf16[128,256]{1,0:T(8,128)(2,1)} %param.27), channel_id=1, source_target_pairs={{0,0},{1,4},{2,1},{3,5},{4,2},{5,6},{6,3},{7,7},{8,8},{9,12},{10,9... | collective-permute-start | bytes 196616 | tf_op jit(solution)/shard_map/ppermute | solution.py:1279
  15.7 30.8 %collective-permute-start.6 = (bf16[128,768]{1,0:T(8,128)(2,1)S(1)}, bf16[128,768]{1,0:T(8,128)(2,1)}, u32[]{:S(2)}, u32[]{:S(2)}) collective-permute-start(bf16[128,768]{1,0:T(8,128)(2,1)S(1)} %copy.107), channel_id=1, source_target_pairs={{0,2},{1,6},{2,3},{3,7},{4,0},{5,4},{6,1},{7,5},{8,10},{9,14},{10,... | collective-permute-start | bytes 589832 | tf_op jit(solution)/shard_map/ppermute | solution.py:1280
  15.8 32.1 %collective-permute-start.5 = (bf16[128,768]{1,0:T(8,128)(2,1)S(1)}, bf16[128,768]{1,0:T(8,128)(2,1)S(1)}, u32[]{:S(2)}, u32[]{:S(2)}) collective-permute-start(bf16[128,768]{1,0:T(8,128)(2,1)S(1)} %copy.107), channel_id=1, source_target_pairs={{0,0},{1,4},{2,1},{3,5},{4,2},{5,6},{6,3},{7,7},{8,8},{9,12},{10,9... | collective-permute-start | bytes 589832 | tf_op jit(solution)/shard_map/ppermute | solution.py:1279
  43.6 30.2 %collective-permute-start.12 = (bf16[128,1024]{1,0:T(8,128)(2,1)}, bf16[128,1024]{1,0:T(8,128)(2,1)S(1)}, u32[]{:S(2)}, u32[]{:S(2)}) collective-permute-start(bf16[128,1024]{1,0:T(8,128)(2,1)} %param.29), channel_id=1, source_target_pairs={{0,2},{1,6},{2,3},{3,7},{4,0},{5,4},{6,1},{7,5},{8,10},{9,14},{10,... | collective-permute-start | bytes 786440 | tf_op jit(solution)/shard_map/ppermute | solution.py:1280
  44.6 33.6 %collective-permute-start.11 = (bf16[128,1024]{1,0:T(8,128)(2,1)}, bf16[128,1024]{1,0:T(8,128)(2,1)S(1)}, u32[]{:S(2)}, u32[]{:S(2)}) collective-permute-start(bf16[128,1024]{1,0:T(8,128)(2,1)} %param.29), channel_id=1, source_target_pairs={{0,0},{1,4},{2,1},{3,5},{4,2},{5,6},{6,3},{7,7},{8,8},{9,12},{10,9... | collective-permute-start | bytes 786440 | tf_op jit(solution)/shard_map/ppermute | solution.py:1279
  46.5 33.6 %collective-permute-start.14 = (bf16[128,1024]{1,0:T(8,128)(2,1)}, bf16[128,1024]{1,0:T(8,128)(2,1)S(1)}, u32[]{:S(2)}, u32[]{:S(2)}) collective-permute-start(bf16[128,1024]{1,0:T(8,128)(2,1)} %param.30), channel_id=1, source_target_pairs={{0,2},{1,6},{2,3},{3,7},{4,0},{5,4},{6,1},{7,5},{8,10},{9,14},{10,... | collective-permute-start | bytes 786440 | tf_op jit(solution)/shard_map/ppermute | solution.py:1280
  53.2 31.2 %collective-permute-start.13 = (bf16[128,1024]{1,0:T(8,128)(2,1)}, bf16[128,1024]{1,0:T(8,128)(2,1)S(1)}, u32[]{:S(2)}, u32[]{:S(2)}) collective-permute-start(bf16[128,1024]{1,0:T(8,128)(2,1)} %param.30), channel_id=1, source_target_pairs={{0,0},{1,4},{2,1},{3,5},{4,2},{5,6},{6,3},{7,7},{8,8},{9,12},{10,9... | collective-permute-start | bytes 786440 | tf_op jit(solution)/shard_map/ppermute | solution.py:1279
  58.4 37.3 %collective-permute-start.2 = (bf16[2,512,256]{2,1,0:T(8,128)(2,1)}, bf16[2,512,256]{2,1,0:T(8,128)(2,1)S(1)}, u32[]{:S(2)}, u32[]{:S(2)}) collective-permute-start(bf16[2,512,256]{2,1,0:T(8,128)(2,1)} %bitcast.52), channel_id=1, source_target_pairs={{0,0},{1,4},{2,1},{3,5},{4,2},{5,6},{6,3},{7,7},{8,8},{9,12},{10,9... | collective-permute-start | bytes 1572872 | tf_op jit(solution)/shard_map/ppermute | solution.py:1279
  73.8 21.9 %collective-permute-start.1 = (f32[128,1024]{1,0:T(8,128)S(1)}, f32[128,1024]{1,0:T(8,128)S(1)}, u32[]{:S(2)}, u32[]{:S(2)}) collective-permute-start(f32[128,1024]{1,0:T(8,128)S(1)} %bitcast_select_fusion), channel_id=1, source_target_pairs={{0,0},{1,4},{2,1},{3,5},{4,2},{5,6},{6,3},{7,7},{8,8},{9,12},{10,9... | collective-permute-start | bytes 1572872 | tf_op jit(solution)/shard_map/ppermute | solution.py:1279
  78.2 18.3 %collective-permute-start = (bf16[256,1024]{1,0:T(8,128)(2,1)}, bf16[256,1024]{1,0:T(8,128)(2,1)S(1)}, u32[]{:S(2)}, u32[]{:S(2)}) collective-permute-start(bf16[256,1024]{1,0:T(8,128)(2,1)} %bitcast.68), channel_id=1, source_target_pairs={{0,0},{1,4},{2,1},{3,5},{4,2},{5,6},{6,3},{7,7},{8,8},{9,12},{10,9... | collective-permute-start | bytes 1572872 | tf_op jit(solution)/shard_map/ppermute | solution.py:1279
  80.2 177.5 %collective-permute-start.15 = (bf16[256,1024]{1,0:T(8,128)(2,1)}, bf16[256,1024]{1,0:T(8,128)(2,1)}, u32[]{:S(2)}, u32[]{:S(2)}) collective-permute-start(bf16[256,1024]{1,0:T(8,128)(2,1)} %bitcast.69), channel_id=1, source_target_pairs={{0,0},{1,4},{2,1},{3,5},{4,2},{5,6},{6,3},{7,7},{8,8},{9,12},{10,9... | collective-permute-start | bytes 1572872 | tf_op jit(solution)/shard_map/ppermute | solution.py:1279
  85.1 228.4 %collective-permute-start.18 = (f32[128,1024]{1,0:T(8,128)}, f32[128,1024]{1,0:T(8,128)S(1)}, u32[]{:S(2)}, u32[]{:S(2)}) collective-permute-start(f32[128,1024]{1,0:T(8,128)} %bitcast.70), channel_id=1, source_target_pairs={{0,0},{1,4},{2,1},{3,5},{4,2},{5,6},{6,3},{7,7},{8,8},{9,12},{10,9... | collective-permute-start | bytes 1572872 | tf_op jit(solution)/shard_map/ppermute | solution.py:1279
  576.8 61.0 %collective-permute-start.17 = (bf16[128,1024]{1,0:T(8,128)(2,1)S(1)}, bf16[128,1024]{1,0:T(8,128)(2,1)S(1)}, u32[]{:S(2)}, u32[]{:S(2)}) collective-permute-start(bf16[128,1024]{1,0:T(8,128)(2,1)S(1)} %convert_element_type.103), channel_id=1, source_target_pairs={{0,0},{4,1},{1,2},{5,3},{2,4},{6,5},{3,6},{7,7},{8,8},{12,9},{9,10... | collective-permute-start | bytes 786440 | tf_op jit(solution)/shard_map/ppermute | solution.py:1281
  579.6 41.7 %collective-permute-start.20 = (bf16[128,1024]{1,0:T(8,128)(2,1)}, bf16[128,1024]{1,0:T(8,128)(2,1)S(1)}, u32[]{:S(2)}, u32[]{:S(2)}) collective-permute-start(bf16[128,1024]{1,0:T(8,128)(2,1)} %convert_element_type.105), channel_id=1, source_target_pairs={{0,0},{4,1},{1,2},{5,3},{2,4},{6,5},{3,6},{7,7},{8,8},{12,9},{9,10... | collective-permute-start | bytes 786440 | tf_op jit(solution)/shard_map/ppermute | solution.py:1281
  582.6 19.0 %collective-permute-start.30 = (bf16[128,768]{1,0:T(8,128)(2,1)S(1)}, bf16[128,768]{1,0:T(8,128)(2,1)S(1)}, u32[]{:S(2)}, u32[]{:S(2)}) collective-permute-start(bf16[128,768]{1,0:T(8,128)(2,1)S(1)} %get-tuple-element.182), channel_id=1, source_target_pairs={{0,0},{4,1},{1,2},{5,3},{2,4},{6,5},{3,6},{7,7},{8,8},{12,9},{9,10... | collective-permute-start | bytes 589832 | tf_op jit(solution)/shard_map/ppermute | solution.py:1281
  587.3 22.7 %collective-permute-start.32 = (bf16[128,768]{1,0:T(8,128)(2,1)S(1)}, bf16[128,768]{1,0:T(8,128)(2,1)S(1)}, u32[]{:S(2)}, u32[]{:S(2)}) collective-permute-start(bf16[128,768]{1,0:T(8,128)(2,1)S(1)} %get-tuple-element.180), channel_id=1, source_target_pairs={{0,0},{4,1},{1,2},{5,3},{2,4},{6,5},{3,6},{7,7},{8,8},{12,9},{9,10... | collective-permute-start | bytes 589832 | tf_op jit(solution)/shard_map/ppermute | solution.py:1281
  601.6 23.0 %collective-permute-start.26 = (bf16[128,1024]{1,0:T(8,128)(2,1)S(1)}, bf16[128,1024]{1,0:T(8,128)(2,1)}, u32[]{:S(2)}, u32[]{:S(2)}) collective-permute-start(bf16[128,1024]{1,0:T(8,128)(2,1)S(1)} %get-tuple-element.178), channel_id=1, source_target_pairs={{0,0},{4,1},{1,2},{5,3},{2,4},{6,5},{3,6},{7,7},{8,8},{12,9},{9,10... | collective-permute-start | bytes 786440 | tf_op jit(solution)/shard_map/ppermute | solution.py:1281
  610.0 24.0 %collective-permute-start.28 = (bf16[128,1024]{1,0:T(8,128)(2,1)S(1)}, bf16[128,1024]{1,0:T(8,128)(2,1)}, u32[]{:S(2)}, u32[]{:S(2)}) collective-permute-start(bf16[128,1024]{1,0:T(8,128)(2,1)S(1)} %get-tuple-element.176), channel_id=1, source_target_pairs={{0,0},{4,1},{1,2},{5,3},{2,4},{6,5},{3,6},{7,7},{8,8},{12,9},{9,10... | collective-permute-start | bytes 786440 | tf_op jit(solution)/shard_map/ppermute | solution.py:1281
  616.7 21.9 %all-to-all-start = ((bf16[128,3,1,256]{3,1,2,0:T(4,128)(2,1)}), bf16[128,3,1,256]{3,1,2,0:T(4,128)(2,1)S(1)}, u32[]{:S(2)}, u32[]{:S(2)}) async-start(bf16[128,3,1,256]{3,1,2,0:T(4,128)(2,1)} %copy.118), calls=%async_computation | async-start | bytes 524288 | tf_op jit(solution)/shard_map/all_to_all | solution.py:1456
  621.4 52.9 %reduce-scatter.4.cloned.1.call-start = ((), (), s32[]{:S(2)}) async-start(), calls=%async_computation.2 | async-start | bytes 294912
  624.6 29.0 %collective-permute-start.19 = (bf16[256,1024]{1,0:T(8,128)(2,1)}, bf16[256,1024]{1,0:T(8,128)(2,1)S(1)}, u32[]{:S(2)}, u32[]{:S(2)}) collective-permute-start(bf16[256,1024]{1,0:T(8,128)(2,1)} %get-tuple-element.84), channel_id=1, source_target_pairs={{0,0},{4,1},{1,2},{5,3},{2,4},{6,5},{3,6},{7,7},{8,8},{12,9},{9,10... | collective-permute-start | bytes 1572872 | tf_op jit(solution)/shard_map/ppermute | solution.py:1281
  628.2 36.6 %collective-permute-start.21 = (bf16[2,512,256]{2,1,0:T(8,128)(2,1)}, bf16[2,512,256]{2,1,0:T(8,128)(2,1)S(1)}, u32[]{:S(2)}, u32[]{:S(2)}) collective-permute-start(bf16[2,512,256]{2,1,0:T(8,128)(2,1)} %get-tuple-element.86), channel_id=1, source_target_pairs={{0,0},{4,1},{1,2},{5,3},{2,4},{6,5},{3,6},{7,7},{8,8},{12,9},{9,10... | collective-permute-start | bytes 1572872 | tf_op jit(solution)/shard_map/ppermute | solution.py:1281
  634.0 40.2 %collective-permute-start.16 = (bf16[256,1024]{1,0:T(8,128)(2,1)S(1)}, bf16[256,1024]{1,0:T(8,128)(2,1)S(1)}, u32[]{:S(2)}, u32[]{:S(2)}) collective-permute-start(bf16[256,1024]{1,0:T(8,128)(2,1)S(1)} %copy-done.17), channel_id=1, source_target_pairs={{0,0},{4,1},{1,2},{5,3},{2,4},{6,5},{3,6},{7,7},{8,8},{12,9},{9,10... | collective-permute-start | bytes 1572872 | tf_op jit(solution)/shard_map/ppermute | solution.py:1281
  (32 other events, 461.9 us)
Sparse Core Ops, SparseCore 0:
  625.8 34.4 reduce-scatter.3

commit v3 on v1

--- a/solution.py
+++ b/solution.py
@@ -3,6 +3,8 @@
 import jax
 import jax.numpy as jnp
 from jax import lax
+from jax.experimental import pallas as pl
+from jax.experimental.pallas import tpu as pltpu
 from jax.sharding import PartitionSpec as P
 
 DH = 128
@@ -515,6 +517,1340 @@
     )
 
 
+MESH = pl.DeviceIdType.MESH
+NN = (((1,), (0,)), ((), ()))
+NT = (((1,), (1,)), ((), ()))
+TN = (((0,), (0,)), ((), ()))
+VMEM_BYTES = 63 * 2**20
+
+
+class Place:
+    def __init__(self):
+        chip_core, level = lax.axis_index("dp"), lax.axis_index("state")
+        core, low = lax.rem(chip_core, 2), lax.rem(level, 2)
+        x, y = lax.rem(chip_core // 2, 2), chip_core // 4
+        flip = lambda bit: 1 - 2 * bit
+        self.dp, self.core, self.level, self.half = chip_core, core, level, level // 2
+        self.rank = 2 * low + core
+        self.ranks = [self.rank, 2 * low + 1 - core, 2 * (1 - low) + core, 2 * (1 - low) + 1 - core]
+        self.mates = [
+            None,
+            (chip_core + flip(core), level),
+            (chip_core, level + flip(low)),
+            (chip_core + flip(core), level + flip(low)),
+        ]
+        self.planes = [2 * y + x, 2 * y + 1 - x, 2 * (1 - y) + x, 2 * (1 - y) + 1 - x]
+        self.plane_mates = [
+            None,
+            (chip_core + 2 * flip(x), level),
+            (chip_core + 4 * flip(y), level),
+            (chip_core + 2 * flip(x) + 4 * flip(y), level),
+        ]
+        first = chip_core - core
+        self.there = (first + low, 2 * core + self.half)
+        self.across = (first + low, 2 * (1 - core) + self.half)
+        self.from_there = (first + self.half, 2 * low + core)
+        self.from_across = (first + 1 - self.half, 2 * low + core)
+        self.stays = (core == low) & (self.half == core)
+
+
+def rows_at(start, size, step=128):
+    return pl.ds(pl.multiple_of(start, step), size)
+
+
+class Links:
+    def __init__(self, send_sems, recv_sems):
+        self.send_sems, self.recv_sems = send_sems, recv_sems
+        self.used = 0
+        self.open_sends = []
+        self.open_turns = []
+
+    def plan(self, source, target, device):
+        at = self.used
+        self.used += 1
+        return pltpu.make_async_remote_copy(
+            src_ref=source,
+            dst_ref=target,
+            send_sem=self.send_sems.at[at],
+            recv_sem=self.recv_sems.at[at],
+            device_id=device,
+            device_id_type=MESH,
+        )
+
+    def copy(self, source, target, device):
+        moved = self.plan(source, target, device)
+        moved.start()
+        self.open_sends.append(moved)
+        return moved
+
+    def sent(self, moved):
+        self.open_sends = [other for other in self.open_sends if other is not moved]
+        moved.wait_send()
+
+    def close(self):
+        for moved in self.open_sends:
+            moved.wait_send()
+        for turn in self.open_turns:
+            turn.sent()
+        self.open_sends, self.open_turns = [], []
+
+
+def greet(devices, turned=None):
+    barrier = pltpu.get_barrier_semaphore()
+    for device in devices:
+        pl.semaphore_signal(barrier, inc=1, device_id=device, device_id_type=MESH)
+    if turned is None:
+        pl.semaphore_wait(barrier, len(devices))
+    else:
+        moves = jnp.logical_not(turned.stays)
+
+        @pl.when(moves)
+        def _():
+            pl.semaphore_signal(barrier, inc=1, device_id=turned.from_there, device_id_type=MESH)
+
+        pl.semaphore_wait(barrier, len(devices) + moves.astype(jnp.int32))
+
+
+class Turn:
+    def __init__(self, links, here, source, target, device):
+        self.stays = here.stays
+        self.moved = links.plan(source, target, device)
+        self.kept = pltpu.make_async_copy(source, target, links.recv_sems.at[links.used - 1])
+        links.open_turns.append(self)
+
+        @pl.when(jnp.logical_not(self.stays))
+        def _():
+            self.moved.start()
+
+        @pl.when(self.stays)
+        def _():
+            self.kept.start()
+
+    def arrived(self):
+        @pl.when(jnp.logical_not(self.stays))
+        def _():
+            self.moved.wait_recv()
+
+        @pl.when(self.stays)
+        def _():
+            self.kept.wait()
+
+    def sent(self):
+        @pl.when(jnp.logical_not(self.stays))
+        def _():
+            self.moved.wait_send()
+
+
+class WeightGather:
+    def __init__(self, links, here, local, full):
+        self.links, self.here, self.local, self.full = links, here, local, full
+        self.rows = local.shape[0]
+
+    def enter(self):
+        target = self.full.at[rows_at(self.here.dp * self.rows, self.rows)]
+        self.turn = Turn(self.links, self.here, self.local, target, self.here.there)
+        self.cross = self.links.copy(self.local, target, self.here.across)
+        return self
+
+    def block(self, k):
+        return self.full.at[rows_at(self.here.planes[k] * 2 * self.rows, 2 * self.rows)]
+
+    def half(self, k, which):
+        start = self.here.planes[k] * 2 * self.rows + which * self.rows
+        return self.full.at[rows_at(start, self.rows)]
+
+    def spread(self):
+        self.turn.arrived()
+        self.cross.wait_recv()
+        mates = self.here.plane_mates
+        self.over_x = self.links.copy(self.block(0), self.block(0), mates[1])
+        self.over_y = self.links.copy(self.block(0), self.block(0), mates[2])
+
+    def forward(self):
+        mates = self.here.plane_mates
+        self.over_x.wait_recv()
+        self.corner_0 = self.links.copy(self.half(1, 0), self.half(1, 0), mates[2])
+        self.over_y.wait_recv()
+        self.corner_1 = self.links.copy(self.half(2, 1), self.half(2, 1), mates[1])
+
+    def finish(self):
+        self.corner_0.wait_recv()
+        self.corner_1.wait_recv()
+
+
+class GateGather:
+    def __init__(self, links, here, local, full, sem):
+        self.links, self.here, self.local, self.full, self.sem = links, here, local, full, sem
+        self.rows = local.shape[0]
+
+    def block(self, k):
+        start = (2 * self.here.planes[k] + self.here.core) * self.rows
+        return self.full.at[rows_at(start, self.rows)]
+
+    def part(self, k, which):
+        size = self.rows // 2
+        start = (2 * self.here.planes[k] + self.here.core) * self.rows + which * size
+        return self.full.at[rows_at(start, size, 64)]
+
+    def spread(self):
+        mates, sibling = self.here.plane_mates, self.here.mates[1]
+        self.over_x = self.links.copy(self.local, self.block(0), mates[1])
+        self.over_y = self.links.copy(self.local, self.block(0), mates[2])
+        self.near = [self.links.copy(self.local, self.block(0), sibling)]
+        self.kept = pltpu.make_async_copy(self.local, self.block(0), self.sem)
+        self.kept.start()
+
+    def forward(self):
+        mates, sibling = self.here.plane_mates, self.here.mates[1]
+        self.over_x.wait_recv()
+        self.corner_0 = self.links.copy(self.part(1, 0), self.part(1, 0), mates[2])
+        self.near.append(self.links.copy(self.block(1), self.block(1), sibling))
+        self.over_y.wait_recv()
+        self.corner_1 = self.links.copy(self.part(2, 1), self.part(2, 1), mates[1])
+        self.near.append(self.links.copy(self.block(2), self.block(2), sibling))
+
+    def last(self):
+        self.corner_0.wait_recv()
+        self.corner_1.wait_recv()
+        self.near.append(self.links.copy(self.block(3), self.block(3), self.here.mates[1]))
+
+    def finish(self):
+        self.kept.wait()
+        for moved in self.near:
+            moved.wait_recv()
+
+
+class RowGather:
+    def __init__(self, links, here, ref, base, rows):
+        self.links, self.here, self.ref, self.base, self.rows = links, here, ref, base, rows
+
+    def part(self, k):
+        return self.ref.at[rows_at(self.base + self.here.ranks[k] * self.rows, self.rows)]
+
+    def start(self):
+        own, mates = self.part(0), self.here.mates
+        self.far = self.links.copy(own, own, mates[2])
+        self.near = self.links.copy(own, own, mates[1])
+        return self
+
+    def ready(self, k):
+        if k == 1:
+            self.near.wait_recv()
+        elif k == 2:
+            self.far.wait_recv()
+            block = self.part(2)
+            self.last = self.links.copy(block, block, self.here.mates[1])
+        elif k == 3:
+            self.last.wait_recv()
+
+    def sent(self):
+        for moved in (self.far, self.near, self.last):
+            self.links.sent(moved)
+
+
+class RowSum:
+    def __init__(self, links, here, stage, near_in, far_out, far_in, rows):
+        self.links, self.here, self.rows = links, here, rows
+        self.stage, self.near_in, self.far_out, self.far_in = stage, near_in, far_out, far_in
+
+    def part(self, k):
+        return self.stage.at[rows_at(self.here.ranks[k] * self.rows, self.rows)]
+
+    def fill(self, make_rows):
+        sibling = self.here.mates[1]
+        for k, slot in ((3, 0), (1, 1)):
+            self.part(k)[...] = make_rows(self.here.ranks[k]).astype(jnp.bfloat16)
+            moved = self.links.copy(self.part(k), self.near_in.at[slot], sibling)
+            if slot == 0:
+                self.near_far = moved
+            else:
+                self.near_own = moved
+        for k in (2, 0):
+            self.part(k)[...] = make_rows(self.here.ranks[k]).astype(jnp.bfloat16)
+        return self
+
+    def forward(self):
+        self.near_far.wait_recv()
+        summed = self.part(2)[...].astype(jnp.float32) + self.near_in[0].astype(jnp.float32)
+        self.far_out[...] = summed.astype(jnp.bfloat16)
+        self.far = self.links.copy(self.far_out, self.far_in, self.here.mates[2])
+        return self
+
+    def sent(self):
+        for moved in (self.near_far, self.near_own, self.far):
+            self.links.sent(moved)
+
+    def finish(self):
+        self.near_own.wait_recv()
+        self.far.wait_recv()
+        return (
+            self.part(0)[...].astype(jnp.float32)
+            + self.near_in[1].astype(jnp.float32)
+            + self.far_in[...].astype(jnp.float32)
+        )
+
+
+def row_sum_scratch(rows, width):
+    return [
+        pltpu.VMEM((4 * rows, width), jnp.bfloat16),
+        pltpu.VMEM((2, rows, width), jnp.bfloat16),
+        pltpu.VMEM((rows, width), jnp.bfloat16),
+        pltpu.VMEM((rows, width), jnp.bfloat16),
+    ]
+
+
+def dot(left, right, dims):
+    return lax.dot_general(left, right, dims, preferred_element_type=jnp.float32)
+
+
+def scale_of(tensor):
+    return lax.rsqrt(jnp.mean(tensor * tensor, axis=-1, keepdims=True) + EPS)
+
+
+def rms_back(tensor, gains_row, cotangent):
+    scale = scale_of(tensor)
+    weighted = cotangent * gains_row
+    inner = jnp.mean(tensor * weighted, axis=-1, keepdims=True)
+    straight = scale * weighted - tensor * (scale * scale * scale * inner)
+    return straight, jnp.sum(cotangent * tensor * scale, axis=0, keepdims=True)
+
+
+def row_mask(facts, start, rows):
+    place_of = lax.broadcasted_iota(jnp.int32, (rows, 1), 0) + start
+    return jnp.where(place_of.astype(jnp.float32) < facts[2:3, 0:1], 1.0, 0.0)
+
+
+def bias_tiles(lines_ref, tiles_ref, heads, width):
+    for head in range(heads):
+        line = lines_ref[head : head + 1, :]
+        spread = jnp.broadcast_to(line, (tiles_ref.shape[1], line.shape[1]))
+        tiles_ref[head] = pltpu.roll(spread, 0, 1, stride=1, stride_axis=0)[:, :width]
+
+
+def softmax_pair(first, second):
+    top = jnp.maximum(
+        jnp.max(first, axis=-1, keepdims=True), jnp.max(second, axis=-1, keepdims=True)
+    )
+    first, second = jnp.exp(first - top), jnp.exp(second - top)
+    total = jnp.sum(first, axis=-1, keepdims=True) + jnp.sum(second, axis=-1, keepdims=True)
+    share = 1.0 / total
+    return (
+        (first * share).astype(jnp.bfloat16),
+        (second * share).astype(jnp.bfloat16),
+        top + jnp.log(total),
+    )
+
+
+TILE = 256
+ROOT = 1.0 / math.sqrt(DH)
+
+
+def forward_kernel(
+    x_in, carried_in, initial_in, far_past, facts_in, far_gout, far_gstate, gains_ref,
+    wst_in, wtok_in, wout_in, gates_in, far_wup, far_wdn,
+    normed, snormed, queries, keys, values, state_qkv, lse_ref, mixed, smixed,
+    far_gate_values, s1_ref, s2_ref, wst, wtok, wout, gates, x_ref, s0_ref, facts, far_gstate_here,
+    block_out, middle_grad, far_wup_grad, far_wdn_grad, small_sums,
+    tiles, a2a_0, a2a_1, initial_all, normed_send, s0_send, gate_values, wup, wdn, middle,
+    middle_normed, gout_rows, gout, slope, hidden, up_grad, grad_stage, *rest,
+):
+    rs = [rest[4 * k : 4 * k + 4] for k in range(4)]
+    links = Links(rest[16], rest[17])
+    local_sems = rest[18]
+    here = Place()
+    rank, ranks, mates = here.rank, here.ranks, here.mates
+    rows = s0_ref.shape[0]
+    window = 4 * rows
+    width = queries.shape[1]
+    heads = width // DH
+    ring = [(lax.rem(here.dp + step, 8), here.level) for step in range(1, 8)]
+    greet(ring + mates[2:] + [here.from_across], here)
+
+    def turn(source, target):
+        return Turn(links, here, source, target, here.there)
+
+    part = initial_in.shape[1]
+    own_columns = pl.ds(pl.multiple_of(here.dp * part, part), part)
+    initial_moves = [links.copy(initial_in, initial_all.at[:, own_columns], mate) for mate in ring]
+    facts_turn = turn(facts_in, facts)
+    gather_wst = WeightGather(links, here, wst_in, wst).enter()
+    initial_all[:, own_columns] = initial_in[...]
+    for moved in initial_moves:
+        moved.wait_recv()
+    is_fresh = facts_in[3:4, :] > 0.5
+    start = jnp.where(is_fresh, initial_all[...].astype(jnp.float32), carried_in[...])
+    s0_send[...] = start
+    normed_send[...] = (start * scale_of(start) * gains_ref[2:3, :]).astype(jnp.bfloat16)
+    normed_turn = turn(normed_send, snormed.at[rows_at(here.level * rows, rows)])
+    x_turn = turn(x_in, x_ref)
+    gather_wtok = WeightGather(links, here, wtok_in, wtok).enter()
+    facts_turn.arrived()
+    bias_tiles(facts, tiles, heads, 3 * TILE)
+    normed_turn.arrived()
+    gather_s0 = RowGather(links, here, snormed, 0, rows).start()
+    gather_wst.spread()
+    past_turns = [
+        turn(far_past.at[0], keys.at[pl.ds(0, window)]),
+        turn(far_past.at[1], values.at[pl.ds(0, window)]),
+    ]
+    gather_wout = WeightGather(links, here, wout_in, wout).enter()
+    x_turn.arrived()
+    gather_x = []
+    for block in range(2):
+        x = x_ref[block * rows : (block + 1) * rows, :].astype(jnp.float32)
+        normed[rows_at(block * window + rank * rows, rows), :] = (
+            x * scale_of(x) * gains_ref[0:1, :]
+        ).astype(jnp.bfloat16)
+        gather_x.append(RowGather(links, here, normed, block * window, rows).start())
+    gather_wst.forward()
+    gather_wtok.spread()
+    s0_turn = turn(s0_send, s0_ref)
+
+    def key_mask(start, size):
+        place_of = lax.broadcasted_iota(jnp.int32, (1, size), 1).astype(jnp.float32)
+        place_of = place_of + float(start - window)
+        own = jnp.where(place_of < facts[2:3, 0:size], 0.0, NEGATIVE)
+        return jnp.where(place_of < 0.0, facts[3:4, 0:size] * NEGATIVE, own)
+
+    def project_state(block, gather):
+        for k in range(4):
+            gather.ready(k)
+            at = rows_at(block * window + ranks[k] * rows, rows)
+            state_qkv[at, :] = dot(snormed[at, :], wst[...], NN).astype(jnp.bfloat16)
+
+    def project_token(block, gather):
+        for k in range(4):
+            gather.ready(k)
+            at = rows_at(block * window + ranks[k] * rows, rows)
+            later = rows_at((block + 1) * window + ranks[k] * rows, rows)
+            out = dot(normed[at, :], wtok[...], NN).astype(jnp.bfloat16)
+            queries[at, :] = out[:, :width]
+            keys[later, :] = out[:, width : 2 * width]
+            values[later, :] = out[:, 2 * width :]
+
+    def state_attention(block):
+        base = block * window
+        own = pl.ds((block + 1) * window, window)
+        whole = pl.ds(base, window)
+        own_mask = key_mask(base + window, window)
+        for head in range(heads):
+            at = head * DH
+            for tile in range(window // TILE):
+                here_rows = pl.ds(base + tile * TILE, TILE)
+                query = state_qkv[here_rows, at : at + DH]
+                first = dot(query, state_qkv[whole, width + at : width + at + DH], NT) * ROOT
+                second = dot(query, keys[own, at : at + DH], NT) * ROOT + own_mask
+                first, second, lse = softmax_pair(first, second)
+                out = dot(first, state_qkv[whole, 2 * width + at : 2 * width + at + DH], NN)
+                out = out + dot(second, values[own, at : at + DH], NN)
+                smixed[here_rows, at : at + DH] = out.astype(jnp.bfloat16)
+                lse_ref[here_rows, heads + head : heads + head + 1] = lse
+
+    def token_attention(block):
+        base = block * window
+        whole = pl.ds(base, window)
+        for tile in range(window // TILE):
+            near_mask = key_mask(base + tile * TILE, 3 * TILE)
+            for head in range(heads):
+                at = head * DH
+                here_rows = pl.ds(base + tile * TILE, TILE)
+                near = pl.ds(base + tile * TILE, 3 * TILE)
+                query = queries[here_rows, at : at + DH]
+                first = dot(query, keys[near, at : at + DH], NT) * ROOT + tiles[head] + near_mask
+                second = dot(query, state_qkv[whole, width + at : width + at + DH], NT) * ROOT
+                first, second, lse = softmax_pair(first, second)
+                out = dot(first, values[near, at : at + DH], NN)
+                out = out + dot(second, state_qkv[whole, 2 * width + at : 2 * width + at + DH], NN)
+                mixed[here_rows, at : at + DH] = out.astype(jnp.bfloat16)
+                lse_ref[here_rows, head : head + 1] = lse
+
+    def spread_state(block, buffer):
+        moves = []
+        columns = pl.ds(pl.multiple_of(rank * width, width), width)
+        for k in (2, 3, 1):
+            source = smixed.at[rows_at(block * window + ranks[k] * rows, rows)]
+            moves.append(links.copy(source, buffer.at[:, columns], mates[k]))
+        buffer[:, columns] = smixed[rows_at(block * window + rank * rows, rows), :]
+        return moves
+
+    def renew(block, buffer, state_now):
+        size = state_now.shape[1]
+        source = buffer[...]
+        parts = []
+        for c in range(3):
+            part = dot(source, gates[:, c * size : (c + 1) * size], NT)
+            gate_values[:, c * size : (c + 1) * size] = part
+            parts.append(part)
+        keep = pltpu.make_async_copy(
+            gate_values, far_gate_values.at[pl.ds(block * rows, rows)], local_sems.at[0]
+        )
+        keep.start()
+        new_state = state_now * jax.nn.sigmoid(parts[2] + 1.0) + jnp.tanh(parts[0]) * jax.nn.sigmoid(
+            parts[1] - 1.0
+        )
+        return new_state, keep
+
+    def branch_rows(block):
+        def make(which):
+            return dot(mixed[rows_at(block * window + which * rows, rows), :], wout[...], NT)
+
+        return make
+
+    sums = [RowSum(links, here, *rs[block], rows) for block in range(2)]
+
+    def finish_branch(block):
+        branch = sums[block].finish()
+        at = slice(block * rows, (block + 1) * rows)
+        total = x_ref[at, :].astype(jnp.float32) + branch
+        middle[at, :] = total
+        middle_normed[rows_at(block * window + rank * rows, rows), :] = (
+            total * scale_of(total) * gains_ref[1:2, :]
+        ).astype(jnp.bfloat16)
+        gather = RowGather(links, here, middle_normed, block * window, rows).start()
+        share = row_mask(facts, block * window + rank * rows, rows)
+        return jnp.sum(branch * branch * share, axis=0, keepdims=True), gather
+
+    def rise(block, gather):
+        root = math.sqrt(2.0 / math.pi)
+        for k in range(4):
+            gather.ready(k)
+            at = rows_at(block * window + ranks[k] * rows, rows)
+            value = dot(middle_normed[at, :], wup[...], NN)
+            square = value * value
+            bend = jnp.tanh(root * value * (1.0 + 0.044715 * square))
+            half = 0.5 * (1.0 + bend)
+            hidden[at, :] = (value * half).astype(jnp.bfloat16)
+            slope[at, :] = half + 0.5 * value * (1.0 - bend * bend) * (
+                root * (1.0 + 3.0 * 0.044715 * square)
+            )
+
+    def feed_sum(block):
+        return RowSum(links, here, *rs[block], rows).fill(
+            lambda which: dot(hidden[rows_at(block * window + which * rows, rows), :], wdn[...], NT)
+        )
+
+    def start_gout(block):
+        at = slice(block * rows, (block + 1) * rows)
+        gout[rows_at(block * window + rank * rows, rows), :] = gout_rows[at, :]
+        return RowGather(links, here, gout, block * window, rows).start()
+
+    def feed_back(block, gather):
+        for k in range(4):
+            gather.ready(k)
+            at = rows_at(block * window + ranks[k] * rows, rows)
+            up_grad[at, :] = (dot(gout[at, :], wdn[...], NN) * slope[at, :]).astype(jnp.bfloat16)
+        return RowSum(links, here, *rs[2 + block], rows).fill(
+            lambda which: dot(up_grad[rows_at(block * window + which * rows, rows), :], wup[...], NT)
+        )
+
+    def weight_grad(stage, left, right, target, sem):
+        step = 256
+        for part in range(stage.shape[0] // step):
+            at = slice(part * step, (part + 1) * step)
+            stage[at, :] = dot(left[:, at], right[...], TN).astype(jnp.bfloat16)
+        keep = pltpu.make_async_copy(stage, target, sem)
+        keep.start()
+        return keep
+
+    gather_wst.finish()
+    project_state(0, gather_s0)
+    gather_wtok.forward()
+    gather_gates = GateGather(links, here, gates_in, gates, local_sems.at[3])
+    gather_gates.spread()
+    gather_wup = WeightGather(links, here, far_wup, wup).enter()
+    gather_wtok.finish()
+    project_token(0, gather_x[0])
+    project_token(1, gather_x[1])
+    for moved in past_turns:
+        moved.arrived()
+    state_attention(0)
+    moves_0 = spread_state(0, a2a_0)
+    gather_wout.spread()
+    gather_gates.forward()
+    gout_turn = turn(far_gout, gout_rows)
+    token_attention(0)
+    gather_wout.forward()
+    gather_gates.last()
+    gather_wdn = WeightGather(links, here, far_wdn, wdn).enter()
+    gather_wup.spread()
+    gather_wout.finish()
+    sums[0].fill(branch_rows(0))
+    for moved in moves_0:
+        moved.wait_recv()
+    gather_gates.finish()
+    s0_turn.arrived()
+    s1, keep_gates = renew(0, a2a_0, s0_ref[...])
+    s1_ref[...] = s1
+    snormed[rows_at(window + rank * rows, rows), :] = (s1 * scale_of(s1) * gains_ref[2:3, :]).astype(
+        jnp.bfloat16
+    )
+    gather_s1 = RowGather(links, here, snormed, window, rows).start()
+    sums[0].forward()
+    gather_wup.forward()
+    gather_wdn.spread()
+    gstate_turn = turn(far_gstate, far_gstate_here)
+    project_state(1, gather_s1)
+    state_attention(1)
+    moves_1 = spread_state(1, a2a_1)
+    branch_total, gather_m0 = finish_branch(0)
+    token_attention(1)
+    gather_wdn.forward()
+    sums[1].fill(branch_rows(1))
+    gather_wup.finish()
+    gout_turn.arrived()
+    gather_g0 = start_gout(0)
+    rise(0, gather_m0)
+    sums[1].forward()
+    for moved in moves_1:
+        moved.wait_recv()
+    keep_gates.wait()
+    s2, keep_gates = renew(1, a2a_1, s1_ref[...])
+    s2_ref[...] = s2.astype(jnp.bfloat16)
+    gather_wdn.finish()
+    sums[0].sent()
+    feed_0 = feed_sum(0)
+    more, gather_m1 = finish_branch(1)
+    branch_total = branch_total + more
+    gather_g1 = start_gout(1)
+    feed_0.forward()
+    back_0 = feed_back(0, gather_g0)
+    rise(1, gather_m1)
+    sums[1].sent()
+    feed_1 = feed_sum(1)
+    back_0.forward()
+    back_1 = feed_back(1, gather_g1)
+    feed_1.forward()
+    keep_down = weight_grad(grad_stage, gout, hidden, far_wdn_grad, local_sems.at[1])
+    back_1.forward()
+    keep_up = weight_grad(hidden, middle_normed, up_grad, far_wup_grad, local_sems.at[2])
+    feed_total, result_total, gain_total = 0.0, 0.0, 0.0
+    for block, feed_here in ((0, feed_0), (1, feed_1)):
+        at = slice(block * rows, (block + 1) * rows)
+        feed = feed_here.finish()
+        result = middle[at, :] + feed
+        block_out[at, :] = result.astype(jnp.bfloat16)
+        share = row_mask(facts, block * window + rank * rows, rows)
+        feed_total = feed_total + jnp.sum(feed * feed * share, axis=0, keepdims=True)
+        result_total = result_total + jnp.sum(result * result * share, axis=0, keepdims=True)
+    for block, back_here in ((1, back_1), (0, back_0)):
+        at = slice(block * rows, (block + 1) * rows)
+        straight, gain = rms_back(middle[at, :], gains_ref[1:2, :], back_here.finish())
+        middle_grad[at, :] = gout_rows[at, :].astype(jnp.float32) + straight
+        gain_total = gain_total + gain
+    small_sums[...] = jnp.concatenate(
+        [gain_total, result_total, branch_total, feed_total]
+        + [jnp.zeros((4, gain_total.shape[1]), jnp.float32)],
+        axis=0,
+    )
+    gstate_turn.arrived()
+    keep_gates.wait()
+    keep_down.wait()
+    keep_up.wait()
+    links.close()
+
+
+class PlaneSum:
+    def __init__(self, links, here, grad, first_in, last_in):
+        self.links, self.here, self.grad = links, here, grad
+        self.first_in, self.last_in = first_in, last_in
+        self.rows = first_in.shape[1]
+
+    def part(self, k, which):
+        start = self.here.planes[k] * 2 * self.rows + which * self.rows
+        return self.grad.at[rows_at(start, self.rows)]
+
+    def start(self):
+        mates = self.here.plane_mates
+        self.firsts = [
+            self.links.copy(self.part(k, which), self.first_in.at[slot], mates[mate])
+            for slot, (k, which, mate) in enumerate(((1, 0, 1), (3, 0, 1), (2, 1, 2), (3, 1, 2)))
+        ]
+        return self
+
+    def add(self, k, which, arrived):
+        part = self.part(k, which)
+        part[...] = (part[...].astype(jnp.float32) + arrived[...].astype(jnp.float32)).astype(part.dtype)
+
+    def forward(self):
+        mates = self.here.plane_mates
+        self.firsts[1].wait_recv()
+        self.add(2, 0, self.first_in.at[1])
+        self.last_0 = self.links.copy(self.part(2, 0), self.last_in.at[0], mates[2])
+        self.firsts[3].wait_recv()
+        self.add(1, 1, self.first_in.at[3])
+        self.last_1 = self.links.copy(self.part(1, 1), self.last_in.at[1], mates[1])
+
+    def finish(self):
+        self.firsts[0].wait_recv()
+        self.add(0, 0, self.first_in.at[0])
+        self.firsts[2].wait_recv()
+        self.add(0, 1, self.first_in.at[2])
+        self.last_0.wait_recv()
+        self.add(0, 0, self.last_in.at[0])
+        self.last_1.wait_recv()
+        self.add(0, 1, self.last_in.at[1])
+
+    def result(self, which):
+        return self.grad.at[
+            rows_at(self.here.planes[0] * 2 * self.rows + which * self.rows, self.rows)
+        ]
+
+
+class FarPlaneSum(PlaneSum):
+    def __init__(self, links, here, grad, first_in, last_in, forwards, brought, brought_sems):
+        super().__init__(links, here, grad, first_in, last_in)
+        self.forwards = forwards
+        self.brought, self.brought_sems = brought, brought_sems
+
+    def total(self, *pieces):
+        brings = [
+            pltpu.make_async_copy(piece, self.brought.at[slot], self.brought_sems.at[slot])
+            for slot, piece in enumerate(pieces)
+        ]
+        for bring in brings:
+            bring.start()
+        for bring in brings:
+            bring.wait()
+        out = self.brought[0].astype(jnp.float32)
+        for slot in range(1, len(pieces)):
+            out = out + self.brought[slot].astype(jnp.float32)
+        return out.astype(jnp.bfloat16)
+
+    def forward(self):
+        mates = self.here.plane_mates
+        self.firsts[1].wait_recv()
+        self.forwards[0] = self.total(self.part(2, 0), self.first_in.at[1])
+        self.last_0 = self.links.copy(self.forwards.at[0], self.last_in.at[0], mates[2])
+        self.firsts[3].wait_recv()
+        self.forwards[1] = self.total(self.part(1, 1), self.first_in.at[3])
+        self.last_1 = self.links.copy(self.forwards.at[1], self.last_in.at[1], mates[1])
+
+    def finish(self):
+        self.firsts[0].wait_recv()
+        self.last_0.wait_recv()
+        self.links.sent(self.last_0)
+        self.forwards[0] = self.total(self.part(0, 0), self.first_in.at[0], self.last_in.at[0])
+        self.firsts[2].wait_recv()
+        self.last_1.wait_recv()
+        self.links.sent(self.last_1)
+        self.forwards[1] = self.total(self.part(0, 1), self.first_in.at[2], self.last_in.at[1])
+
+    def result(self, which):
+        return self.forwards.at[which]
+
+
+class Settle:
+    def __init__(self, links, here, summed, target):
+        half = here.half
+        self.straight = Turn(links, here, summed.result(half), target.at[0], here.from_there)
+        self.crossed = links.copy(summed.result(1 - half), target.at[1], here.from_across)
+
+    def arrived(self):
+        self.straight.arrived()
+        self.crossed.wait_recv()
+
+
+def cotangent_kernel(
+    middle_grad, gstate_ref, x_ref, s0_ref, s1_ref, far_gate_values, gains_ref, facts, facts_home,
+    small_sums,
+    far_normed, far_snormed, queries, keys, values, state_qkv, lse_ref, mixed, smixed,
+    wst, wtok, wout, gates, far_wup_grad, far_wdn_grad, far_block_out, far_state_out,
+    block_home, state_home, tokens_home, past_home, carried_grad, initial_grad, totals,
+    up_home, down_home, wst_home, wtok_home, wout_home, gates_home,
+    up_first, down_first, up_last, down_last,
+    tiles, tile_grads, branch_grad, mixed_grad, gate_rows, state_mixed_grad, key_grad, value_grad,
+    skey_grad, svalue_grad, token_cot, state_cot, gate_values, sending,
+    tokens_send, carried_send, carried_in, past_send, initial_send, initial_in,
+    wst_grad, wtok_grad, wout_grad, gates_grad,
+    wst_first, wtok_first, wout_first, gates_first, wst_last, wtok_last, wout_last, gates_last,
+    up_forwards, down_forwards, brought, ring_in, level_in, ring_send, level_send,
+    *rest,
+):
+    rs = [rest[0:4], rest[4:8], rest[8:12]]
+    links = Links(rest[12], rest[13])
+    local_sems, brought_sems = rest[14], rest[15]
+    here = Place()
+    rank, ranks, mates = here.rank, here.ranks, here.mates
+    rows = s0_ref.shape[0]
+    window = 4 * rows
+    width = queries.shape[1]
+    heads = width // DH
+    size = s0_ref.shape[1]
+    ring = [(lax.rem(here.dp + step, 8), here.level) for step in range(1, 8)]
+    other = here.dp + 1 - 2 * here.core
+    column = [
+        (chip, lax.rem(here.level + step, 4)) for step in range(1, 4) for chip in (here.dp, other)
+    ]
+    greet(ring + column)
+    bring_gates = pltpu.make_async_copy(
+        far_gate_values.at[pl.ds(rows, rows)], gate_values, local_sems.at[0]
+    )
+    bring_gates.start()
+    branch_gathers = []
+    for block in (1, 0):
+        at = slice(block * rows, (block + 1) * rows)
+        branch_grad[rows_at(block * window + rank * rows, rows), :] = middle_grad[at, :].astype(
+            jnp.bfloat16
+        )
+
+    def home(source, target):
+        return Turn(links, here, source, target, here.from_there)
+
+    def gates_back(block, state, state_grad):
+        spot = rows_at(block * window + rank * rows, rows)
+        keep = jax.nn.sigmoid(gate_values[:, 2 * size : 3 * size] + 1.0)
+        fresh = jnp.tanh(gate_values[:, 0:size])
+        let_in = jax.nn.sigmoid(gate_values[:, size : 2 * size] - 1.0)
+        gate_rows[spot, 0:size] = (state_grad * let_in * (1.0 - fresh * fresh)).astype(jnp.bfloat16)
+        gate_rows[spot, size : 2 * size] = (
+            state_grad * fresh * let_in * (1.0 - let_in)
+        ).astype(jnp.bfloat16)
+        gate_rows[spot, 2 * size : 3 * size] = (
+            state_grad * state * keep * (1.0 - keep)
+        ).astype(jnp.bfloat16)
+        out = dot(gate_rows[spot, 0:size], gates[:, 0:size], NN)
+        out = out + dot(gate_rows[spot, size : 2 * size], gates[:, size : 2 * size], NN)
+        out = out + dot(gate_rows[spot, 2 * size : 3 * size], gates[:, 2 * size : 3 * size], NN)
+        sending[block] = out.astype(jnp.bfloat16)
+        moves = []
+        for k in (2, 3, 1):
+            columns = pl.ds(pl.multiple_of(ranks[k] * width, width), width)
+            moves.append(
+                links.copy(sending.at[block, :, columns], state_mixed_grad.at[spot], mates[k])
+            )
+        columns = pl.ds(pl.multiple_of(rank * width, width), width)
+        state_mixed_grad[spot, :] = sending[block, :, columns]
+        return state_grad * keep, moves
+
+    def key_mask(start, size):
+        place_of = lax.broadcasted_iota(jnp.int32, (1, size), 1).astype(jnp.float32)
+        place_of = place_of + float(start - window)
+        own = jnp.where(place_of < facts[2:3, 0:size], 0.0, NEGATIVE)
+        return jnp.where(place_of < 0.0, facts[3:4, 0:size] * NEGATIVE, own)
+
+    def pair_back(first, second, lse, first_grad, second_grad):
+        first, second = jnp.exp(first - lse), jnp.exp(second - lse)
+        inner = jnp.sum(first * first_grad, axis=-1, keepdims=True) + jnp.sum(
+            second * second_grad, axis=-1, keepdims=True
+        )
+        return (
+            first.astype(jnp.bfloat16),
+            second.astype(jnp.bfloat16),
+            (first * (first_grad - inner)).astype(jnp.bfloat16),
+            (second * (second_grad - inner)).astype(jnp.bfloat16),
+        )
+
+    def token_back(block):
+        base = block * window
+        whole = pl.ds(base, window)
+        for tile in range(window // TILE):
+            near_mask = key_mask(base + tile * TILE, 3 * TILE)
+            for head in range(heads):
+                at = head * DH
+                lanes = slice(at, at + DH)
+                skey_lanes = slice(width + at, width + at + DH)
+                svalue_lanes = slice(2 * width + at, 2 * width + at + DH)
+                here_rows = pl.ds(base + tile * TILE, TILE)
+                near = pl.ds(base + tile * TILE, 3 * TILE)
+                query = queries[here_rows, lanes]
+                out_grad = mixed_grad[here_rows, lanes]
+                first = dot(query, keys[near, lanes], NT) * ROOT + tiles[head] + near_mask
+                second = dot(query, state_qkv[whole, skey_lanes], NT) * ROOT
+                first, second, first_grad, second_grad = pair_back(
+                    first,
+                    second,
+                    lse_ref[here_rows, head : head + 1],
+                    dot(out_grad, values[near, lanes], NT),
+                    dot(out_grad, state_qkv[whole, svalue_lanes], NT),
+                )
+                value_grad[near, lanes] += dot(first, out_grad, TN)
+                svalue_grad[:, lanes] += dot(second, out_grad, TN)
+                part = dot(first_grad, keys[near, lanes], NN) + dot(
+                    second_grad, state_qkv[whole, skey_lanes], NN
+                )
+                token_cot[here_rows, lanes] = (part * ROOT).astype(jnp.bfloat16)
+                key_grad[near, lanes] += dot(first_grad, query, TN) * ROOT
+                skey_grad[:, lanes] += dot(second_grad, query, TN) * ROOT
+                tile_grads[head, :, 0 : 3 * TILE] += first_grad.astype(jnp.float32)
+
+    def state_back(block):
+        base = block * window
+        whole = pl.ds(base, window)
+        own = pl.ds(base + window, window)
+        own_mask = key_mask(base + window, window)
+        for head in range(heads):
+            at = head * DH
+            lanes = slice(at, at + DH)
+            skey_lanes = slice(width + at, width + at + DH)
+            svalue_lanes = slice(2 * width + at, 2 * width + at + DH)
+            for tile in range(window // TILE):
+                here_rows = pl.ds(base + tile * TILE, TILE)
+                query = state_qkv[here_rows, lanes]
+                out_grad = state_mixed_grad[here_rows, lanes]
+                first = dot(query, state_qkv[whole, skey_lanes], NT) * ROOT
+                second = dot(query, keys[own, lanes], NT) * ROOT + own_mask
+                first, second, first_grad, second_grad = pair_back(
+                    first,
+                    second,
+                    lse_ref[here_rows, heads + head : heads + head + 1],
+                    dot(out_grad, state_qkv[whole, svalue_lanes], NT),
+                    dot(out_grad, values[own, lanes], NT),
+                )
+                svalue_grad[:, lanes] += dot(first, out_grad, TN)
+                value_grad[own, lanes] += dot(second, out_grad, TN)
+                part = dot(first_grad, state_qkv[whole, skey_lanes], NN) + dot(
+                    second_grad, keys[own, lanes], NN
+                )
+                state_cot[here_rows, lanes] = (part * ROOT).astype(jnp.bfloat16)
+                skey_grad[:, lanes] += dot(first_grad, query, TN) * ROOT
+                key_grad[own, lanes] += dot(second_grad, query, TN) * ROOT
+
+    def gather_cot(block):
+        whole = pl.ds(block * window, window)
+        own = pl.ds(block * window + window, window)
+        token_cot[whole, width : 2 * width] = key_grad[own, :].astype(jnp.bfloat16)
+        token_cot[whole, 2 * width : 3 * width] = value_grad[own, :].astype(jnp.bfloat16)
+        state_cot[whole, width : 2 * width] = skey_grad[...].astype(jnp.bfloat16)
+        state_cot[whole, 2 * width : 3 * width] = svalue_grad[...].astype(jnp.bfloat16)
+
+    def state_sum(block):
+        return RowSum(links, here, *rs[0], rows).fill(
+            lambda which: dot(state_cot[rows_at(block * window + which * rows, rows), :], wst[...], NT)
+        )
+
+    def token_sum(block):
+        return RowSum(links, here, *rs[1 + block], rows).fill(
+            lambda which: dot(token_cot[rows_at(block * window + which * rows, rows), :], wtok[...], NT)
+        )
+
+    def mix_back(block):
+        for k in range(4):
+            branch_gathers[1 - block].ready(k)
+            at = rows_at(block * window + ranks[k] * rows, rows)
+            mixed_grad[at, :] = dot(branch_grad[at, :], wout[...], NN).astype(jnp.bfloat16)
+
+    def weight_grad(target, left, right, lanes):
+        step = 256
+        for part in range(size // step):
+            at = slice(part * step, (part + 1) * step)
+            target[at, lanes] = dot(left[:, at], right, TN).astype(jnp.bfloat16)
+
+    def finish_tokens(block, summed):
+        at = slice(block * rows, (block + 1) * rows)
+        straight, gain = rms_back(x_ref[at, :].astype(jnp.float32), gains_ref[0:1, :], summed.finish())
+        tokens_send[at, :] = (middle_grad[at, :] + straight).astype(jnp.bfloat16)
+        return gain, home(tokens_send.at[pl.ds(block * rows, rows)], tokens_home.at[pl.ds(block * rows, rows)])
+
+    bring_gates.wait()
+    direct_1, moves_1 = gates_back(1, s1_ref[...], gstate_ref[...])
+    for block in (1, 0):
+        branch_gathers.append(RowGather(links, here, branch_grad, block * window, rows).start())
+    up_sum = FarPlaneSum(
+        links, here, far_wup_grad, up_first, up_last, up_forwards, brought, brought_sems
+    ).start()
+    down_sum = FarPlaneSum(
+        links, here, far_wdn_grad, down_first, down_last, down_forwards, brought, brought_sems
+    ).start()
+    gate_gather_1 = RowGather(links, here, gate_rows, window, rows).start()
+    bring_gates = pltpu.make_async_copy(far_gate_values.at[pl.ds(0, rows)], gate_values, local_sems.at[0])
+    bring_gates.start()
+    for ref in (tile_grads, key_grad, value_grad, skey_grad, svalue_grad):
+        ref[...] = jnp.zeros(ref.shape, ref.dtype)
+    bias_tiles(facts, tiles, heads, 3 * TILE)
+    mix_back(1)
+    token_back(1)
+    for moved in moves_1:
+        moved.wait_recv()
+    block_turn = home(far_block_out, block_home)
+    state_turn = home(far_state_out, state_home)
+    state_back(1)
+    gather_cot(1)
+    state_sum_1 = state_sum(1)
+    token_sum_1 = token_sum(1)
+    state_sum_1.forward()
+    mix_back(0)
+    up_sum.forward()
+    bring_gates.wait()
+    state_norm_grad, gain_2 = rms_back(s1_ref[...], gains_ref[2:3, :], state_sum_1.finish())
+    direct_0, moves_0 = gates_back(0, s0_ref[...], direct_1 + state_norm_grad)
+    token_sum_1.forward()
+    down_sum.forward()
+    weight_grad(wout_grad, branch_grad, mixed[...], slice(0, width))
+    wout_sum = PlaneSum(links, here, wout_grad, wout_first, wout_last).start()
+    for k in range(1, 4):
+        gate_gather_1.ready(k)
+    gate_gather_0 = RowGather(links, here, gate_rows, 0, rows).start()
+    bring_snormed = pltpu.make_async_copy(far_snormed, branch_grad, local_sems.at[2])
+    for ref in (skey_grad, svalue_grad):
+        ref[...] = jnp.zeros(ref.shape, ref.dtype)
+    token_back(0)
+    past_send[0] = key_grad[0:window, :].astype(jnp.bfloat16)
+    past_send[1] = value_grad[0:window, :].astype(jnp.bfloat16)
+    up_sum.finish()
+    up_settle = Settle(links, here, up_sum, up_home)
+    gain_1, turn_1 = finish_tokens(1, token_sum_1)
+    for k in range(1, 4):
+        gate_gather_0.ready(k)
+    for c in range(3):
+        weight_grad(
+            gates_grad,
+            gate_rows.at[:, c * size : (c + 1) * size],
+            smixed[...],
+            slice(c * width, (c + 1) * width),
+        )
+    gates_sum = PlaneSum(links, here, gates_grad, gates_first, gates_last).start()
+    down_sum.finish()
+    down_settle = Settle(links, here, down_sum, down_home)
+    wout_sum.forward()
+    for moved in moves_0:
+        moved.wait_recv()
+    for gather in branch_gathers:
+        gather.sent()
+    bring_snormed.start()
+    state_back(0)
+    gather_cot(0)
+    state_sum_1.sent()
+    state_sum_0 = state_sum(0)
+    token_sum_0 = token_sum(0)
+    past_turn = home(past_send, past_home)
+    bring_snormed.wait()
+    weight_grad(wst_grad, branch_grad, state_cot[...], slice(0, 3 * width))
+    wst_sum = PlaneSum(links, here, wst_grad, wst_first, wst_last).start()
+    for gather in (gate_gather_1, gate_gather_0):
+        gather.sent()
+    normed = gate_rows.at[:, 0:size]
+    bring_normed = pltpu.make_async_copy(far_normed, normed, local_sems.at[2])
+    bring_normed.start()
+    state_sum_0.forward()
+    gates_sum.forward()
+    bring_normed.wait()
+    weight_grad(wtok_grad, normed, token_cot[...], slice(0, 3 * width))
+    wtok_sum = PlaneSum(links, here, wtok_grad, wtok_first, wtok_last).start()
+    token_sum_0.forward()
+    state_norm_grad, gain = rms_back(s0_ref[...], gains_ref[2:3, :], state_sum_0.finish())
+    carried_send[...] = (direct_0 + state_norm_grad).astype(jnp.bfloat16)
+    carried_turn = home(carried_send, carried_in)
+    gain_2 = gain_2 + gain
+    wout_sum.finish()
+    wout_settle = Settle(links, here, wout_sum, wout_home)
+    gain_0, turn_0 = finish_tokens(0, token_sum_0)
+
+    for head in range(heads):
+        lines = tile_grads[head, 0:8, :]
+        span = lines.shape[1]
+        for group in range(1, TILE // 8):
+            lines = lines + pltpu.roll(tile_grads[head, 8 * group : 8 * group + 8, :], span - 8 * group, 1)
+        total = lines[0:1]
+        for line in range(1, 8):
+            total = total + pltpu.roll(lines[line : line + 1], span - line, 1)
+        for owner in range(4):
+            at = 8 + heads * owner + head
+            ring_send[at : at + 1, :] = jnp.where(rank == owner, total, 0.0)
+    ring_send[0:1, :] = gain_0 + gain_1
+    ring_send[1:2, :] = small_sums[0:1, :]
+    ring_send[2:3, :] = gain_2
+    ring_send[3:6, :] = small_sums[1:4, :]
+    counted = jnp.zeros((1, 1), jnp.float32)
+    for block in range(2):
+        valid_rows = row_mask(facts, block * window + rank * rows, rows)
+        counted = counted + jnp.sum(valid_rows, axis=0, keepdims=True)
+    ring_send[6:7, :] = jnp.broadcast_to(counted, (1, size))
+    ring_send[7:8, :] = jnp.zeros((1, size), jnp.float32)
+    ring_moves = [
+        links.copy(ring_send, ring_in.at[step - 1], ring[step - 1]) for step in range(1, 8)
+    ]
+    wst_sum.forward()
+    wtok_sum.forward()
+    carried_turn.arrived()
+    is_fresh = facts_home[3:4, :] > 0.5
+    came = carried_in[...]
+    carried_grad[...] = jnp.where(is_fresh, 0.0, came.astype(jnp.float32))
+    initial_send[...] = jnp.where(is_fresh, came, jnp.zeros_like(came))
+    part = initial_grad.shape[1]
+    initial_moves = []
+    for step in range(1, 8):
+        to = lax.rem(here.dp + step, 8)
+        columns = pl.ds(pl.multiple_of(to * part, part), part)
+        initial_moves.append(
+            links.copy(initial_send.at[:, columns], initial_in.at[step - 1], ring[step - 1])
+        )
+    for moved in ring_moves:
+        moved.wait_recv()
+    total = ring_send[...]
+    for step in range(7):
+        total = total + ring_in[step]
+    level_send[...] = total
+    level_moves = [
+        links.copy(level_send, level_in.at[step - 1], (here.dp, lax.rem(here.level + step, 4)))
+        for step in range(1, 4)
+    ]
+    gates_sum.finish()
+    slot = here.half * 4 + rank
+    piece = rows // 4
+    gate_moves = []
+    for step in range(4):
+        to_level = lax.rem(here.level + step, 4)
+        for to_core, chip in ((here.core, here.dp), (1 - here.core, other)):
+            start = here.planes[0] * 2 * rows + to_core * rows + to_level * piece
+            source = gates_grad.at[rows_at(start, piece, piece)]
+            if step == 0 and chip is here.dp:
+                kept = pltpu.make_async_copy(source, gates_home.at[slot], local_sems.at[3])
+                kept.start()
+            else:
+                gate_moves.append(links.copy(source, gates_home.at[slot], (chip, to_level)))
+    wst_sum.finish()
+    wst_settle = Settle(links, here, wst_sum, wst_home)
+    wtok_sum.finish()
+    wtok_settle = Settle(links, here, wtok_sum, wtok_home)
+    for moved in initial_moves:
+        moved.wait_recv()
+    own_columns = pl.ds(pl.multiple_of(here.dp * part, part), part)
+    initial = initial_send[:, own_columns].astype(jnp.float32)
+    for step in range(7):
+        initial = initial + initial_in[step].astype(jnp.float32)
+    initial_grad[...] = initial
+    for moved in level_moves:
+        moved.wait_recv()
+    total = level_send[...]
+    for step in range(3):
+        total = total + level_in[step]
+    totals[...] = total
+    kept.wait()
+    for moved in gate_moves:
+        moved.wait_recv()
+    for turn in (block_turn, state_turn, past_turn, turn_1, turn_0):
+        turn.arrived()
+    for settle in (up_settle, down_settle, wout_settle, wst_settle, wtok_settle):
+        settle.arrived()
+    links.close()
+
+
+def run_kernel(body, outs, scratch, collective, name, operands, far_in=(), far_out=()):
+    vmem = pl.BlockSpec(memory_space=pltpu.VMEM)
+    far = pl.BlockSpec(memory_space=pl.ANY)
+    return pl.pallas_call(
+        body,
+        out_shape=outs,
+        in_specs=[far if at in far_in else vmem for at in range(len(operands))],
+        out_specs=[far if at in far_out else vmem for at in range(len(outs))],
+        scratch_shapes=scratch,
+        compiler_params=pltpu.CompilerParams(
+            collective_id=collective, has_side_effects=True, vmem_limit_bytes=VMEM_BYTES
+        ),
+        name=name,
+    )(*operands)
+
+
+def sems(count):
+    return [pltpu.SemaphoreType.DMA((count,)), pltpu.SemaphoreType.DMA((count,))]
+
+
+def grouped(
+    tokens, carried_state, past_keys, fresh_start, valid_count, bucket_ids, grad_output, grad_state,
+    norm_gains, token_qkv, token_out, bias_table, mlp_up, mlp_down, state_qkv, state_gates, initial_state,
+):
+    dp_size, levels = lax.axis_size("dp"), lax.axis_size("state")
+    dp_at, level = lax.axis_index("dp"), lax.axis_index("state")
+    _, blocks, rows, size = tokens.shape
+    window = rows * levels
+    width = token_qkv.shape[2]
+    heads = width // DH
+    units = mlp_up.shape[1]
+    model_rows = token_qkv.shape[0]
+    low, full = jnp.bfloat16, jnp.float32
+
+    one_hot = (bucket_ids[:, None] == jnp.arange(bias_table.shape[0])[None, :]).astype(full)
+    per_offset = jnp.dot(one_hot, bias_table, precision=HIGHEST)
+    lines = jnp.pad(per_offset[::-1].T, ((0, 0), (1, window - 1)), constant_values=NEGATIVE)
+    numbers = jnp.stack([valid_count[0], fresh_start[0]]).astype(full)
+    facts_in = jnp.concatenate(
+        [
+            lines,
+            jnp.broadcast_to(numbers[:, None], (2, lines.shape[1])),
+            jnp.zeros((4, lines.shape[1]), full),
+        ]
+    )
+
+    shape = jax.ShapeDtypeStruct
+    vmem = pltpu.VMEM
+    rs = row_sum_scratch(rows, size)
+    (
+        normed, snormed, queries, keys, values, sqkv, lse, mixed, smixed,
+        gate_values, s1, s2, wst_all, wtok_all, wout_all, gates_all, x, s0, facts, gstate,
+        block_out, middle_grad, wup_grad, wdn_grad, small_sums,
+    ) = run_kernel(
+        forward_kernel,
+        [
+            shape((2 * window, size), low),
+            shape((2 * window, size), low),
+            shape((2 * window, width), low),
+            shape((3 * window, width), low),
+            shape((3 * window, width), low),
+            shape((2 * window, 3 * width), low),
+            shape((2 * window, 2 * heads), full),
+            shape((2 * window, width), low),
+            shape((2 * window, width), low),
+            shape((2 * rows, 3 * size), full),
+            shape((rows, size), full),
+            shape((rows, size), low),
+            shape((size, 3 * width), low),
+            shape((size, 3 * width), low),
+            shape((size, width), low),
+            shape((size, 3 * size), low),
+            shape((2 * rows, size), low),
+            shape((rows, size), full),
+            shape((8, 2 * window), full),
+            shape((rows, size), full),
+            shape((2 * rows, size), low),
+            shape((2 * rows, size), full),
+            shape((size, units), low),
+            shape((size, units), low),
+            shape((8, size), full),
+        ],
+        [
+            vmem((heads, TILE, 3 * TILE), full),
+            vmem((rows, size), low),
+            vmem((rows, size), low),
+            vmem((rows, size), low),
+            vmem((rows, size), low),
+            vmem((rows, size), full),
+            vmem((rows, 3 * size), full),
+            vmem((size, units), low),
+            vmem((size, units), low),
+            vmem((2 * rows, size), full),
+            vmem((2 * window, size), low),
+            vmem((2 * rows, size), low),
+            vmem((2 * window, size), low),
+            vmem((2 * window, units), full),
+            vmem((2 * window, units), low),
+            vmem((2 * window, units), low),
+            vmem((size, units), low),
+        ]
+        + rs * 4
+        + sems(128)
+        + [pltpu.SemaphoreType.DMA((4,))],
+        0,
+        "forward",
+        [
+            tokens[0].reshape(blocks * rows, size),
+            carried_state[0],
+            initial_state,
+            jnp.swapaxes(past_keys[0], 0, 1),
+            facts_in,
+            grad_output[0].reshape(blocks * rows, size),
+            grad_state[0],
+            norm_gains,
+            state_qkv.reshape(model_rows, 3 * width),
+            token_qkv.reshape(model_rows, 3 * width),
+            token_out,
+            state_gates.reshape(model_rows, 3 * size),
+            mlp_up,
+            mlp_down,
+        ],
+        far_in=(3, 5, 6, 12, 13),
+        far_out=(9, 19, 22, 23),
+    )
+    grads = [("wst", 3 * width), ("wtok", 3 * width), ("wout", width), ("gates", 3 * width)]
+    (
+        block_home, state_home, tokens_home, past_home, carried_grad, initial_grad, totals,
+        up_home, down_home, wst_home, wtok_home, wout_home, gates_home, *_,
+    ) = run_kernel(
+        cotangent_kernel,
+        [
+            shape((2 * rows, size), low),
+            shape((rows, size), low),
+            shape((2 * rows, size), low),
+            shape((2, window, width), low),
+            shape((rows, size), full),
+            shape((rows, size // dp_size), full),
+            shape((16, size), full),
+            shape((2, rows, units), low),
+            shape((2, rows, units), low),
+            shape((2, rows, 3 * width), low),
+            shape((2, rows, 3 * width), low),
+            shape((2, rows, width), low),
+            shape((8, rows // 4, 3 * width), low),
+            shape((4, rows, units), low),
+            shape((4, rows, units), low),
+            shape((2, rows, units), low),
+            shape((2, rows, units), low),
+        ],
+        [
+            vmem((heads, TILE, 3 * TILE), full),
+            vmem((heads, TILE, 4 * TILE), full),
+            vmem((2 * window, size), low),
+            vmem((2 * window, width), low),
+            vmem((2 * window, 3 * size), low),
+            vmem((2 * window, width), low),
+            vmem((3 * window, width), full),
+            vmem((3 * window, width), full),
+            vmem((window, width), full),
+            vmem((window, width), full),
+            vmem((2 * window, 3 * width), low),
+            vmem((2 * window, 3 * width), low),
+            vmem((rows, 3 * size), full),
+            vmem((2, rows, size), low),
+            vmem((2 * rows, size), low),
+            vmem((rows, size), low),
+            vmem((rows, size), low),
+            vmem((2, window, width), low),
+            vmem((rows, size), low),
+            vmem((dp_size - 1, rows, size // dp_size), low),
+        ]
+        + [vmem((size, columns), low) for _, columns in grads]
+        + [vmem((4, rows, columns), low) for _, columns in grads]
+        + [vmem((2, rows, columns), low) for _, columns in grads]
+        + [vmem((2, rows, units), low)] * 2
+        + [
+            vmem((3, rows, units), low),
+            vmem((dp_size - 1, 16, size), full),
+            vmem((levels - 1, 16, size), full),
+            vmem((16, size), full),
+            vmem((16, size), full),
+        ]
+        + rs * 3
+        + sems(128)
+        + [pltpu.SemaphoreType.DMA((4,)), pltpu.SemaphoreType.DMA((3,))],
+        1,
+        "cotangent",
+        [
+            middle_grad, gstate, x, s0, s1, gate_values, norm_gains, facts, facts_in,
+            small_sums,
+            normed, snormed, queries, keys, values, sqkv, lse, mixed, smixed,
+            wst_all, wtok_all, wout_all, gates_all, wup_grad, wdn_grad, block_out, s2,
+        ],
+        far_in=(5, 10, 11, 23, 24, 25, 26),
+        far_out=(0, 1, 2, 3, 7, 8, 9, 10, 11, 12, 13, 14, 15, 16),
+    )
+    both = lambda pair: pair[0].astype(full) + pair[1].astype(full)
+    gates_out = gates_home.astype(full).reshape(2, levels, rows // 4, 3, width)
+    gates_out = jnp.transpose(both(gates_out), (1, 2, 0, 3)).reshape(rows // 4, 3, size)
+    line_sums = totals[8 : 8 + levels * heads, 1 : window + 1][:, ::-1]
+    table_all = jnp.dot(one_hot.T, line_sums.T, precision=HIGHEST)
+    table_rows = table_all.shape[0] // dp_size
+    table_out = lax.dynamic_slice(table_all, (dp_at * table_rows, level * heads), (table_rows, heads))
+    share = size // (dp_size * levels)
+    gains_out = lax.dynamic_slice(totals, (0, (dp_at * levels + level) * share), (3, share))
+    rms_stats = jnp.sqrt(jnp.sum(totals[3:6], axis=1) / totals[6, 0])
+    return (
+        block_home.reshape(1, blocks, rows, size),
+        state_home.astype(full)[None],
+        rms_stats,
+        tokens_home.reshape(1, blocks, rows, size),
+        carried_grad[None],
+        jnp.swapaxes(past_home.astype(full), 0, 1)[None],
+        gains_out,
+        both(wtok_home).reshape(model_rows, 3, width),
+        both(wout_home),
+        table_out,
+        both(up_home),
+        both(down_home),
+        both(wst_home).reshape(model_rows, 3, width),
+        gates_out,
+        initial_grad,
+    )
+
+
 def solution(mesh):
     in_specs = (
         P("dp", None, "state", None),
@@ -552,4 +1888,5 @@
         P(("dp", "state"), None, None),
         P("state", "dp"),
     )
-    return jax.shard_map(shards, mesh=mesh, in_specs=in_specs, out_specs=out_specs, check_vma=False)
+    body = grouped if dict(mesh.shape) == {"dp": 8, "state": 4} else shards
+    return jax.shard_map(body, mesh=mesh, in_specs=in_specs, out_specs=out_specs, check_vma=False)

time: 1370 us -> 392 us (0.29)
  waiting for transfers between devices: 889 us -> 0 us
  Pallas kernels: 0 us -> 361 us
  matrix products: 164 us -> 1.26 us
  local copies, waits for them, and re-layouts: 128 us -> 17.3 us
  blocking collectives: 72.7 us -> 0 us
  other arithmetic: 77.9 us -> 6.24 us
  between operations: 20.2 us -> 2.34 us
    all_gather x17 -> x0, waiting for transfers between devices: 419 us -> none  [the longest x4 92.4 us: whole_rows(): return lax.all_gather(partial_value, 'state', axis=1, tiled=True)]
    reduce_scatter x17 -> x0, waiting for transfers between devices: 407 us -> none  [the longest x4 99.5 us: sum_rows(): lax.psum_scatter(partial_value.astype(jnp.bfloat16), 'state', scatter_dim...]
    pallas_call x0 -> x2, Pallas kernels: none -> 361 us  [run_kernel(): pl.pallas_call(body, out_shape=outs, in_specs=[far if at in far_in else v...]
    dot_general x62 -> x2, matrix products: 164 us -> 1.26 us  [the longest x1 0.99 us: grouped(): per_offset = jnp.dot(one_hot, bias_table, precision=HIGHEST)]
    unnamed x40 -> x0, waiting for transfers between devices: 63.1 us -> none
    unnamed x358 -> x43, local copies, waits for them, and re-layouts: 65.5 us -> 10.1 us
    psum x1 -> x0, blocking collectives: 39.1 us -> none  [shards(): lax.psum((square_sums, valid_total), ('dp', 'state'))]
    convert_element_type x22 -> x2, other arithmetic: 30.2 us -> 0.13 us  [the longest x1 0.08 us: grouped(): numbers = jnp.stack([valid_count[0], fresh_start[0]]).astype(full)]
  transfers between devices with their start and end apart: 39 -> 0, of which waited for: 32 -> 0; matrix products, arithmetic and copies ran while one was open for 24% -> 0% of each run, Pallas kernels for 0% -> 0%
where the time goes in v3:
time: 392 us; the launch traced here: 388 us
  Pallas kernels  361 us (92%)
  local copies, waits for them, and re-layouts  17.3 us (4%)
  other arithmetic  6.24 us (2%)
    pallas_call x2, Pallas kernels, run_kernel(): pl.pallas_call(body, out_shape=outs, in_specs=[far if at in far_in else v...  361 us
    unnamed x43, local copies, waits for them, and re-layouts  10.1 us

profile of v3, /device:TPU:0, one launch (start us, length us, event | category | flops | bytes accessed | tf_op | source)
XLA Modules:
  0.0 387.9 jit_solution(13696451774761351528)
XLA Ops:
  0.7 0.7 copy-done
  1.3 1.0 fusion.1
  4.2 0.7 fusion.4.facts_in.facts_home
  4.9 1.5 copy.55
  6.5 1.2 copy.58.gates_in
  7.6 0.9 copy.66
  8.7 0.8 copy.56.wst_in
  9.7 0.8 copy.57.wtok_in
  10.5 186.5 %forward.1 = (bf16[1024,1024]{1,0:T(8,128)(2,1)}, bf16[1024,1024]{1,0:T(8,128)(2,1)}, bf16[1024,256]{1,0:T(8,128)(2,1)}, bf16[1536,256]{1,0:T(8,128)(2,1)}, bf16...) custom-call(bf16[256,1024]{1,0:T(8,128)(2,1)} %bitcast.44, ...), custom_call_target="tpu_custom_call" | custom-call | tf_op jit(solution)/shard_map/forward/pallas_call | solution.py:1631
  197.0 174.2 %cotangent.1 = (bf16[256,1024]{1,0:T(8,128)(2,1)}, bf16[128,1024]{1,0:T(8,128)(2,1)}, bf16[256,1024]{1,0:T(8,128)(2,1)}, bf16[2,512,256]{2,1,0:T(8,128)(2,1)}, f...) custom-call(f32[256,1024]{1,0:T(8,128)} %get-tuple-element.53.middle, ...), custom_call_target="tpu_custom_call" | custom-call | tf_op jit(solution)/shard_map/cotangent/pallas_call | solution.py:1631
  371.2 2.4 add_bitcast_fusion
  373.9 0.9 copy.63
  375.0 0.9 copy.64
  376.5 0.9 reshape.96
  377.6 1.8 copy.62
  380.0 1.2 divide_sqrt_fusion
  381.2 0.8 bitcast_convert_fusion
  382.0 0.7 add_bitcast_fusion.2
  383.4 0.7 dynamic_slice.7
  384.0 0.6 constant_dynamic-slice_fusion
  384.7 0.8 copy.73
  385.5 0.8 copy.74
  386.3 0.8 copy.75
  387.0 0.6 copy.76
  (51 shorter events, 3.3 us)
Async XLA Ops:
  0.6 0.7 copy-start
  0.7 7.0 %copy-start.2 = (bf16[1,512,2,256]{3,2,1,0:T(2,128)(2,1)S(1)}, bf16[1,512,2,256]{3,2,1,0:T(2,128)(2,1)}, u32[]{:S(2)}) copy-start(bf16[1,512,2,256]{3,2,1,0:T(2,128)(2,1)} %param.19) | copy-start | bytes 1572868
  4.9 3.6 copy-start.10
  6.5 3.0 copy-start.11
  371.2 2.4 copy-start.7
  371.2 2.4 copy-start.8
  373.7 2.3 copy-start.6
  376.0 1.5 copy-start.1
  376.5 2.9 copy-start.14
  376.5 4.7 %copy-start.9 = (bf16[128,1024]{1,0:T(8,128)(2,1)S(1)}, bf16[128,1024]{1,0:T(8,128)(2,1)}, u32[]{:S(2)}) copy-start(bf16[128,1024]{1,0:T(8,128)(2,1)} %get-tuple-element.79) | copy-start | bytes 786436
  377.5 4.5 %copy-start.12 = (bf16[2,128,256]{2,1,0:T(8,128)(2,1)S(1)}, bf16[2,128,256]{2,1,0:T(8,128)(2,1)}, u32[]{:S(2)}) copy-start(bf16[2,128,256]{2,1,0:T(8,128)(2,1)} %get-tuple-element.85) | copy-start | bytes 393220
  377.5 5.6 %copy-start.15 = (s32[512]{0:T(512)S(1)}, s32[512]{0:T(512)}, u32[]{:S(2)}) copy-start(s32[512]{0:T(512)} %param.22) | copy-start | bytes 6148
  377.5 7.2 %copy-start.5 = (bf16[256,1024]{1,0:T(8,128)(2,1)S(1)}, bf16[256,1024]{1,0:T(8,128)(2,1)}, u32[]{:S(2)}) copy-start(bf16[256,1024]{1,0:T(8,128)(2,1)} %get-tuple-element.78) | copy-start | bytes 1572868
  377.6 7.9 %copy-start.4 = (bf16[256,1024]{1,0:T(8,128)(2,1)S(1)}, bf16[256,1024]{1,0:T(8,128)(2,1)}, u32[]{:S(2)}) copy-start(bf16[256,1024]{1,0:T(8,128)(2,1)} %get-tuple-element.81) | copy-start | bytes 1572868
  379.4 6.9 %copy-start.3 = (f32[128,1024]{1,0:T(8,128)S(1)}, f32[128,1024]{1,0:T(8,128)}, u32[]{:S(2)}) copy-start(f32[128,1024]{1,0:T(8,128)} %get-tuple-element.82) | copy-start | bytes 1572868
  381.2 5.8 %copy-start.13 = (f32[128,128]{1,0:T(8,128)S(1)}, f32[128,128]{1,0:T(8,128)}, u32[]{:S(2)}) copy-start(f32[128,128]{1,0:T(8,128)} %get-tuple-element.169) | copy-start | bytes 196612

commit v4 on v3

--- a/solution.py
+++ b/solution.py
@@ -848,15 +848,25 @@
 def forward_kernel(
     x_in, carried_in, initial_in, far_past, facts_in, far_gout, far_gstate, gains_ref,
     wst_in, wtok_in, wout_in, gates_in, far_wup, far_wdn,
-    normed, snormed, queries, keys, values, state_qkv, lse_ref, mixed, smixed,
-    far_gate_values, s1_ref, s2_ref, wst, wtok, wout, gates, x_ref, s0_ref, facts, far_gstate_here,
-    block_out, middle_grad, far_wup_grad, far_wdn_grad, small_sums,
-    tiles, a2a_0, a2a_1, initial_all, normed_send, s0_send, gate_values, wup, wdn, middle,
+    far_normed, far_snormed, far_queries, far_keys, far_values, far_state_qkv, far_lse, far_mixed,
+    far_wst, far_wtok, far_wout, far_gates, far_x, far_s0, far_s1,
+    far_gate_values, far_gstate_here, far_wup_grad, far_wdn_grad,
+    smixed_rows, s2_ref, facts, block_out, middle_grad, small_sums,
+    normed, snormed, queries, keys, values, state_qkv, lse_ref, mixed,
+    wst, wtok, wout, gates, x_ref, s0_ref, s1_ref,
+    smixed, tiles, initial_all, normed_send, s0_send, gate_values, wup, wdn, middle,
     middle_normed, gout_rows, gout, slope, hidden, up_grad, grad_stage, *rest,
 ):
     rs = [rest[4 * k : 4 * k + 4] for k in range(4)]
     links = Links(rest[16], rest[17])
-    local_sems = rest[18]
+    local_sems, keep_sems = rest[18], rest[19]
+    kept = []
+
+    def keep(source, target):
+        moved = pltpu.make_async_copy(source, target, keep_sems.at[len(kept)])
+        moved.start()
+        kept.append(moved)
+
     here = Place()
     rank, ranks, mates = here.rank, here.ranks, here.mates
     rows = s0_ref.shape[0]
@@ -882,29 +892,29 @@
     s0_send[...] = start
     normed_send[...] = (start * scale_of(start) * gains_ref[2:3, :]).astype(jnp.bfloat16)
     normed_turn = turn(normed_send, snormed.at[rows_at(here.level * rows, rows)])
-    x_turn = turn(x_in, x_ref)
-    gather_wtok = WeightGather(links, here, wtok_in, wtok).enter()
     facts_turn.arrived()
     bias_tiles(facts, tiles, heads, 3 * TILE)
+    gather_wst.spread()
+    gather_wtok = WeightGather(links, here, wtok_in, wtok).enter()
     normed_turn.arrived()
     gather_s0 = RowGather(links, here, snormed, 0, rows).start()
-    gather_wst.spread()
-    past_turns = [
-        turn(far_past.at[0], keys.at[pl.ds(0, window)]),
-        turn(far_past.at[1], values.at[pl.ds(0, window)]),
-    ]
-    gather_wout = WeightGather(links, here, wout_in, wout).enter()
-    x_turn.arrived()
-    gather_x = []
-    for block in range(2):
+
+    def enter_x(block):
+        at = pl.ds(block * rows, rows)
+        return turn(x_in.at[at], x_ref.at[at])
+
+    def norm_x(block, moved):
+        moved.arrived()
         x = x_ref[block * rows : (block + 1) * rows, :].astype(jnp.float32)
         normed[rows_at(block * window + rank * rows, rows), :] = (
             x * scale_of(x) * gains_ref[0:1, :]
         ).astype(jnp.bfloat16)
-        gather_x.append(RowGather(links, here, normed, block * window, rows).start())
+        return RowGather(links, here, normed, block * window, rows).start()
+
+    x_turn_0 = enter_x(0)
     gather_wst.forward()
     gather_wtok.spread()
-    s0_turn = turn(s0_send, s0_ref)
+    x_turn_1 = enter_x(1)
 
     def key_mask(start, size):
         place_of = lax.broadcasted_iota(jnp.int32, (1, size), 1).astype(jnp.float32)
@@ -981,14 +991,14 @@
             part = dot(source, gates[:, c * size : (c + 1) * size], NT)
             gate_values[:, c * size : (c + 1) * size] = part
             parts.append(part)
-        keep = pltpu.make_async_copy(
+        stored = pltpu.make_async_copy(
             gate_values, far_gate_values.at[pl.ds(block * rows, rows)], local_sems.at[0]
         )
-        keep.start()
+        stored.start()
         new_state = state_now * jax.nn.sigmoid(parts[2] + 1.0) + jnp.tanh(parts[0]) * jax.nn.sigmoid(
             parts[1] - 1.0
         )
-        return new_state, keep
+        return new_state, stored
 
     def branch_rows(block):
         def make(which):
@@ -1048,39 +1058,59 @@
         for part in range(stage.shape[0] // step):
             at = slice(part * step, (part + 1) * step)
             stage[at, :] = dot(left[:, at], right[...], TN).astype(jnp.bfloat16)
-        keep = pltpu.make_async_copy(stage, target, sem)
-        keep.start()
-        return keep
+        stored = pltpu.make_async_copy(stage, target, sem)
+        stored.start()
+        return stored
 
     gather_wst.finish()
+    keep(wst, far_wst)
     project_state(0, gather_s0)
+    gather_x0 = norm_x(0, x_turn_0)
     gather_wtok.forward()
     gather_gates = GateGather(links, here, gates_in, gates, local_sems.at[3])
     gather_gates.spread()
+    gather_wout = WeightGather(links, here, wout_in, wout).enter()
+    past_turns = [
+        turn(far_past.at[0], keys.at[pl.ds(0, window)]),
+        turn(far_past.at[1], values.at[pl.ds(0, window)]),
+    ]
+    gather_x1 = norm_x(1, x_turn_1)
+    gather_wtok.finish()
+    keep(wtok, far_wtok)
+    keep(x_ref, far_x)
+    project_token(0, gather_x0)
+    state_attention(0)
+    a2a_0 = smixed_rows.at[pl.ds(0, rows)]
+    a2a_1 = smixed_rows.at[pl.ds(rows, rows)]
+    moves_0 = spread_state(0, a2a_0)
+    s0_turn = turn(s0_send, s0_ref)
+    gather_wout.spread()
     gather_wup = WeightGather(links, here, far_wup, wup).enter()
-    gather_wtok.finish()
-    project_token(0, gather_x[0])
-    project_token(1, gather_x[1])
+    project_token(1, gather_x1)
+    keep(normed, far_normed)
+    keep(queries, far_queries)
+    gather_gates.forward()
     for moved in past_turns:
         moved.arrived()
-    state_attention(0)
-    moves_0 = spread_state(0, a2a_0)
-    gather_wout.spread()
-    gather_gates.forward()
-    gout_turn = turn(far_gout, gout_rows)
+    keep(keys, far_keys)
+    keep(values, far_values)
     token_attention(0)
     gather_wout.forward()
     gather_gates.last()
     gather_wdn = WeightGather(links, here, far_wdn, wdn).enter()
     gather_wup.spread()
     gather_wout.finish()
+    keep(wout, far_wout)
     sums[0].fill(branch_rows(0))
     for moved in moves_0:
         moved.wait_recv()
     gather_gates.finish()
+    keep(gates, far_gates)
     s0_turn.arrived()
+    keep(s0_ref, far_s0)
     s1, keep_gates = renew(0, a2a_0, s0_ref[...])
     s1_ref[...] = s1
+    keep(s1_ref, far_s1)
     snormed[rows_at(window + rank * rows, rows), :] = (s1 * scale_of(s1) * gains_ref[2:3, :]).astype(
         jnp.bfloat16
     )
@@ -1088,12 +1118,16 @@
     sums[0].forward()
     gather_wup.forward()
     gather_wdn.spread()
-    gstate_turn = turn(far_gstate, far_gstate_here)
     project_state(1, gather_s1)
+    gout_turn = turn(far_gout, gout_rows)
+    keep(snormed, far_snormed)
+    keep(state_qkv, far_state_qkv)
     state_attention(1)
     moves_1 = spread_state(1, a2a_1)
     branch_total, gather_m0 = finish_branch(0)
     token_attention(1)
+    keep(lse_ref, far_lse)
+    keep(mixed, far_mixed)
     gather_wdn.forward()
     sums[1].fill(branch_rows(1))
     gather_wup.finish()
@@ -1105,6 +1139,7 @@
         moved.wait_recv()
     keep_gates.wait()
     s2, keep_gates = renew(1, a2a_1, s1_ref[...])
+    gstate_turn = turn(far_gstate, far_gstate_here)
     s2_ref[...] = s2.astype(jnp.bfloat16)
     gather_wdn.finish()
     sums[0].sent()
@@ -1146,6 +1181,8 @@
     keep_gates.wait()
     keep_down.wait()
     keep_up.wait()
+    for moved in kept:
+        moved.wait()
     links.close()
 
 
@@ -1202,38 +1239,45 @@
         self.forwards = forwards
         self.brought, self.brought_sems = brought, brought_sems
 
-    def total(self, *pieces):
-        brings = [
-            pltpu.make_async_copy(piece, self.brought.at[slot], self.brought_sems.at[slot])
-            for slot, piece in enumerate(pieces)
-        ]
-        for bring in brings:
-            bring.start()
+    def totals(self, *groups):
+        brings, at, outs = [], 0, []
+        for pieces in groups:
+            for piece in pieces:
+                brings.append(pltpu.make_async_copy(piece, self.brought.at[at], self.brought_sems.at[at]))
+                brings[-1].start()
+                at += 1
         for bring in brings:
             bring.wait()
-        out = self.brought[0].astype(jnp.float32)
-        for slot in range(1, len(pieces)):
-            out = out + self.brought[slot].astype(jnp.float32)
-        return out.astype(jnp.bfloat16)
+        at = 0
+        for slot, pieces in enumerate(groups):
+            out = self.brought[at].astype(jnp.float32)
+            for step in range(1, len(pieces)):
+                out = out + self.brought[at + step].astype(jnp.float32)
+            at += len(pieces)
+            self.forwards[slot] = out.astype(jnp.bfloat16)
 
     def forward(self):
         mates = self.here.plane_mates
         self.firsts[1].wait_recv()
-        self.forwards[0] = self.total(self.part(2, 0), self.first_in.at[1])
+        self.firsts[3].wait_recv()
+        self.totals(
+            (self.part(2, 0), self.first_in.at[1]),
+            (self.part(1, 1), self.first_in.at[3]),
+        )
         self.last_0 = self.links.copy(self.forwards.at[0], self.last_in.at[0], mates[2])
-        self.firsts[3].wait_recv()
-        self.forwards[1] = self.total(self.part(1, 1), self.first_in.at[3])
         self.last_1 = self.links.copy(self.forwards.at[1], self.last_in.at[1], mates[1])
 
     def finish(self):
         self.firsts[0].wait_recv()
+        self.firsts[2].wait_recv()
         self.last_0.wait_recv()
+        self.last_1.wait_recv()
         self.links.sent(self.last_0)
-        self.forwards[0] = self.total(self.part(0, 0), self.first_in.at[0], self.last_in.at[0])
-        self.firsts[2].wait_recv()
-        self.last_1.wait_recv()
         self.links.sent(self.last_1)
-        self.forwards[1] = self.total(self.part(0, 1), self.first_in.at[2], self.last_in.at[1])
+        self.totals(
+            (self.part(0, 0), self.first_in.at[0], self.last_in.at[0]),
+            (self.part(0, 1), self.first_in.at[2], self.last_in.at[1]),
+        )
 
     def result(self, which):
         return self.forwards.at[which]
@@ -1253,13 +1297,13 @@
 def cotangent_kernel(
     middle_grad, gstate_ref, x_ref, s0_ref, s1_ref, far_gate_values, gains_ref, facts, facts_home,
     small_sums,
-    far_normed, far_snormed, queries, keys, values, state_qkv, lse_ref, mixed, smixed,
+    far_normed, far_snormed, queries, keys, values, state_qkv, lse_ref, mixed, smixed_rows,
     wst, wtok, wout, gates, far_wup_grad, far_wdn_grad, far_block_out, far_state_out,
     block_home, state_home, tokens_home, past_home, carried_grad, initial_grad, totals,
     up_home, down_home, wst_home, wtok_home, wout_home, gates_home,
     up_first, down_first, up_last, down_last,
     tiles, tile_grads, branch_grad, mixed_grad, gate_rows, state_mixed_grad, key_grad, value_grad,
-    skey_grad, svalue_grad, token_cot, state_cot, gate_values, sending,
+    skey_grad, svalue_grad, token_cot, state_cot, gate_values, smixed_pair, sending,
     tokens_send, carried_send, carried_in, past_send, initial_send, initial_in,
     wst_grad, wtok_grad, wout_grad, gates_grad,
     wst_first, wtok_first, wout_first, gates_first, wst_last, wtok_last, wout_last, gates_last,
@@ -1286,7 +1330,6 @@
         far_gate_values.at[pl.ds(rows, rows)], gate_values, local_sems.at[0]
     )
     bring_gates.start()
-    branch_gathers = []
     for block in (1, 0):
         at = slice(block * rows, (block + 1) * rows)
         branch_grad[rows_at(block * window + rank * rows, rows), :] = middle_grad[at, :].astype(
@@ -1296,8 +1339,11 @@
     def home(source, target):
         return Turn(links, here, source, target, here.from_there)
 
+    def pair_rows(block):
+        return rows_at((2 * block + here.core) * rows, rows)
+
     def gates_back(block, state, state_grad):
-        spot = rows_at(block * window + rank * rows, rows)
+        spot = pair_rows(block)
         keep = jax.nn.sigmoid(gate_values[:, 2 * size : 3 * size] + 1.0)
         fresh = jnp.tanh(gate_values[:, 0:size])
         let_in = jax.nn.sigmoid(gate_values[:, size : 2 * size] - 1.0)
@@ -1312,6 +1358,7 @@
         out = out + dot(gate_rows[spot, size : 2 * size], gates[:, size : 2 * size], NN)
         out = out + dot(gate_rows[spot, 2 * size : 3 * size], gates[:, 2 * size : 3 * size], NN)
         sending[block] = out.astype(jnp.bfloat16)
+        spot = rows_at(block * window + rank * rows, rows)
         moves = []
         for k in (2, 3, 1):
             columns = pl.ds(pl.multiple_of(ranks[k] * width, width), width)
@@ -1320,7 +1367,8 @@
             )
         columns = pl.ds(pl.multiple_of(rank * width, width), width)
         state_mixed_grad[spot, :] = sending[block, :, columns]
-        return state_grad * keep, moves
+        pair = gate_rows.at[pair_rows(block)]
+        return state_grad * keep, moves, links.copy(pair, pair, mates[1])
 
     def key_mask(start, size):
         place_of = lax.broadcasted_iota(jnp.int32, (1, size), 1).astype(jnp.float32)
@@ -1371,7 +1419,7 @@
                 token_cot[here_rows, lanes] = (part * ROOT).astype(jnp.bfloat16)
                 key_grad[near, lanes] += dot(first_grad, query, TN) * ROOT
                 skey_grad[:, lanes] += dot(second_grad, query, TN) * ROOT
-                tile_grads[head, :, 0 : 3 * TILE] += first_grad.astype(jnp.float32)
+                tile_grads[head] += first_grad.astype(jnp.float32)
 
     def state_back(block):
         base = block * window
@@ -1423,13 +1471,14 @@
             lambda which: dot(token_cot[rows_at(block * window + which * rows, rows), :], wtok[...], NT)
         )
 
-    def mix_back(block):
+    def mix_back(block, gather):
         for k in range(4):
-            branch_gathers[1 - block].ready(k)
+            gather.ready(k)
             at = rows_at(block * window + ranks[k] * rows, rows)
             mixed_grad[at, :] = dot(branch_grad[at, :], wout[...], NN).astype(jnp.bfloat16)
 
     def weight_grad(target, left, right, lanes):
+        right = right[...]
         step = 256
         for part in range(size // step):
             at = slice(part * step, (part + 1) * step)
@@ -1441,98 +1490,121 @@
         tokens_send[at, :] = (middle_grad[at, :] + straight).astype(jnp.bfloat16)
         return gain, home(tokens_send.at[pl.ds(block * rows, rows)], tokens_home.at[pl.ds(block * rows, rows)])
 
+    reach = 2 * width
+    other_half = pl.ds(pl.multiple_of((1 - here.core) * reach, reach), reach)
+    own_half = pl.ds(pl.multiple_of(here.core * reach, reach), reach)
+    smixed_moves = []
+    for block in range(2):
+        own_rows = pl.ds(block * rows, rows)
+        smixed_pair[pair_rows(block), :] = smixed_rows[own_rows, own_half]
+        smixed_moves.append(
+            links.copy(
+                smixed_rows.at[own_rows, other_half], smixed_pair.at[pair_rows(block)], mates[1]
+            )
+        )
+    branch_1 = RowGather(links, here, branch_grad, window, rows).start()
     bring_gates.wait()
-    direct_1, moves_1 = gates_back(1, s1_ref[...], gstate_ref[...])
-    for block in (1, 0):
-        branch_gathers.append(RowGather(links, here, branch_grad, block * window, rows).start())
+    direct_1, moves_1, pair_1 = gates_back(1, s1_ref[...], gstate_ref[...].astype(jnp.float32))
     up_sum = FarPlaneSum(
         links, here, far_wup_grad, up_first, up_last, up_forwards, brought, brought_sems
     ).start()
     down_sum = FarPlaneSum(
         links, here, far_wdn_grad, down_first, down_last, down_forwards, brought, brought_sems
     ).start()
-    gate_gather_1 = RowGather(links, here, gate_rows, window, rows).start()
     bring_gates = pltpu.make_async_copy(far_gate_values.at[pl.ds(0, rows)], gate_values, local_sems.at[0])
     bring_gates.start()
     for ref in (tile_grads, key_grad, value_grad, skey_grad, svalue_grad):
         ref[...] = jnp.zeros(ref.shape, ref.dtype)
     bias_tiles(facts, tiles, heads, 3 * TILE)
-    mix_back(1)
+    mix_back(1, branch_1)
+    branch_0 = RowGather(links, here, branch_grad, 0, rows).start()
+    block_turn = home(far_block_out, block_home)
+    state_turn = home(far_state_out, state_home)
     token_back(1)
     for moved in moves_1:
         moved.wait_recv()
-    block_turn = home(far_block_out, block_home)
-    state_turn = home(far_state_out, state_home)
     state_back(1)
     gather_cot(1)
     state_sum_1 = state_sum(1)
     token_sum_1 = token_sum(1)
     state_sum_1.forward()
-    mix_back(0)
+    mix_back(0, branch_0)
+    for ref in (skey_grad, svalue_grad):
+        ref[...] = jnp.zeros(ref.shape, ref.dtype)
     up_sum.forward()
+    down_sum.forward()
+    token_back(0)
+    token_sum_1.forward()
     bring_gates.wait()
     state_norm_grad, gain_2 = rms_back(s1_ref[...], gains_ref[2:3, :], state_sum_1.finish())
-    direct_0, moves_0 = gates_back(0, s0_ref[...], direct_1 + state_norm_grad)
-    token_sum_1.forward()
-    down_sum.forward()
-    weight_grad(wout_grad, branch_grad, mixed[...], slice(0, width))
-    wout_sum = PlaneSum(links, here, wout_grad, wout_first, wout_last).start()
-    for k in range(1, 4):
-        gate_gather_1.ready(k)
-    gate_gather_0 = RowGather(links, here, gate_rows, 0, rows).start()
-    bring_snormed = pltpu.make_async_copy(far_snormed, branch_grad, local_sems.at[2])
-    for ref in (skey_grad, svalue_grad):
-        ref[...] = jnp.zeros(ref.shape, ref.dtype)
-    token_back(0)
+    direct_0, moves_0, pair_0 = gates_back(0, s0_ref[...], direct_1 + state_norm_grad)
     past_send[0] = key_grad[0:window, :].astype(jnp.bfloat16)
     past_send[1] = value_grad[0:window, :].astype(jnp.bfloat16)
-    up_sum.finish()
-    up_settle = Settle(links, here, up_sum, up_home)
-    gain_1, turn_1 = finish_tokens(1, token_sum_1)
-    for k in range(1, 4):
-        gate_gather_0.ready(k)
+    for moved in smixed_moves + [pair_1, pair_0]:
+        moved.wait_recv()
     for c in range(3):
         weight_grad(
             gates_grad,
             gate_rows.at[:, c * size : (c + 1) * size],
-            smixed[...],
-            slice(c * width, (c + 1) * width),
+            smixed_pair,
+            slice(c * reach, (c + 1) * reach),
         )
     gates_sum = PlaneSum(links, here, gates_grad, gates_first, gates_last).start()
+    weight_grad(wout_grad, branch_grad, mixed, slice(0, width))
+    wout_sum = PlaneSum(links, here, wout_grad, wout_first, wout_last).start()
+    up_sum.finish()
+    up_settle = Settle(links, here, up_sum, up_home)
+    for moved in moves_0:
+        moved.wait_recv()
+    past_turn = home(past_send, past_home)
     down_sum.finish()
     down_settle = Settle(links, here, down_sum, down_home)
-    wout_sum.forward()
-    for moved in moves_0:
-        moved.wait_recv()
-    for gather in branch_gathers:
+    for gather in (branch_1, branch_0):
         gather.sent()
+    bring_snormed = pltpu.make_async_copy(far_snormed, branch_grad, local_sems.at[2])
     bring_snormed.start()
+    for moved in (pair_1, pair_0):
+        links.sent(moved)
+    bring_normed = []
+    for block in range(2):
+        bring_normed.append(
+            pltpu.make_async_copy(
+                far_normed.at[pl.ds(block * window, window)],
+                gate_rows.at[:, block * size : (block + 1) * size],
+                local_sems.at[4 + block],
+            )
+        )
+        bring_normed[block].start()
     state_back(0)
     gather_cot(0)
+    bring_snormed.wait()
+    weight_grad(wst_grad, branch_grad, state_cot, slice(0, 3 * width))
+    wst_sum = PlaneSum(links, here, wst_grad, wst_first, wst_last).start()
+    for block in range(2):
+        bring_normed[block].wait()
+    for part in range(size // 256):
+        at = slice(part * 256, (part + 1) * 256)
+        later = slice(size + part * 256, size + (part + 1) * 256)
+        summed = dot(gate_rows[:, at], token_cot[0:window, :], TN)
+        summed = summed + dot(gate_rows[:, later], token_cot[window : 2 * window, :], TN)
+        wtok_grad[at, :] = summed.astype(jnp.bfloat16)
+    wtok_sum = PlaneSum(links, here, wtok_grad, wtok_first, wtok_last).start()
     state_sum_1.sent()
     state_sum_0 = state_sum(0)
     token_sum_0 = token_sum(0)
-    past_turn = home(past_send, past_home)
-    bring_snormed.wait()
-    weight_grad(wst_grad, branch_grad, state_cot[...], slice(0, 3 * width))
-    wst_sum = PlaneSum(links, here, wst_grad, wst_first, wst_last).start()
-    for gather in (gate_gather_1, gate_gather_0):
-        gather.sent()
-    normed = gate_rows.at[:, 0:size]
-    bring_normed = pltpu.make_async_copy(far_normed, normed, local_sems.at[2])
-    bring_normed.start()
+    gain_1, turn_1 = finish_tokens(1, token_sum_1)
     state_sum_0.forward()
+    token_sum_0.forward()
+    wst_sum.forward()
     gates_sum.forward()
-    bring_normed.wait()
-    weight_grad(wtok_grad, normed, token_cot[...], slice(0, 3 * width))
-    wtok_sum = PlaneSum(links, here, wtok_grad, wtok_first, wtok_last).start()
-    token_sum_0.forward()
+    wtok_sum.forward()
+    wout_sum.forward()
     state_norm_grad, gain = rms_back(s0_ref[...], gains_ref[2:3, :], state_sum_0.finish())
     carried_send[...] = (direct_0 + state_norm_grad).astype(jnp.bfloat16)
     carried_turn = home(carried_send, carried_in)
     gain_2 = gain_2 + gain
-    wout_sum.finish()
-    wout_settle = Settle(links, here, wout_sum, wout_home)
+    wst_sum.finish()
+    wst_settle = Settle(links, here, wst_sum, wst_home)
     gain_0, turn_0 = finish_tokens(0, token_sum_0)
 
     for head in range(heads):
@@ -1545,7 +1617,8 @@
             total = total + pltpu.roll(lines[line : line + 1], span - line, 1)
         for owner in range(4):
             at = 8 + heads * owner + head
-            ring_send[at : at + 1, :] = jnp.where(rank == owner, total, 0.0)
+            ring_send[at : at + 1, :] = jnp.zeros((1, size), jnp.float32)
+            ring_send[at : at + 1, 0:span] = jnp.where(rank == owner, total, 0.0)
     ring_send[0:1, :] = gain_0 + gain_1
     ring_send[1:2, :] = small_sums[0:1, :]
     ring_send[2:3, :] = gain_2
@@ -1559,8 +1632,24 @@
     ring_moves = [
         links.copy(ring_send, ring_in.at[step - 1], ring[step - 1]) for step in range(1, 8)
     ]
-    wst_sum.forward()
-    wtok_sum.forward()
+    wtok_sum.finish()
+    wtok_settle = Settle(links, here, wtok_sum, wtok_home)
+    gates_sum.finish()
+    slot = here.level * 2 + here.core
+    piece = rows // 4
+    gate_moves = []
+    for step in range(4):
+        to_level = lax.rem(here.level + step, 4)
+        for to_core, chip in ((here.core, here.dp), (1 - here.core, other)):
+            start = here.planes[0] * 2 * rows + to_core * rows + to_level * piece
+            source = gates_grad.at[rows_at(start, piece, piece)]
+            if step == 0 and chip is here.dp:
+                kept = pltpu.make_async_copy(source, gates_home.at[slot], local_sems.at[3])
+                kept.start()
+            else:
+                gate_moves.append(links.copy(source, gates_home.at[slot], (chip, to_level)))
+    wout_sum.finish()
+    wout_settle = Settle(links, here, wout_sum, wout_home)
     carried_turn.arrived()
     is_fresh = facts_home[3:4, :] > 0.5
     came = carried_in[...]
@@ -1584,24 +1673,6 @@
         links.copy(level_send, level_in.at[step - 1], (here.dp, lax.rem(here.level + step, 4)))
         for step in range(1, 4)
     ]
-    gates_sum.finish()
-    slot = here.half * 4 + rank
-    piece = rows // 4
-    gate_moves = []
-    for step in range(4):
-        to_level = lax.rem(here.level + step, 4)
-        for to_core, chip in ((here.core, here.dp), (1 - here.core, other)):
-            start = here.planes[0] * 2 * rows + to_core * rows + to_level * piece
-            source = gates_grad.at[rows_at(start, piece, piece)]
-            if step == 0 and chip is here.dp:
-                kept = pltpu.make_async_copy(source, gates_home.at[slot], local_sems.at[3])
-                kept.start()
-            else:
-                gate_moves.append(links.copy(source, gates_home.at[slot], (chip, to_level)))
-    wst_sum.finish()
-    wst_settle = Settle(links, here, wst_sum, wst_home)
-    wtok_sum.finish()
-    wtok_settle = Settle(links, here, wtok_sum, wtok_home)
     for moved in initial_moves:
         moved.wait_recv()
     own_columns = pl.ds(pl.multiple_of(here.dp * part, part), part)
@@ -1674,43 +1745,46 @@
     shape = jax.ShapeDtypeStruct
     vmem = pltpu.VMEM
     rs = row_sum_scratch(rows, size)
+    kept = [
+        ((2 * window, size), low),
+        ((2 * window, size), low),
+        ((2 * window, width), low),
+        ((3 * window, width), low),
+        ((3 * window, width), low),
+        ((2 * window, 3 * width), low),
+        ((2 * window, 2 * heads), full),
+        ((2 * window, width), low),
+        ((size, 3 * width), low),
+        ((size, 3 * width), low),
+        ((size, width), low),
+        ((size, 3 * size), low),
+        ((2 * rows, size), low),
+        ((rows, size), full),
+        ((rows, size), full),
+    ]
     (
-        normed, snormed, queries, keys, values, sqkv, lse, mixed, smixed,
-        gate_values, s1, s2, wst_all, wtok_all, wout_all, gates_all, x, s0, facts, gstate,
-        block_out, middle_grad, wup_grad, wdn_grad, small_sums,
+        normed, snormed, queries, keys, values, sqkv, lse, mixed, wst_all, wtok_all, wout_all, gates_all,
+        x, s0, s1, gate_values, gstate, wup_grad, wdn_grad, smixed_rows, s2, facts,
+        block_out, middle_grad, small_sums,
     ) = run_kernel(
         forward_kernel,
-        [
-            shape((2 * window, size), low),
-            shape((2 * window, size), low),
-            shape((2 * window, width), low),
-            shape((3 * window, width), low),
-            shape((3 * window, width), low),
-            shape((2 * window, 3 * width), low),
-            shape((2 * window, 2 * heads), full),
-            shape((2 * window, width), low),
-            shape((2 * window, width), low),
+        [shape(*of) for of in kept]
+        + [
             shape((2 * rows, 3 * size), full),
-            shape((rows, size), full),
             shape((rows, size), low),
-            shape((size, 3 * width), low),
-            shape((size, 3 * width), low),
-            shape((size, width), low),
-            shape((size, 3 * size), low),
+            shape((size, units), low),
+            shape((size, units), low),
             shape((2 * rows, size), low),
-            shape((rows, size), full),
+            shape((rows, size), low),
             shape((8, 2 * window), full),
-            shape((rows, size), full),
             shape((2 * rows, size), low),
             shape((2 * rows, size), full),
-            shape((size, units), low),
-            shape((size, units), low),
             shape((8, size), full),
         ],
-        [
+        [vmem(*of) for of in kept]
+        + [
+            vmem((2 * window, width), low),
             vmem((heads, TILE, 3 * TILE), full),
-            vmem((rows, size), low),
-            vmem((rows, size), low),
             vmem((rows, size), low),
             vmem((rows, size), low),
             vmem((rows, size), full),
@@ -1728,7 +1802,7 @@
         ]
         + rs * 4
         + sems(128)
-        + [pltpu.SemaphoreType.DMA((4,))],
+        + [pltpu.SemaphoreType.DMA((4,)), pltpu.SemaphoreType.DMA((len(kept),))],
         0,
         "forward",
         [
@@ -1738,7 +1812,7 @@
             jnp.swapaxes(past_keys[0], 0, 1),
             facts_in,
             grad_output[0].reshape(blocks * rows, size),
-            grad_state[0],
+            grad_state[0].astype(low),
             norm_gains,
             state_qkv.reshape(model_rows, 3 * width),
             token_qkv.reshape(model_rows, 3 * width),
@@ -1748,9 +1822,9 @@
             mlp_down,
         ],
         far_in=(3, 5, 6, 12, 13),
-        far_out=(9, 19, 22, 23),
-    )
-    grads = [("wst", 3 * width), ("wtok", 3 * width), ("wout", width), ("gates", 3 * width)]
+        far_out=range(len(kept) + 4),
+    )
+    grads = [("wst", 3 * width), ("wtok", 3 * width), ("wout", width), ("gates", 6 * width)]
     (
         block_home, state_home, tokens_home, past_home, carried_grad, initial_grad, totals,
         up_home, down_home, wst_home, wtok_home, wout_home, gates_home, *_,
@@ -1769,7 +1843,7 @@
             shape((2, rows, 3 * width), low),
             shape((2, rows, 3 * width), low),
             shape((2, rows, width), low),
-            shape((8, rows // 4, 3 * width), low),
+            shape((8, rows // 4, 6 * width), low),
             shape((4, rows, units), low),
             shape((4, rows, units), low),
             shape((2, rows, units), low),
@@ -1777,10 +1851,10 @@
         ],
         [
             vmem((heads, TILE, 3 * TILE), full),
-            vmem((heads, TILE, 4 * TILE), full),
+            vmem((heads, TILE, 3 * TILE), full),
             vmem((2 * window, size), low),
             vmem((2 * window, width), low),
-            vmem((2 * window, 3 * size), low),
+            vmem((4 * rows, 3 * size), low),
             vmem((2 * window, width), low),
             vmem((3 * window, width), full),
             vmem((3 * window, width), full),
@@ -1789,6 +1863,7 @@
             vmem((2 * window, 3 * width), low),
             vmem((2 * window, 3 * width), low),
             vmem((rows, 3 * size), full),
+            vmem((4 * rows, 2 * width), low),
             vmem((2, rows, size), low),
             vmem((2 * rows, size), low),
             vmem((rows, size), low),
@@ -1802,7 +1877,7 @@
         + [vmem((2, rows, columns), low) for _, columns in grads]
         + [vmem((2, rows, units), low)] * 2
         + [
-            vmem((3, rows, units), low),
+            vmem((6, rows, units), low),
             vmem((dp_size - 1, 16, size), full),
             vmem((levels - 1, 16, size), full),
             vmem((16, size), full),
@@ -1810,21 +1885,21 @@
         ]
         + rs * 3
         + sems(128)
-        + [pltpu.SemaphoreType.DMA((4,)), pltpu.SemaphoreType.DMA((3,))],
+        + [pltpu.SemaphoreType.DMA((6,)), pltpu.SemaphoreType.DMA((6,))],
         1,
         "cotangent",
         [
             middle_grad, gstate, x, s0, s1, gate_values, norm_gains, facts, facts_in,
             small_sums,
-            normed, snormed, queries, keys, values, sqkv, lse, mixed, smixed,
+            normed, snormed, queries, keys, values, sqkv, lse, mixed, smixed_rows,
             wst_all, wtok_all, wout_all, gates_all, wup_grad, wdn_grad, block_out, s2,
         ],
         far_in=(5, 10, 11, 23, 24, 25, 26),
         far_out=(0, 1, 2, 3, 7, 8, 9, 10, 11, 12, 13, 14, 15, 16),
     )
     both = lambda pair: pair[0].astype(full) + pair[1].astype(full)
-    gates_out = gates_home.astype(full).reshape(2, levels, rows // 4, 3, width)
-    gates_out = jnp.transpose(both(gates_out), (1, 2, 0, 3)).reshape(rows // 4, 3, size)
+    gates_out = jnp.sum(gates_home.astype(full).reshape(levels, 2, rows // 4, 3, 2 * width), axis=0)
+    gates_out = jnp.transpose(gates_out, (1, 2, 0, 3)).reshape(rows // 4, 3, size)
     line_sums = totals[8 : 8 + levels * heads, 1 : window + 1][:, ::-1]
     table_all = jnp.dot(one_hot.T, line_sums.T, precision=HIGHEST)
     table_rows = table_all.shape[0] // dp_size

time: 392 us -> 354 us (0.903)
  Pallas kernels: 361 us -> 318 us
    pallas_call x2, Pallas kernels: 361 us -> 318 us  [run_kernel(): pl.pallas_call(body, out_shape=outs, in_specs=[far if at in far_in else v...]
    unnamed x43 -> x45, local copies, waits for them, and re-layouts: 10.1 us -> 10.1 us
where the time goes in v4:
time: 354 us; the launch traced here: 348 us
  Pallas kernels  318 us (90%)
  local copies, waits for them, and re-layouts  18.7 us (5%)
  other arithmetic  7.51 us (2%)
    pallas_call x2, Pallas kernels, run_kernel(): pl.pallas_call(body, out_shape=outs, in_specs=[far if at in far_in else v...  318 us
    unnamed x45, local copies, waits for them, and re-layouts  10.1 us

profile of v4, /device:TPU:0, one launch (start us, length us, event | category | flops | bytes accessed | tf_op | source)
XLA Modules:
  0.0 348.2 jit_solution(4318410832097213886)
XLA Ops:
  0.7 0.7 copy-done
  1.3 1.0 fusion.1
  4.2 0.7 fusion.4.facts_in.facts_home
  4.9 1.5 copy.66
  6.5 1.2 copy.69.gates_in
  7.7 0.9 copy.77
  8.7 0.8 copy.67.wst_in
  9.7 0.8 copy.68.wtok_in
  10.5 0.7 convert_bitcast_fusion.1.far_gstate
  11.3 172.0 %forward.1 = (bf16[1024,1024]{1,0:T(8,128)(2,1)}, bf16[1024,1024]{1,0:T(8,128)(2,1)}, bf16[1024,256]{1,0:T(8,128)(2,1)}, bf16[1536,256]{1,0:T(8,128)(2,1)}, bf16...) custom-call(bf16[256,1024]{1,0:T(8,128)(2,1)} %bitcast.48, ...), custom_call_target="tpu_custom_call" | custom-call | tf_op jit(solution)/shard_map/forward/pallas_call | solution.py:1702
  183.3 146.4 %cotangent.1 = (bf16[256,1024]{1,0:T(8,128)(2,1)}, bf16[128,1024]{1,0:T(8,128)(2,1)}, bf16[256,1024]{1,0:T(8,128)(2,1)}, bf16[2,512,256]{2,1,0:T(8,128)(2,1)}, f...) custom-call(f32[256,1024]{1,0:T(8,128)} %get-tuple-element.53.middle, ...), custom_call_target="tpu_custom_call" | custom-call | tf_op jit(solution)/shard_map/cotangent/pallas_call | solution.py:1702
  329.8 2.4 add_bitcast_fusion
  332.4 0.9 copy.74
  333.5 0.9 copy.75
  334.4 1.4 reshape.103
  336.8 1.1 reshape.99
  338.0 1.8 copy.73
  340.4 1.2 divide_sqrt_fusion
  341.6 0.8 bitcast_convert_fusion
  342.4 0.7 add_bitcast_fusion.2
  343.7 0.7 dynamic_slice.7
  345.0 0.8 copy.84
  345.8 0.8 copy.85
  346.6 0.8 copy.86
  (53 shorter events, 4.9 us)
Async XLA Ops:
  0.6 0.7 copy-start
  0.7 7.0 %copy-start.4 = (bf16[1,512,2,256]{3,2,1,0:T(2,128)(2,1)S(1)}, bf16[1,512,2,256]{3,2,1,0:T(2,128)(2,1)}, u32[]{:S(2)}) copy-start(bf16[1,512,2,256]{3,2,1,0:T(2,128)(2,1)} %param.19) | copy-start | bytes 1572868
  4.9 3.6 %copy-start.11 = (bf16[128,3,256]{2,0,1:T(8,128)(2,1)S(1)}, bf16[128,3,256]{2,0,1:T(8,128)(2,1)}, u32[]{:S(2)}) copy-start(bf16[128,3,256]{2,0,1:T(8,128)(2,1)} %param.31) | copy-start | bytes 589828
  6.5 3.1 copy-start.12
  6.5 4.1 %copy-start.3 = (f32[1,128,1024]{2,1,0:T(8,128)S(1)}, f32[1,128,1024]{2,1,0:T(8,128)}, u32[]{:S(2)}) copy-start(f32[1,128,1024]{2,1,0:T(8,128)} %param.24) | copy-start | bytes 1572868
  329.7 2.4 copy-start.8
  329.7 2.4 copy-start.9
  332.2 2.3 copy-start.1
  335.8 2.1 copy-start.2
  336.8 3.0 copy-start.15
  336.8 4.8 %copy-start.10 = (bf16[128,1024]{1,0:T(8,128)(2,1)S(1)}, bf16[128,1024]{1,0:T(8,128)(2,1)}, u32[]{:S(2)}) copy-start(bf16[128,1024]{1,0:T(8,128)(2,1)} %get-tuple-element.79) | copy-start | bytes 786436
  337.9 4.5 %copy-start.13 = (bf16[2,128,256]{2,1,0:T(8,128)(2,1)S(1)}, bf16[2,128,256]{2,1,0:T(8,128)(2,1)}, u32[]{:S(2)}) copy-start(bf16[2,128,256]{2,1,0:T(8,128)(2,1)} %get-tuple-element.85) | copy-start | bytes 393220
  337.9 5.6 %copy-start.16 = (s32[512]{0:T(512)S(1)}, s32[512]{0:T(512)}, u32[]{:S(2)}) copy-start(s32[512]{0:T(512)} %param.22) | copy-start | bytes 6148
  337.9 7.2 %copy-start.7 = (bf16[256,1024]{1,0:T(8,128)(2,1)S(1)}, bf16[256,1024]{1,0:T(8,128)(2,1)}, u32[]{:S(2)}) copy-start(bf16[256,1024]{1,0:T(8,128)(2,1)} %get-tuple-element.78) | copy-start | bytes 1572868
  338.0 7.9 %copy-start.6 = (bf16[256,1024]{1,0:T(8,128)(2,1)S(1)}, bf16[256,1024]{1,0:T(8,128)(2,1)}, u32[]{:S(2)}) copy-start(bf16[256,1024]{1,0:T(8,128)(2,1)} %get-tuple-element.81) | copy-start | bytes 1572868
  339.8 6.9 %copy-start.5 = (f32[128,1024]{1,0:T(8,128)S(1)}, f32[128,1024]{1,0:T(8,128)}, u32[]{:S(2)}) copy-start(f32[128,1024]{1,0:T(8,128)} %get-tuple-element.82) | copy-start | bytes 1572868
  341.6 5.8 %copy-start.14 = (f32[128,128]{1,0:T(8,128)S(1)}, f32[128,128]{1,0:T(8,128)}, u32[]{:S(2)}) copy-start(f32[128,128]{1,0:T(8,128)} %get-tuple-element.184) | copy-start | bytes 196612

commit v5 on v4

--- a/solution.py
+++ b/solution.py
@@ -521,7 +521,7 @@
 NN = (((1,), (0,)), ((), ()))
 NT = (((1,), (1,)), ((), ()))
 TN = (((0,), (0,)), ((), ()))
-VMEM_BYTES = 63 * 2**20
+VMEM_BYTES = 127 * 2**19
 
 
 class Place:
@@ -558,6 +558,11 @@
     return pl.ds(pl.multiple_of(start, step), size)
 
 
+def rows_of(ref, start, size, step=128):
+    at = rows_at(start, size, step)
+    return ref.at[:, at] if len(ref.shape) == 3 else ref.at[at]
+
+
 class Links:
     def __init__(self, send_sems, recv_sems):
         self.send_sems, self.recv_sems = send_sems, recv_sems
@@ -644,20 +649,20 @@
 class WeightGather:
     def __init__(self, links, here, local, full):
         self.links, self.here, self.local, self.full = links, here, local, full
-        self.rows = local.shape[0]
+        self.rows = local.shape[-2]
 
     def enter(self):
-        target = self.full.at[rows_at(self.here.dp * self.rows, self.rows)]
+        target = rows_of(self.full, self.here.dp * self.rows, self.rows)
         self.turn = Turn(self.links, self.here, self.local, target, self.here.there)
         self.cross = self.links.copy(self.local, target, self.here.across)
         return self
 
     def block(self, k):
-        return self.full.at[rows_at(self.here.planes[k] * 2 * self.rows, 2 * self.rows)]
+        return rows_of(self.full, self.here.planes[k] * 2 * self.rows, 2 * self.rows)
 
     def half(self, k, which):
         start = self.here.planes[k] * 2 * self.rows + which * self.rows
-        return self.full.at[rows_at(start, self.rows)]
+        return rows_of(self.full, start, self.rows)
 
     def spread(self):
         self.turn.arrived()
@@ -681,16 +686,16 @@
 class GateGather:
     def __init__(self, links, here, local, full, sem):
         self.links, self.here, self.local, self.full, self.sem = links, here, local, full, sem
-        self.rows = local.shape[0]
+        self.rows = local.shape[-2]
 
     def block(self, k):
         start = (2 * self.here.planes[k] + self.here.core) * self.rows
-        return self.full.at[rows_at(start, self.rows)]
+        return rows_of(self.full, start, self.rows)
 
     def part(self, k, which):
         size = self.rows // 2
         start = (2 * self.here.planes[k] + self.here.core) * self.rows + which * size
-        return self.full.at[rows_at(start, size, 64)]
+        return rows_of(self.full, start, size, 64)
 
     def spread(self):
         mates, sibling = self.here.plane_mates, self.here.mates[1]
@@ -820,9 +825,9 @@
     return jnp.where(place_of.astype(jnp.float32) < facts[2:3, 0:1], 1.0, 0.0)
 
 
-def bias_tiles(lines_ref, tiles_ref, heads, width):
+def bias_tiles(lines_ref, tiles_ref, heads, width, scale=1.0):
     for head in range(heads):
-        line = lines_ref[head : head + 1, :]
+        line = lines_ref[head : head + 1, :] * scale
         spread = jnp.broadcast_to(line, (tiles_ref.shape[1], line.shape[1]))
         tiles_ref[head] = pltpu.roll(spread, 0, 1, stride=1, stride_axis=0)[:, :width]
 
@@ -842,19 +847,20 @@
 
 
 TILE = 256
+LOG2E = math.log2(math.e)
 ROOT = 1.0 / math.sqrt(DH)
 
 
 def forward_kernel(
-    x_in, carried_in, initial_in, far_past, facts_in, far_gout, far_gstate, gains_ref,
+    x_in, carried_in, initial_in, far_past, facts_in, far_gout, gstate_in, gains_ref,
     wst_in, wtok_in, wout_in, gates_in, far_wup, far_wdn,
     far_normed, far_snormed, far_queries, far_keys, far_values, far_state_qkv, far_lse, far_mixed,
     far_wst, far_wtok, far_wout, far_gates, far_x, far_s0, far_s1,
     far_gate_values, far_gstate_here, far_wup_grad, far_wdn_grad,
-    smixed_rows, s2_ref, facts, block_out, middle_grad, small_sums,
+    smixed_rows, s2_ref, facts, block_out, middle_grad, branch_rows, small_sums,
     normed, snormed, queries, keys, values, state_qkv, lse_ref, mixed,
     wst, wtok, wout, gates, x_ref, s0_ref, s1_ref,
-    smixed, tiles, initial_all, normed_send, s0_send, gate_values, wup, wdn, middle,
+    smixed, tiles, initial_all, normed_send, gstate_send, s0_send, gate_values, wup, wdn, middle,
     middle_normed, gout_rows, gout, slope, hidden, up_grad, grad_stage, *rest,
 ):
     rs = [rest[4 * k : 4 * k + 4] for k in range(4)]
@@ -926,17 +932,19 @@
         for k in range(4):
             gather.ready(k)
             at = rows_at(block * window + ranks[k] * rows, rows)
-            state_qkv[at, :] = dot(snormed[at, :], wst[...], NN).astype(jnp.bfloat16)
+            for c in range(3):
+                state_qkv[at, c * width : (c + 1) * width] = dot(snormed[at, :], wst[c], NN).astype(
+                    jnp.bfloat16
+                )
 
     def project_token(block, gather):
         for k in range(4):
             gather.ready(k)
             at = rows_at(block * window + ranks[k] * rows, rows)
             later = rows_at((block + 1) * window + ranks[k] * rows, rows)
-            out = dot(normed[at, :], wtok[...], NN).astype(jnp.bfloat16)
-            queries[at, :] = out[:, :width]
-            keys[later, :] = out[:, width : 2 * width]
-            values[later, :] = out[:, 2 * width :]
+            queries[at, :] = dot(normed[at, :], wtok[0], NN).astype(jnp.bfloat16)
+            keys[later, :] = dot(normed[at, :], wtok[1], NN).astype(jnp.bfloat16)
+            values[later, :] = dot(normed[at, :], wtok[2], NN).astype(jnp.bfloat16)
 
     def state_attention(block):
         base = block * window
@@ -988,7 +996,7 @@
         source = buffer[...]
         parts = []
         for c in range(3):
-            part = dot(source, gates[:, c * size : (c + 1) * size], NT)
+            part = dot(source, gates[c], NT)
             gate_values[:, c * size : (c + 1) * size] = part
             parts.append(part)
         stored = pltpu.make_async_copy(
@@ -1000,7 +1008,7 @@
         )
         return new_state, stored
 
-    def branch_rows(block):
+    def out_rows(block):
         def make(which):
             return dot(mixed[rows_at(block * window + which * rows, rows), :], wout[...], NT)
 
@@ -1101,7 +1109,7 @@
     gather_wup.spread()
     gather_wout.finish()
     keep(wout, far_wout)
-    sums[0].fill(branch_rows(0))
+    sums[0].fill(out_rows(0))
     for moved in moves_0:
         moved.wait_recv()
     gather_gates.finish()
@@ -1122,36 +1130,37 @@
     gout_turn = turn(far_gout, gout_rows)
     keep(snormed, far_snormed)
     keep(state_qkv, far_state_qkv)
-    state_attention(1)
-    moves_1 = spread_state(1, a2a_1)
     branch_total, gather_m0 = finish_branch(0)
     token_attention(1)
+    keep(mixed, far_mixed)
+    sums[1].fill(out_rows(1))
+    gather_wdn.forward()
+    state_attention(1)
     keep(lse_ref, far_lse)
-    keep(mixed, far_mixed)
-    gather_wdn.forward()
-    sums[1].fill(branch_rows(1))
+    sums[1].forward()
+    moves_1 = spread_state(1, a2a_1)
     gather_wup.finish()
+    rise(0, gather_m0)
+    more, gather_m1 = finish_branch(1)
+    branch_total = branch_total + more
     gout_turn.arrived()
     gather_g0 = start_gout(0)
-    rise(0, gather_m0)
-    sums[1].forward()
+    gather_wdn.finish()
+    sums[0].sent()
+    feed_0 = feed_sum(0)
     for moved in moves_1:
         moved.wait_recv()
     keep_gates.wait()
     s2, keep_gates = renew(1, a2a_1, s1_ref[...])
-    gstate_turn = turn(far_gstate, far_gstate_here)
+    gstate_send[...] = gstate_in[...].astype(jnp.bfloat16)
+    gstate_turn = turn(gstate_send, far_gstate_here)
     s2_ref[...] = s2.astype(jnp.bfloat16)
-    gather_wdn.finish()
-    sums[0].sent()
-    feed_0 = feed_sum(0)
-    more, gather_m1 = finish_branch(1)
-    branch_total = branch_total + more
+    rise(1, gather_m1)
     gather_g1 = start_gout(1)
+    sums[1].sent()
+    feed_1 = feed_sum(1)
     feed_0.forward()
     back_0 = feed_back(0, gather_g0)
-    rise(1, gather_m1)
-    sums[1].sent()
-    feed_1 = feed_sum(1)
     back_0.forward()
     back_1 = feed_back(1, gather_g1)
     feed_1.forward()
@@ -1170,7 +1179,9 @@
     for block, back_here in ((1, back_1), (0, back_0)):
         at = slice(block * rows, (block + 1) * rows)
         straight, gain = rms_back(middle[at, :], gains_ref[1:2, :], back_here.finish())
-        middle_grad[at, :] = gout_rows[at, :].astype(jnp.float32) + straight
+        total = gout_rows[at, :].astype(jnp.float32) + straight
+        middle_grad[at, :] = total
+        branch_rows[at, :] = total.astype(jnp.bfloat16)
         gain_total = gain_total + gain
     small_sums[...] = jnp.concatenate(
         [gain_total, result_total, branch_total, feed_total]
@@ -1190,11 +1201,11 @@
     def __init__(self, links, here, grad, first_in, last_in):
         self.links, self.here, self.grad = links, here, grad
         self.first_in, self.last_in = first_in, last_in
-        self.rows = first_in.shape[1]
+        self.rows = first_in.shape[-2]
 
     def part(self, k, which):
         start = self.here.planes[k] * 2 * self.rows + which * self.rows
-        return self.grad.at[rows_at(start, self.rows)]
+        return rows_of(self.grad, start, self.rows)
 
     def start(self):
         mates = self.here.plane_mates
@@ -1228,59 +1239,61 @@
         self.add(0, 1, self.last_in.at[1])
 
     def result(self, which):
-        return self.grad.at[
-            rows_at(self.here.planes[0] * 2 * self.rows + which * self.rows, self.rows)
+        return rows_of(self.grad, self.here.planes[0] * 2 * self.rows + which * self.rows, self.rows)
+
+
+class FarPlaneSum(PlaneSum):
+    def __init__(self, links, here, grad, first_in, last_in, held, held_sems):
+        super().__init__(links, here, grad, first_in, last_in)
+        self.held, self.held_sems = held, held_sems
+
+    def bring(self, *pieces):
+        self.brings = [
+            pltpu.make_async_copy(self.part(k, which), self.held.at[slot], self.held_sems.at[slot])
+            for slot, (k, which) in enumerate(pieces)
         ]
-
-
-class FarPlaneSum(PlaneSum):
-    def __init__(self, links, here, grad, first_in, last_in, forwards, brought, brought_sems):
-        super().__init__(links, here, grad, first_in, last_in)
-        self.forwards = forwards
-        self.brought, self.brought_sems = brought, brought_sems
-
-    def totals(self, *groups):
-        brings, at, outs = [], 0, []
-        for pieces in groups:
-            for piece in pieces:
-                brings.append(pltpu.make_async_copy(piece, self.brought.at[at], self.brought_sems.at[at]))
-                brings[-1].start()
-                at += 1
-        for bring in brings:
-            bring.wait()
-        at = 0
-        for slot, pieces in enumerate(groups):
-            out = self.brought[at].astype(jnp.float32)
-            for step in range(1, len(pieces)):
-                out = out + self.brought[at + step].astype(jnp.float32)
-            at += len(pieces)
-            self.forwards[slot] = out.astype(jnp.bfloat16)
+        for moved in self.brings:
+            moved.start()
+
+    def start(self):
+        super().start()
+        self.bring((2, 0), (1, 1))
+        return self
+
+    def add_to(self, slot, *arrived):
+        total = self.held[slot].astype(jnp.float32)
+        for piece in arrived:
+            total = total + piece.astype(jnp.float32)
+        self.held[slot] = total.astype(jnp.bfloat16)
 
     def forward(self):
         mates = self.here.plane_mates
+        for moved in self.brings:
+            moved.wait()
         self.firsts[1].wait_recv()
+        self.add_to(0, self.first_in[1])
+        self.last_0 = self.links.copy(self.held.at[0], self.last_in.at[0], mates[2])
         self.firsts[3].wait_recv()
-        self.totals(
-            (self.part(2, 0), self.first_in.at[1]),
-            (self.part(1, 1), self.first_in.at[3]),
-        )
-        self.last_0 = self.links.copy(self.forwards.at[0], self.last_in.at[0], mates[2])
-        self.last_1 = self.links.copy(self.forwards.at[1], self.last_in.at[1], mates[1])
-
-    def finish(self):
-        self.firsts[0].wait_recv()
-        self.firsts[2].wait_recv()
-        self.last_0.wait_recv()
-        self.last_1.wait_recv()
+        self.add_to(1, self.first_in[3])
+        self.last_1 = self.links.copy(self.held.at[1], self.last_in.at[1], mates[1])
+
+    def bring_own(self):
         self.links.sent(self.last_0)
         self.links.sent(self.last_1)
-        self.totals(
-            (self.part(0, 0), self.first_in.at[0], self.last_in.at[0]),
-            (self.part(0, 1), self.first_in.at[2], self.last_in.at[1]),
-        )
+        self.bring((0, 0), (0, 1))
+
+    def finish(self):
+        for moved in self.brings:
+            moved.wait()
+        self.firsts[0].wait_recv()
+        self.last_0.wait_recv()
+        self.add_to(0, self.first_in[0], self.last_in[0])
+        self.firsts[2].wait_recv()
+        self.last_1.wait_recv()
+        self.add_to(1, self.first_in[2], self.last_in[1])
 
     def result(self, which):
-        return self.forwards.at[which]
+        return self.held.at[which]
 
 
 class Settle:
@@ -1295,24 +1308,25 @@
 
 
 def cotangent_kernel(
-    middle_grad, gstate_ref, x_ref, s0_ref, s1_ref, far_gate_values, gains_ref, facts, facts_home,
+    far_middle_grad, far_branch_rows, gstate_ref, far_x, s0_ref, s1_ref, far_gate_values, gains_ref, facts, facts_home,
     small_sums,
-    far_normed, far_snormed, queries, keys, values, state_qkv, lse_ref, mixed, smixed_rows,
-    wst, wtok, wout, gates, far_wup_grad, far_wdn_grad, far_block_out, far_state_out,
+    far_normed, far_snormed, far_queries, far_keys, far_values, far_state_qkv, far_lse, far_mixed,
+    far_smixed, far_wst, far_wtok, far_wout, far_gates, far_wup_grad, far_wdn_grad, far_block_out, far_state_out,
     block_home, state_home, tokens_home, past_home, carried_grad, initial_grad, totals,
     up_home, down_home, wst_home, wtok_home, wout_home, gates_home,
-    up_first, down_first, up_last, down_last,
+    gates, wout, queries, keys, state_qkv, values, lse_ref, mixed, wst, wtok,
     tiles, tile_grads, branch_grad, mixed_grad, gate_rows, state_mixed_grad, key_grad, value_grad,
     skey_grad, svalue_grad, token_cot, state_cot, gate_values, smixed_pair, sending,
-    tokens_send, carried_send, carried_in, past_send, initial_send, initial_in,
+    tokens_send, carried_send, carried_in, initial_send, initial_in,
     wst_grad, wtok_grad, wout_grad, gates_grad,
     wst_first, wtok_first, wout_first, gates_first, wst_last, wtok_last, wout_last, gates_last,
-    up_forwards, down_forwards, brought, ring_in, level_in, ring_send, level_send,
+    up_first, down_first, up_last, down_last, up_held, down_held, ring_in, level_in, ring_send, level_send,
+    late_in, late_level_in, late_send, late_level_send,
     *rest,
 ):
     rs = [rest[0:4], rest[4:8], rest[8:12]]
     links = Links(rest[12], rest[13])
-    local_sems, brought_sems = rest[14], rest[15]
+    local_sems, held_sems, bring_sems = rest[14], rest[15], rest[16]
     here = Place()
     rank, ranks, mates = here.rank, here.ranks, here.mates
     rows = s0_ref.shape[0]
@@ -1320,27 +1334,48 @@
     width = queries.shape[1]
     heads = width // DH
     size = s0_ref.shape[1]
+    reach = 2 * width
+    other_half = pl.ds(pl.multiple_of((1 - here.core) * reach, reach), reach)
+    own_half = pl.ds(pl.multiple_of(here.core * reach, reach), reach)
+
+    def pair_rows(block):
+        return rows_at((2 * block + here.core) * rows, rows)
+
+    def own_branch(block):
+        return branch_grad.at[rows_at(block * window + rank * rows, rows)]
+
+    brings = []
+    for source, target in (
+        (far_branch_rows.at[pl.ds(rows, rows)], own_branch(1)),
+        (far_branch_rows.at[pl.ds(0, rows)], own_branch(0)),
+        (far_gates, gates),
+        (far_wout, wout),
+        (far_queries, queries),
+        (far_keys, keys),
+        (far_state_qkv, state_qkv),
+        (far_values, values),
+        (far_lse, lse_ref),
+        (far_mixed, mixed),
+        (far_wst, wst),
+        (far_wtok, wtok),
+        (far_x, tokens_send),
+        (far_smixed.at[pl.ds(0, rows), own_half], smixed_pair.at[pair_rows(0)]),
+        (far_smixed.at[pl.ds(rows, rows), own_half], smixed_pair.at[pair_rows(1)]),
+    ):
+        brings.append(pltpu.make_async_copy(source, target, bring_sems.at[len(brings)]))
+        brings[-1].start()
     ring = [(lax.rem(here.dp + step, 8), here.level) for step in range(1, 8)]
     other = here.dp + 1 - 2 * here.core
     column = [
         (chip, lax.rem(here.level + step, 4)) for step in range(1, 4) for chip in (here.dp, other)
     ]
-    greet(ring + column)
     bring_gates = pltpu.make_async_copy(
         far_gate_values.at[pl.ds(rows, rows)], gate_values, local_sems.at[0]
     )
     bring_gates.start()
-    for block in (1, 0):
-        at = slice(block * rows, (block + 1) * rows)
-        branch_grad[rows_at(block * window + rank * rows, rows), :] = middle_grad[at, :].astype(
-            jnp.bfloat16
-        )
-
+    greet(ring + column)
     def home(source, target):
         return Turn(links, here, source, target, here.from_there)
-
-    def pair_rows(block):
-        return rows_at((2 * block + here.core) * rows, rows)
 
     def gates_back(block, state, state_grad):
         spot = pair_rows(block)
@@ -1354,39 +1389,44 @@
         gate_rows[spot, 2 * size : 3 * size] = (
             state_grad * state * keep * (1.0 - keep)
         ).astype(jnp.bfloat16)
-        out = dot(gate_rows[spot, 0:size], gates[:, 0:size], NN)
-        out = out + dot(gate_rows[spot, size : 2 * size], gates[:, size : 2 * size], NN)
-        out = out + dot(gate_rows[spot, 2 * size : 3 * size], gates[:, 2 * size : 3 * size], NN)
-        sending[block] = out.astype(jnp.bfloat16)
+        out = dot(gate_rows[spot, 0:size], gates[0], NN)
+        out = out + dot(gate_rows[spot, size : 2 * size], gates[1], NN)
+        out = out + dot(gate_rows[spot, 2 * size : 3 * size], gates[2], NN)
+        sending[...] = out.astype(jnp.bfloat16)
         spot = rows_at(block * window + rank * rows, rows)
         moves = []
         for k in (2, 3, 1):
             columns = pl.ds(pl.multiple_of(ranks[k] * width, width), width)
             moves.append(
-                links.copy(sending.at[block, :, columns], state_mixed_grad.at[spot], mates[k])
+                links.copy(sending.at[:, columns], state_mixed_grad.at[spot], mates[k])
             )
         columns = pl.ds(pl.multiple_of(rank * width, width), width)
-        state_mixed_grad[spot, :] = sending[block, :, columns]
+        state_mixed_grad[spot, :] = sending[:, columns]
         pair = gate_rows.at[pair_rows(block)]
         return state_grad * keep, moves, links.copy(pair, pair, mates[1])
 
+    lane = lax.broadcasted_iota(jnp.int32, (1, DH), 1)
+
+    def widen(columns, value):
+        high = value.astype(jnp.bfloat16).astype(jnp.float32)
+        middle = (value - high).astype(jnp.bfloat16).astype(jnp.float32)
+        more = jnp.where(lane == 1, high, jnp.where(lane == 2, middle, value - high - middle))
+        more = jnp.where(lane == 0, 1.0, jnp.where(lane < 4, more, 0.0))
+        return jnp.concatenate([columns, more.astype(jnp.bfloat16)], axis=1)
+
+    plain = jnp.where((lane > 0) & (lane < 4), 1.0, 0.0)
+
+    def beside(columns, mask=None):
+        more = jnp.broadcast_to(plain, (columns.shape[0], DH))
+        if mask is not None:
+            more = jnp.where(lane == 0, mask, more)
+        return jnp.concatenate([columns, more.astype(jnp.bfloat16)], axis=1)
+
     def key_mask(start, size):
-        place_of = lax.broadcasted_iota(jnp.int32, (1, size), 1).astype(jnp.float32)
+        place_of = lax.broadcasted_iota(jnp.int32, (size, 1), 0).astype(jnp.float32)
         place_of = place_of + float(start - window)
-        own = jnp.where(place_of < facts[2:3, 0:size], 0.0, NEGATIVE)
-        return jnp.where(place_of < 0.0, facts[3:4, 0:size] * NEGATIVE, own)
-
-    def pair_back(first, second, lse, first_grad, second_grad):
-        first, second = jnp.exp(first - lse), jnp.exp(second - lse)
-        inner = jnp.sum(first * first_grad, axis=-1, keepdims=True) + jnp.sum(
-            second * second_grad, axis=-1, keepdims=True
-        )
-        return (
-            first.astype(jnp.bfloat16),
-            second.astype(jnp.bfloat16),
-            (first * (first_grad - inner)).astype(jnp.bfloat16),
-            (second * (second_grad - inner)).astype(jnp.bfloat16),
-        )
+        own = jnp.where(place_of < facts[2:3, 0:1], 0.0, NEGATIVE)
+        return jnp.where(place_of < 0.0, facts[3:4, 0:1] * NEGATIVE, own)
 
     def token_back(block):
         base = block * window
@@ -1402,24 +1442,32 @@
                 near = pl.ds(base + tile * TILE, 3 * TILE)
                 query = queries[here_rows, lanes]
                 out_grad = mixed_grad[here_rows, lanes]
-                first = dot(query, keys[near, lanes], NT) * ROOT + tiles[head] + near_mask
-                second = dot(query, state_qkv[whole, skey_lanes], NT) * ROOT
-                first, second, first_grad, second_grad = pair_back(
-                    first,
-                    second,
-                    lse_ref[here_rows, head : head + 1],
-                    dot(out_grad, values[near, lanes], NT),
-                    dot(out_grad, state_qkv[whole, svalue_lanes], NT),
+                wide = widen(query, lse_ref[here_rows, head : head + 1] * (-1.0 / ROOT))
+                inner = jnp.sum(
+                    out_grad.astype(jnp.float32) * mixed[here_rows, lanes].astype(jnp.float32),
+                    axis=-1,
+                    keepdims=True,
                 )
-                value_grad[near, lanes] += dot(first, out_grad, TN)
-                svalue_grad[:, lanes] += dot(second, out_grad, TN)
+                wide_grad = widen(out_grad, -inner)
+                first = jnp.exp2(
+                    dot(wide, beside(keys[near, lanes], near_mask), NT) * (ROOT * LOG2E) + tiles[head]
+                )
+                second = jnp.exp2(
+                    dot(wide, beside(state_qkv[whole, skey_lanes]), NT) * (ROOT * LOG2E)
+                )
+                first_low, second_low = first.astype(jnp.bfloat16), second.astype(jnp.bfloat16)
+                first = first * dot(wide_grad, beside(values[near, lanes]), NT)
+                second = second * dot(wide_grad, beside(state_qkv[whole, svalue_lanes]), NT)
+                first_grad, second_grad = first.astype(jnp.bfloat16), second.astype(jnp.bfloat16)
+                value_grad[near, lanes] += dot(first_low, out_grad, TN)
+                svalue_grad[:, lanes] += dot(second_low, out_grad, TN)
                 part = dot(first_grad, keys[near, lanes], NN) + dot(
                     second_grad, state_qkv[whole, skey_lanes], NN
                 )
                 token_cot[here_rows, lanes] = (part * ROOT).astype(jnp.bfloat16)
                 key_grad[near, lanes] += dot(first_grad, query, TN) * ROOT
                 skey_grad[:, lanes] += dot(second_grad, query, TN) * ROOT
-                tile_grads[head] += first_grad.astype(jnp.float32)
+                tile_grads[head] += first
 
     def state_back(block):
         base = block * window
@@ -1431,21 +1479,25 @@
             lanes = slice(at, at + DH)
             skey_lanes = slice(width + at, width + at + DH)
             svalue_lanes = slice(2 * width + at, 2 * width + at + DH)
+            wide_skeys = beside(state_qkv[whole, skey_lanes])
+            wide_keys = beside(keys[own, lanes], own_mask)
             for tile in range(window // TILE):
                 here_rows = pl.ds(base + tile * TILE, TILE)
                 query = state_qkv[here_rows, lanes]
                 out_grad = state_mixed_grad[here_rows, lanes]
-                first = dot(query, state_qkv[whole, skey_lanes], NT) * ROOT
-                second = dot(query, keys[own, lanes], NT) * ROOT + own_mask
-                first, second, first_grad, second_grad = pair_back(
-                    first,
-                    second,
-                    lse_ref[here_rows, heads + head : heads + head + 1],
-                    dot(out_grad, state_qkv[whole, svalue_lanes], NT),
-                    dot(out_grad, values[own, lanes], NT),
+                wide = widen(query, lse_ref[here_rows, heads + head : heads + head + 1] * (-1.0 / ROOT))
+                first = jnp.exp2(dot(wide, wide_skeys, NT) * (ROOT * LOG2E))
+                second = jnp.exp2(dot(wide, wide_keys, NT) * (ROOT * LOG2E))
+                first_low, second_low = first.astype(jnp.bfloat16), second.astype(jnp.bfloat16)
+                first_grad = dot(out_grad, state_qkv[whole, svalue_lanes], NT)
+                second_grad = dot(out_grad, values[own, lanes], NT)
+                inner = jnp.sum(first * first_grad, axis=-1, keepdims=True) + jnp.sum(
+                    second * second_grad, axis=-1, keepdims=True
                 )
-                svalue_grad[:, lanes] += dot(first, out_grad, TN)
-                value_grad[own, lanes] += dot(second, out_grad, TN)
+                first_grad = (first * (first_grad - inner)).astype(jnp.bfloat16)
+                second_grad = (second * (second_grad - inner)).astype(jnp.bfloat16)
+                svalue_grad[:, lanes] += dot(first_low, out_grad, TN)
+                value_grad[own, lanes] += dot(second_low, out_grad, TN)
                 part = dot(first_grad, state_qkv[whole, skey_lanes], NN) + dot(
                     second_grad, keys[own, lanes], NN
                 )
@@ -1461,15 +1513,21 @@
         state_cot[whole, width : 2 * width] = skey_grad[...].astype(jnp.bfloat16)
         state_cot[whole, 2 * width : 3 * width] = svalue_grad[...].astype(jnp.bfloat16)
 
+    def back_rows(cots, weight, block):
+        def make(which):
+            at = rows_at(block * window + which * rows, rows)
+            out = dot(cots[at, 0:width], weight[0], NT)
+            for c in (1, 2):
+                out = out + dot(cots[at, c * width : (c + 1) * width], weight[c], NT)
+            return out
+
+        return make
+
     def state_sum(block):
-        return RowSum(links, here, *rs[0], rows).fill(
-            lambda which: dot(state_cot[rows_at(block * window + which * rows, rows), :], wst[...], NT)
-        )
+        return RowSum(links, here, *rs[0], rows).fill(back_rows(state_cot, wst, block))
 
     def token_sum(block):
-        return RowSum(links, here, *rs[1 + block], rows).fill(
-            lambda which: dot(token_cot[rows_at(block * window + which * rows, rows), :], wtok[...], NT)
-        )
+        return RowSum(links, here, *rs[1 + block], rows).fill(back_rows(token_cot, wtok, block))
 
     def mix_back(block, gather):
         for k in range(4):
@@ -1477,45 +1535,55 @@
             at = rows_at(block * window + ranks[k] * rows, rows)
             mixed_grad[at, :] = dot(branch_grad[at, :], wout[...], NN).astype(jnp.bfloat16)
 
-    def weight_grad(target, left, right, lanes):
-        right = right[...]
+    def store_grad(target, at, out):
+        if len(target.shape) == 2:
+            target[at, :] = out.astype(jnp.bfloat16)
+        else:
+            for c in range(3):
+                target[c, at, :] = out[:, c * width : (c + 1) * width].astype(jnp.bfloat16)
+
+    def weight_grad(target, left, right):
         step = 256
         for part in range(size // step):
             at = slice(part * step, (part + 1) * step)
-            target[at, lanes] = dot(left[:, at], right, TN).astype(jnp.bfloat16)
+            store_grad(target, at, dot(left[:, at], right[...], TN))
 
     def finish_tokens(block, summed):
         at = slice(block * rows, (block + 1) * rows)
-        straight, gain = rms_back(x_ref[at, :].astype(jnp.float32), gains_ref[0:1, :], summed.finish())
-        tokens_send[at, :] = (middle_grad[at, :] + straight).astype(jnp.bfloat16)
+        x = tokens_send[at, :].astype(jnp.float32)
+        straight, gain = rms_back(x, gains_ref[0:1, :], summed.finish())
+        middle_grad = gate_values[:, block * size : (block + 1) * size]
+        tokens_send[at, :] = (middle_grad + straight).astype(jnp.bfloat16)
         return gain, home(tokens_send.at[pl.ds(block * rows, rows)], tokens_home.at[pl.ds(block * rows, rows)])
 
-    reach = 2 * width
-    other_half = pl.ds(pl.multiple_of((1 - here.core) * reach, reach), reach)
-    own_half = pl.ds(pl.multiple_of(here.core * reach, reach), reach)
     smixed_moves = []
     for block in range(2):
-        own_rows = pl.ds(block * rows, rows)
-        smixed_pair[pair_rows(block), :] = smixed_rows[own_rows, own_half]
         smixed_moves.append(
             links.copy(
-                smixed_rows.at[own_rows, other_half], smixed_pair.at[pair_rows(block)], mates[1]
+                far_smixed.at[pl.ds(block * rows, rows), other_half],
+                smixed_pair.at[pair_rows(block)],
+                mates[1],
             )
         )
+    brings[0].wait()
     branch_1 = RowGather(links, here, branch_grad, window, rows).start()
     bring_gates.wait()
+    brings[2].wait()
     direct_1, moves_1, pair_1 = gates_back(1, s1_ref[...], gstate_ref[...].astype(jnp.float32))
     up_sum = FarPlaneSum(
-        links, here, far_wup_grad, up_first, up_last, up_forwards, brought, brought_sems
+        links, here, far_wup_grad, up_first, up_last, up_held, held_sems.at[pl.ds(0, 2)]
     ).start()
     down_sum = FarPlaneSum(
-        links, here, far_wdn_grad, down_first, down_last, down_forwards, brought, brought_sems
+        links, here, far_wdn_grad, down_first, down_last, down_held, held_sems.at[pl.ds(2, 2)]
     ).start()
     bring_gates = pltpu.make_async_copy(far_gate_values.at[pl.ds(0, rows)], gate_values, local_sems.at[0])
     bring_gates.start()
     for ref in (tile_grads, key_grad, value_grad, skey_grad, svalue_grad):
         ref[...] = jnp.zeros(ref.shape, ref.dtype)
-    bias_tiles(facts, tiles, heads, 3 * TILE)
+    bias_tiles(facts, tiles, heads, 3 * TILE, LOG2E)
+    brings[1].wait()
+    for moved in brings[3:]:
+        moved.wait()
     mix_back(1, branch_1)
     branch_0 = RowGather(links, here, branch_grad, 0, rows).start()
     block_turn = home(far_block_out, block_home)
@@ -1525,39 +1593,85 @@
         moved.wait_recv()
     state_back(1)
     gather_cot(1)
+    up_sum.forward()
     state_sum_1 = state_sum(1)
     token_sum_1 = token_sum(1)
     state_sum_1.forward()
+    down_sum.forward()
+    up_sum.bring_own()
     mix_back(0, branch_0)
     for ref in (skey_grad, svalue_grad):
         ref[...] = jnp.zeros(ref.shape, ref.dtype)
-    up_sum.forward()
-    down_sum.forward()
+    up_sum.finish()
+    up_settle = Settle(links, here, up_sum, up_home)
     token_back(0)
+    for head in range(heads):
+        lines = tile_grads[head, 0:8, :]
+        span = lines.shape[1]
+        for group in range(1, TILE // 8):
+            lines = lines + pltpu.roll(tile_grads[head, 8 * group : 8 * group + 8, :], span - 8 * group, 1)
+        total = lines[0:1]
+        for line in range(1, 8):
+            total = total + pltpu.roll(lines[line : line + 1], span - line, 1)
+        for owner in range(4):
+            at = 8 + heads * owner + head
+            ring_send[at : at + 1, :] = jnp.zeros((1, size), jnp.float32)
+            ring_send[at : at + 1, 0:span] = jnp.where(rank == owner, total, 0.0)
+    ring_send[1:2, :] = small_sums[0:1, :]
+    ring_send[3:6, :] = small_sums[1:4, :]
+    counted = jnp.zeros((1, 1), jnp.float32)
+    for block in range(2):
+        valid_rows = row_mask(facts, block * window + rank * rows, rows)
+        counted = counted + jnp.sum(valid_rows, axis=0, keepdims=True)
+    ring_send[6:7, :] = jnp.broadcast_to(counted, (1, size))
+    for line in (0, 2, 7):
+        ring_send[line : line + 1, :] = jnp.zeros((1, size), jnp.float32)
+    ring_moves = [
+        links.copy(ring_send, ring_in.at[step - 1], ring[step - 1]) for step in range(1, 8)
+    ]
     token_sum_1.forward()
     bring_gates.wait()
     state_norm_grad, gain_2 = rms_back(s1_ref[...], gains_ref[2:3, :], state_sum_1.finish())
+    for moved in moves_1:
+        links.sent(moved)
     direct_0, moves_0, pair_0 = gates_back(0, s0_ref[...], direct_1 + state_norm_grad)
-    past_send[0] = key_grad[0:window, :].astype(jnp.bfloat16)
-    past_send[1] = value_grad[0:window, :].astype(jnp.bfloat16)
+    bring_middle = [
+        pltpu.make_async_copy(
+            far_middle_grad.at[pl.ds(block * rows, rows)],
+            gate_values.at[:, pl.ds(block * size, size)],
+            local_sems.at[6 + block],
+        )
+        for block in range(2)
+    ]
+    for moved in bring_middle:
+        moved.start()
+    mixed_grad[0:window, :] = key_grad[0:window, :].astype(jnp.bfloat16)
+    mixed_grad[window : 2 * window, :] = value_grad[0:window, :].astype(jnp.bfloat16)
+    down_sum.bring_own()
     for moved in smixed_moves + [pair_1, pair_0]:
         moved.wait_recv()
     for c in range(3):
-        weight_grad(
-            gates_grad,
-            gate_rows.at[:, c * size : (c + 1) * size],
-            smixed_pair,
-            slice(c * reach, (c + 1) * reach),
-        )
+        weight_grad(gates_grad.at[c], gate_rows.at[:, c * size : (c + 1) * size], smixed_pair)
     gates_sum = PlaneSum(links, here, gates_grad, gates_first, gates_last).start()
-    weight_grad(wout_grad, branch_grad, mixed, slice(0, width))
+    weight_grad(wout_grad, branch_grad, mixed)
     wout_sum = PlaneSum(links, here, wout_grad, wout_first, wout_last).start()
-    up_sum.finish()
-    up_settle = Settle(links, here, up_sum, up_home)
+    for moved in ring_moves:
+        moved.wait_recv()
+    total = ring_send[...]
+    for step in range(7):
+        total = total + ring_in[step]
+    level_send[...] = total
+    level_moves = [
+        links.copy(level_send, level_in.at[step - 1], (here.dp, lax.rem(here.level + step, 4)))
+        for step in range(1, 4)
+    ]
+    down_sum.finish()
+    for moved in bring_middle:
+        moved.wait()
+    gain_1, turn_1 = finish_tokens(1, token_sum_1)
     for moved in moves_0:
         moved.wait_recv()
-    past_turn = home(past_send, past_home)
-    down_sum.finish()
+    past_turn = home(mixed_grad, past_home)
     down_settle = Settle(links, here, down_sum, down_home)
     for gather in (branch_1, branch_0):
         gather.sent()
@@ -1578,7 +1692,7 @@
     state_back(0)
     gather_cot(0)
     bring_snormed.wait()
-    weight_grad(wst_grad, branch_grad, state_cot, slice(0, 3 * width))
+    weight_grad(wst_grad, branch_grad, state_cot)
     wst_sum = PlaneSum(links, here, wst_grad, wst_first, wst_last).start()
     for block in range(2):
         bring_normed[block].wait()
@@ -1587,53 +1701,21 @@
         later = slice(size + part * 256, size + (part + 1) * 256)
         summed = dot(gate_rows[:, at], token_cot[0:window, :], TN)
         summed = summed + dot(gate_rows[:, later], token_cot[window : 2 * window, :], TN)
-        wtok_grad[at, :] = summed.astype(jnp.bfloat16)
+        store_grad(wtok_grad, at, summed)
     wtok_sum = PlaneSum(links, here, wtok_grad, wtok_first, wtok_last).start()
+    gates_sum.forward()
     state_sum_1.sent()
     state_sum_0 = state_sum(0)
     token_sum_0 = token_sum(0)
-    gain_1, turn_1 = finish_tokens(1, token_sum_1)
     state_sum_0.forward()
     token_sum_0.forward()
     wst_sum.forward()
-    gates_sum.forward()
     wtok_sum.forward()
     wout_sum.forward()
     state_norm_grad, gain = rms_back(s0_ref[...], gains_ref[2:3, :], state_sum_0.finish())
     carried_send[...] = (direct_0 + state_norm_grad).astype(jnp.bfloat16)
     carried_turn = home(carried_send, carried_in)
     gain_2 = gain_2 + gain
-    wst_sum.finish()
-    wst_settle = Settle(links, here, wst_sum, wst_home)
-    gain_0, turn_0 = finish_tokens(0, token_sum_0)
-
-    for head in range(heads):
-        lines = tile_grads[head, 0:8, :]
-        span = lines.shape[1]
-        for group in range(1, TILE // 8):
-            lines = lines + pltpu.roll(tile_grads[head, 8 * group : 8 * group + 8, :], span - 8 * group, 1)
-        total = lines[0:1]
-        for line in range(1, 8):
-            total = total + pltpu.roll(lines[line : line + 1], span - line, 1)
-        for owner in range(4):
-            at = 8 + heads * owner + head
-            ring_send[at : at + 1, :] = jnp.zeros((1, size), jnp.float32)
-            ring_send[at : at + 1, 0:span] = jnp.where(rank == owner, total, 0.0)
-    ring_send[0:1, :] = gain_0 + gain_1
-    ring_send[1:2, :] = small_sums[0:1, :]
-    ring_send[2:3, :] = gain_2
-    ring_send[3:6, :] = small_sums[1:4, :]
-    counted = jnp.zeros((1, 1), jnp.float32)
-    for block in range(2):
-        valid_rows = row_mask(facts, block * window + rank * rows, rows)
-        counted = counted + jnp.sum(valid_rows, axis=0, keepdims=True)
-    ring_send[6:7, :] = jnp.broadcast_to(counted, (1, size))
-    ring_send[7:8, :] = jnp.zeros((1, size), jnp.float32)
-    ring_moves = [
-        links.copy(ring_send, ring_in.at[step - 1], ring[step - 1]) for step in range(1, 8)
-    ]
-    wtok_sum.finish()
-    wtok_settle = Settle(links, here, wtok_sum, wtok_home)
     gates_sum.finish()
     slot = here.level * 2 + here.core
     piece = rows // 4
@@ -1642,12 +1724,25 @@
         to_level = lax.rem(here.level + step, 4)
         for to_core, chip in ((here.core, here.dp), (1 - here.core, other)):
             start = here.planes[0] * 2 * rows + to_core * rows + to_level * piece
-            source = gates_grad.at[rows_at(start, piece, piece)]
+            source = rows_of(gates_grad, start, piece, piece)
             if step == 0 and chip is here.dp:
                 kept = pltpu.make_async_copy(source, gates_home.at[slot], local_sems.at[3])
                 kept.start()
             else:
                 gate_moves.append(links.copy(source, gates_home.at[slot], (chip, to_level)))
+    wst_sum.finish()
+    wst_settle = Settle(links, here, wst_sum, wst_home)
+    gain_0, turn_0 = finish_tokens(0, token_sum_0)
+
+    late_send[...] = jnp.concatenate(
+        [gain[:, step * 256 : (step + 1) * 256] for gain in (gain_0 + gain_1, gain_2) for step in range(4)],
+        axis=0,
+    )
+    late_moves = [
+        links.copy(late_send, late_in.at[step - 1], ring[step - 1]) for step in range(1, 8)
+    ]
+    wtok_sum.finish()
+    wtok_settle = Settle(links, here, wtok_sum, wtok_home)
     wout_sum.finish()
     wout_settle = Settle(links, here, wout_sum, wout_home)
     carried_turn.arrived()
@@ -1663,14 +1758,14 @@
         initial_moves.append(
             links.copy(initial_send.at[:, columns], initial_in.at[step - 1], ring[step - 1])
         )
-    for moved in ring_moves:
+    for moved in late_moves:
         moved.wait_recv()
-    total = ring_send[...]
+    late = late_send[...]
     for step in range(7):
-        total = total + ring_in[step]
-    level_send[...] = total
-    level_moves = [
-        links.copy(level_send, level_in.at[step - 1], (here.dp, lax.rem(here.level + step, 4)))
+        late = late + late_in[step]
+    late_level_send[...] = late
+    late_level_moves = [
+        links.copy(late_level_send, late_level_in.at[step - 1], (here.dp, lax.rem(here.level + step, 4)))
         for step in range(1, 4)
     ]
     for moved in initial_moves:
@@ -1686,6 +1781,14 @@
     for step in range(3):
         total = total + level_in[step]
     totals[...] = total
+    for moved in late_level_moves:
+        moved.wait_recv()
+    late = late_level_send[...]
+    for step in range(3):
+        late = late + late_level_in[step]
+    for row, first in ((0, 0), (2, 4)):
+        for step in range(4):
+            totals[row : row + 1, step * 256 : (step + 1) * 256] = late[first + step : first + step + 1, :]
     kept.wait()
     for moved in gate_moves:
         moved.wait_recv()
@@ -1742,6 +1845,7 @@
         ]
     )
 
+    stacked = lambda weight: jnp.transpose(weight, (1, 0, 2))
     shape = jax.ShapeDtypeStruct
     vmem = pltpu.VMEM
     rs = row_sum_scratch(rows, size)
@@ -1754,10 +1858,10 @@
         ((2 * window, 3 * width), low),
         ((2 * window, 2 * heads), full),
         ((2 * window, width), low),
-        ((size, 3 * width), low),
-        ((size, 3 * width), low),
+        ((3, size, width), low),
+        ((3, size, width), low),
         ((size, width), low),
-        ((size, 3 * size), low),
+        ((3, size, size), low),
         ((2 * rows, size), low),
         ((rows, size), full),
         ((rows, size), full),
@@ -1765,7 +1869,7 @@
     (
         normed, snormed, queries, keys, values, sqkv, lse, mixed, wst_all, wtok_all, wout_all, gates_all,
         x, s0, s1, gate_values, gstate, wup_grad, wdn_grad, smixed_rows, s2, facts,
-        block_out, middle_grad, small_sums,
+        block_out, middle_grad, branch_rows, small_sums,
     ) = run_kernel(
         forward_kernel,
         [shape(*of) for of in kept]
@@ -1779,12 +1883,14 @@
             shape((8, 2 * window), full),
             shape((2 * rows, size), low),
             shape((2 * rows, size), full),
+            shape((2 * rows, size), low),
             shape((8, size), full),
         ],
         [vmem(*of) for of in kept]
         + [
             vmem((2 * window, width), low),
             vmem((heads, TILE, 3 * TILE), full),
+            vmem((rows, size), low),
             vmem((rows, size), low),
             vmem((rows, size), low),
             vmem((rows, size), full),
@@ -1812,44 +1918,50 @@
             jnp.swapaxes(past_keys[0], 0, 1),
             facts_in,
             grad_output[0].reshape(blocks * rows, size),
-            grad_state[0].astype(low),
+            grad_state[0],
             norm_gains,
-            state_qkv.reshape(model_rows, 3 * width),
-            token_qkv.reshape(model_rows, 3 * width),
+            stacked(state_qkv),
+            stacked(token_qkv),
             token_out,
-            state_gates.reshape(model_rows, 3 * size),
+            stacked(state_gates),
             mlp_up,
             mlp_down,
         ],
-        far_in=(3, 5, 6, 12, 13),
+        far_in=(3, 5, 12, 13),
         far_out=range(len(kept) + 4),
     )
-    grads = [("wst", 3 * width), ("wtok", 3 * width), ("wout", width), ("gates", 6 * width)]
+    grads = [((3,), width), ((3,), width), ((), width), ((3,), 2 * width)]
     (
         block_home, state_home, tokens_home, past_home, carried_grad, initial_grad, totals,
-        up_home, down_home, wst_home, wtok_home, wout_home, gates_home, *_,
+        up_home, down_home, wst_home, wtok_home, wout_home, gates_home,
     ) = run_kernel(
         cotangent_kernel,
         [
             shape((2 * rows, size), low),
             shape((rows, size), low),
             shape((2 * rows, size), low),
-            shape((2, window, width), low),
+            shape((2 * window, width), low),
             shape((rows, size), full),
             shape((rows, size // dp_size), full),
             shape((16, size), full),
             shape((2, rows, units), low),
             shape((2, rows, units), low),
-            shape((2, rows, 3 * width), low),
-            shape((2, rows, 3 * width), low),
+            shape((2, 3, rows, width), low),
+            shape((2, 3, rows, width), low),
             shape((2, rows, width), low),
-            shape((8, rows // 4, 6 * width), low),
-            shape((4, rows, units), low),
-            shape((4, rows, units), low),
-            shape((2, rows, units), low),
-            shape((2, rows, units), low),
+            shape((8, 3, rows // 4, 2 * width), low),
         ],
         [
+            vmem((3, size, size), low),
+            vmem((size, width), low),
+            vmem((2 * window, width), low),
+            vmem((3 * window, width), low),
+            vmem((2 * window, 3 * width), low),
+            vmem((3 * window, width), low),
+            vmem((2 * window, 2 * heads), full),
+            vmem((2 * window, width), low),
+            vmem((3, size, width), low),
+            vmem((3, size, width), low),
             vmem((heads, TILE, 3 * TILE), full),
             vmem((heads, TILE, 3 * TILE), full),
             vmem((2 * window, size), low),
@@ -1864,42 +1976,45 @@
             vmem((2 * window, 3 * width), low),
             vmem((rows, 3 * size), full),
             vmem((4 * rows, 2 * width), low),
-            vmem((2, rows, size), low),
+            vmem((rows, size), low),
             vmem((2 * rows, size), low),
             vmem((rows, size), low),
             vmem((rows, size), low),
-            vmem((2, window, width), low),
             vmem((rows, size), low),
             vmem((dp_size - 1, rows, size // dp_size), low),
         ]
-        + [vmem((size, columns), low) for _, columns in grads]
-        + [vmem((4, rows, columns), low) for _, columns in grads]
-        + [vmem((2, rows, columns), low) for _, columns in grads]
-        + [vmem((2, rows, units), low)] * 2
+        + [vmem((*stack, size, columns), low) for stack, columns in grads]
+        + [vmem((4, *stack, rows, columns), low) for stack, columns in grads]
+        + [vmem((2, *stack, rows, columns), low) for stack, columns in grads]
+        + [vmem((4, rows, units), low)] * 2
+        + [vmem((2, rows, units), low)] * 4
         + [
-            vmem((6, rows, units), low),
             vmem((dp_size - 1, 16, size), full),
             vmem((levels - 1, 16, size), full),
             vmem((16, size), full),
             vmem((16, size), full),
+            vmem((dp_size - 1, 8, size // 4), full),
+            vmem((levels - 1, 8, size // 4), full),
+            vmem((8, size // 4), full),
+            vmem((8, size // 4), full),
         ]
         + rs * 3
         + sems(128)
-        + [pltpu.SemaphoreType.DMA((6,)), pltpu.SemaphoreType.DMA((6,))],
+        + [pltpu.SemaphoreType.DMA((8,)), pltpu.SemaphoreType.DMA((4,)), pltpu.SemaphoreType.DMA((15,))],
         1,
         "cotangent",
         [
-            middle_grad, gstate, x, s0, s1, gate_values, norm_gains, facts, facts_in,
+            middle_grad, branch_rows, gstate, x, s0, s1, gate_values, norm_gains, facts, facts_in,
             small_sums,
             normed, snormed, queries, keys, values, sqkv, lse, mixed, smixed_rows,
             wst_all, wtok_all, wout_all, gates_all, wup_grad, wdn_grad, block_out, s2,
         ],
-        far_in=(5, 10, 11, 23, 24, 25, 26),
-        far_out=(0, 1, 2, 3, 7, 8, 9, 10, 11, 12, 13, 14, 15, 16),
+        far_in=(0, 1, 3, 6, *range(11, 28)),
+        far_out=(0, 1, 2, 3, 7, 8, 9, 10, 11, 12),
     )
     both = lambda pair: pair[0].astype(full) + pair[1].astype(full)
-    gates_out = jnp.sum(gates_home.astype(full).reshape(levels, 2, rows // 4, 3, 2 * width), axis=0)
-    gates_out = jnp.transpose(gates_out, (1, 2, 0, 3)).reshape(rows // 4, 3, size)
+    gates_out = jnp.sum(gates_home.astype(full).reshape(levels, 2, 3, rows // 4, 2 * width), axis=0)
+    gates_out = jnp.transpose(gates_out, (2, 1, 0, 3)).reshape(rows // 4, 3, size)
     line_sums = totals[8 : 8 + levels * heads, 1 : window + 1][:, ::-1]
     table_all = jnp.dot(one_hot.T, line_sums.T, precision=HIGHEST)
     table_rows = table_all.shape[0] // dp_size
@@ -1913,14 +2028,14 @@
         rms_stats,
         tokens_home.reshape(1, blocks, rows, size),
         carried_grad[None],
-        jnp.swapaxes(past_home.astype(full), 0, 1)[None],
+        jnp.swapaxes(past_home.reshape(2, window, width).astype(full), 0, 1)[None],
         gains_out,
-        both(wtok_home).reshape(model_rows, 3, width),
+        stacked(both(wtok_home)),
         both(wout_home),
         table_out,
         both(up_home),
         both(down_home),
-        both(wst_home).reshape(model_rows, 3, width),
+        stacked(both(wst_home)),
         gates_out,
         initial_grad,
     )

time: 354 us -> 343 us (0.969)
  local copies, waits for them, and re-layouts: 18.7 us -> 10.6 us
    reshape x5 -> x1, local copies, waits for them, and re-layouts: 5.3 us -> 0.78 us  [grouped(): jnp.transpose(gates_out, (2, 1, 0, 3)).reshape(rows // 4, 3, size)]
    unnamed x45 -> x31, local copies, waits for them, and re-layouts: 10.1 us -> 5.64 us
where the time goes in v5:
time: 343 us; the launch traced here: 337 us
  Pallas kernels  316 us (92%)
  local copies, waits for them, and re-layouts  10.6 us (3%)
  other arithmetic  7.1 us (2%)
    pallas_call x2, Pallas kernels, run_kernel(): pl.pallas_call(body, out_shape=outs, in_specs=[far if at in far_in else v...  316 us

profile of v5, /device:TPU:0, one launch (start us, length us, event | category | flops | bytes accessed | tf_op | source)
XLA Modules:
  0.0 337.5 jit_solution(8908199348165394623)
XLA Ops:
  0.7 0.7 copy-done
  1.3 1.0 fusion.1
  2.3 0.4 rev.6
  4.2 0.7 fusion.4.facts_in.facts_home
  4.9 1.9 copy.43
  6.8 172.5 %forward.1 = (bf16[1024,1024]{1,0:T(8,128)(2,1)}, bf16[1024,1024]{1,0:T(8,128)(2,1)}, bf16[1024,256]{1,0:T(8,128)(2,1)}, bf16[1536,256]{1,0:T(8,128)(2,1)}, bf16...) custom-call(bf16[256,1024]{1,0:T(8,128)(2,1)} %bitcast.53, ...), custom_call_target="tpu_custom_call" | custom-call | tf_op jit(solution)/shard_map/forward/pallas_call | solution.py:1805
  179.3 143.5 %cotangent.1 = (bf16[256,1024]{1,0:T(8,128)(2,1)}, bf16[128,1024]{1,0:T(8,128)(2,1)}, bf16[256,1024]{1,0:T(8,128)(2,1)}, bf16[1024,256]{1,0:T(8,128)(2,1)}, f32[...) custom-call(f32[256,1024]{1,0:T(8,128)} %get-tuple-element.54.far_mi, ...), custom_call_target="tpu_custom_call" | custom-call | tf_op jit(solution)/shard_map/cotangent/pallas_call | solution.py:1805
  322.9 2.4 add_bitcast_fusion
  325.3 1.0 add_bitcast_fusion.2
  326.3 0.5 slice.40
  326.8 0.1 slice_reduce_fusion
  326.9 1.2 divide_sqrt_fusion
  328.1 1.5 copy.42
  329.8 0.8 copy.39
  330.6 0.8 bitcast_convert_fusion
  331.4 0.7 add_bitcast_fusion.4
  332.2 0.3 rev.7
  332.4 0.3 fusion
  332.7 0.7 dynamic_slice.7
  333.4 0.6 constant_dynamic-slice_fusion
  334.0 0.8 copy.50
  334.8 0.8 copy.51
  335.6 0.8 copy.52
  336.4 0.6 copy.53
  (31 shorter events, 0.5 us)
Async XLA Ops:
  0.6 0.7 copy-start
  322.9 2.5 copy-start.6
  322.9 2.5 copy-start.7
  322.9 3.4 %copy-start.11 = (f32[16,1024]{1,0:T(8,128)S(1)}, f32[16,1024]{1,0:T(8,128)}, u32[]{:S(2)}) copy-start(f32[16,1024]{1,0:T(8,128)} %get-tuple-element.82) | copy-start | bytes 196612
  322.9 5.2 %copy-start.2 = (bf16[1024,256]{1,0:T(8,128)(2,1)S(1)}, bf16[1024,256]{1,0:T(8,128)(2,1)}, u32[]{:S(2)}) copy-start(bf16[1024,256]{1,0:T(8,128)(2,1)} %get-tuple-element.85) | copy-start | bytes 1572868
  325.3 4.3 %copy-start.1 = (bf16[8,3,32,512]{3,2,1,0:T(8,128)(2,1)S(1)}, bf16[8,3,32,512]{3,2,1,0:T(8,128)(2,1)}, u32[]{:S(2)}) copy-start(bf16[8,3,32,512]{3,2,1,0:T(8,128)(2,1)} %get-tuple-element.91) | copy-start | bytes 2359300
  326.3 4.3 %copy-start.8 = (bf16[128,1024]{1,0:T(8,128)(2,1)S(1)}, bf16[128,1024]{1,0:T(8,128)(2,1)}, u32[]{:S(2)}) copy-start(bf16[128,1024]{1,0:T(8,128)(2,1)} %get-tuple-element.81) | copy-start | bytes 786436
  328.1 3.3 copy-start.9
  328.1 4.3 %copy-start.12 = (s32[512]{0:T(512)S(1)}, s32[512]{0:T(512)}, u32[]{:S(2)}) copy-start(s32[512]{0:T(512)} %param.22) | copy-start | bytes 6148
  328.1 5.9 %copy-start.5 = (bf16[256,1024]{1,0:T(8,128)(2,1)S(1)}, bf16[256,1024]{1,0:T(8,128)(2,1)}, u32[]{:S(2)}) copy-start(bf16[256,1024]{1,0:T(8,128)(2,1)} %get-tuple-element.80) | copy-start | bytes 1572868
  329.6 5.2 %copy-start.4 = (bf16[256,1024]{1,0:T(8,128)(2,1)S(1)}, bf16[256,1024]{1,0:T(8,128)(2,1)}, u32[]{:S(2)}) copy-start(bf16[256,1024]{1,0:T(8,128)(2,1)} %get-tuple-element.83) | copy-start | bytes 1572868
  329.8 5.8 %copy-start.3 = (f32[128,1024]{1,0:T(8,128)S(1)}, f32[128,1024]{1,0:T(8,128)}, u32[]{:S(2)}) copy-start(f32[128,1024]{1,0:T(8,128)} %get-tuple-element.84) | copy-start | bytes 1572868
  330.6 5.8 %copy-start.10 = (f32[128,128]{1,0:T(8,128)S(1)}, f32[128,128]{1,0:T(8,128)}, u32[]{:S(2)}) copy-start(f32[128,128]{1,0:T(8,128)} %get-tuple-element.126) | copy-start | bytes 196612

commit v6 on v5

--- a/solution.py
+++ b/solution.py
@@ -1307,6 +1307,63 @@
         self.crossed.wait_recv()
 
 
+class GateHome:
+    def __init__(self, links, here, grad, target, rows):
+        self.links, self.here = links, here
+        low = lax.rem(here.level, 2)
+        piece = rows // 4
+        self.slot = target.at[2 * here.half + here.core]
+        chip = here.dp - here.core + low
+        self.stays = here.core == low
+        self.moves = {}
+        for step in range(4):
+            to_level = lax.rem(here.level + step, 4)
+            start = here.planes[0] * 2 * rows + low * rows + to_level * piece
+            source = rows_of(grad, start, piece, piece)
+            for core in range(2):
+                moved = links.plan(source, self.slot, (chip, to_level))
+                self.moves[step, core] = moved
+                sends = here.core == core
+                if step == 0:
+                    kept = pltpu.make_async_copy(source, self.slot, links.recv_sems.at[links.used - 1])
+                    self.moves[core] = kept
+
+                    @pl.when(sends & self.stays)
+                    def _(kept=kept):
+                        kept.start()
+
+                    sends = sends & jnp.logical_not(self.stays)
+
+                @pl.when(sends)
+                def _(moved=moved):
+                    moved.start()
+
+    def arrived(self):
+        for step in range(4):
+            comes = lax.rem(self.here.level + step, 2) == self.here.core
+            for core in range(2):
+                own = self.here.core == core
+                if step == 0:
+
+                    @pl.when(comes & own)
+                    def _(kept=self.moves[core]):
+                        kept.wait()
+
+                    comes_here = comes & jnp.logical_not(own)
+                else:
+                    comes_here = comes
+
+                @pl.when(comes_here)
+                def _(moved=self.moves[step, core]):
+                    moved.wait_recv()
+
+                sent = own & jnp.logical_not(self.stays) if step == 0 else own
+
+                @pl.when(sent)
+                def _(moved=self.moves[step, core]):
+                    moved.wait_send()
+
+
 def cotangent_kernel(
     far_middle_grad, far_branch_rows, gstate_ref, far_x, s0_ref, s1_ref, far_gate_values, gains_ref, facts, facts_home,
     small_sums,
@@ -1321,7 +1378,7 @@
     wst_grad, wtok_grad, wout_grad, gates_grad,
     wst_first, wtok_first, wout_first, gates_first, wst_last, wtok_last, wout_last, gates_last,
     up_first, down_first, up_last, down_last, up_held, down_held, ring_in, level_in, ring_send, level_send,
-    late_in, late_level_in, late_send, late_level_send,
+    late_in, late_level_in, late_send, late_level_send, gate_pair_in,
     *rest,
 ):
     rs = [rest[0:4], rest[4:8], rest[8:12]]
@@ -1717,19 +1774,8 @@
     carried_turn = home(carried_send, carried_in)
     gain_2 = gain_2 + gain
     gates_sum.finish()
-    slot = here.level * 2 + here.core
-    piece = rows // 4
-    gate_moves = []
-    for step in range(4):
-        to_level = lax.rem(here.level + step, 4)
-        for to_core, chip in ((here.core, here.dp), (1 - here.core, other)):
-            start = here.planes[0] * 2 * rows + to_core * rows + to_level * piece
-            source = rows_of(gates_grad, start, piece, piece)
-            if step == 0 and chip is here.dp:
-                kept = pltpu.make_async_copy(source, gates_home.at[slot], local_sems.at[3])
-                kept.start()
-            else:
-                gate_moves.append(links.copy(source, gates_home.at[slot], (chip, to_level)))
+    low = lax.rem(here.level, 2)
+    gates_pair = links.copy(gates_sum.result(1 - low), gate_pair_in, mates[2])
     wst_sum.finish()
     wst_settle = Settle(links, here, wst_sum, wst_home)
     gain_0, turn_0 = finish_tokens(0, token_sum_0)
@@ -1741,6 +1787,12 @@
     late_moves = [
         links.copy(late_send, late_in.at[step - 1], ring[step - 1]) for step in range(1, 8)
     ]
+    gates_pair.wait_recv()
+    gates_part = gates_sum.result(low)
+    gates_part[...] = (
+        gates_part[...].astype(jnp.float32) + gate_pair_in[...].astype(jnp.float32)
+    ).astype(jnp.bfloat16)
+    gate_moves = GateHome(links, here, gates_grad, gates_home, rows)
     wtok_sum.finish()
     wtok_settle = Settle(links, here, wtok_sum, wtok_home)
     wout_sum.finish()
@@ -1789,9 +1841,7 @@
     for row, first in ((0, 0), (2, 4)):
         for step in range(4):
             totals[row : row + 1, step * 256 : (step + 1) * 256] = late[first + step : first + step + 1, :]
-    kept.wait()
-    for moved in gate_moves:
-        moved.wait_recv()
+    gate_moves.arrived()
     for turn in (block_turn, state_turn, past_turn, turn_1, turn_0):
         turn.arrived()
     for settle in (up_settle, down_settle, wout_settle, wst_settle, wtok_settle):
@@ -1949,7 +1999,7 @@
             shape((2, 3, rows, width), low),
             shape((2, 3, rows, width), low),
             shape((2, rows, width), low),
-            shape((8, 3, rows // 4, 2 * width), low),
+            shape((4, 3, rows // 4, 2 * width), low),
         ],
         [
             vmem((3, size, size), low),
@@ -1997,6 +2047,7 @@
             vmem((levels - 1, 8, size // 4), full),
             vmem((8, size // 4), full),
             vmem((8, size // 4), full),
+            vmem((3, rows, 2 * width), low),
         ]
         + rs * 3
         + sems(128)
@@ -2013,7 +2064,7 @@
         far_out=(0, 1, 2, 3, 7, 8, 9, 10, 11, 12),
     )
     both = lambda pair: pair[0].astype(full) + pair[1].astype(full)
-    gates_out = jnp.sum(gates_home.astype(full).reshape(levels, 2, 3, rows // 4, 2 * width), axis=0)
+    gates_out = jnp.sum(gates_home.astype(full).reshape(2, 2, 3, rows // 4, 2 * width), axis=0)
     gates_out = jnp.transpose(gates_out, (2, 1, 0, 3)).reshape(rows // 4, 3, size)
     line_sums = totals[8 : 8 + levels * heads, 1 : window + 1][:, ::-1]
     table_all = jnp.dot(one_hot.T, line_sums.T, precision=HIGHEST)

time: 343 us -> 338 us (0.985)
  Pallas kernels: 316 us -> 312 us
    pallas_call x2, Pallas kernels: 316 us -> 312 us  [run_kernel(): pl.pallas_call(body, out_shape=outs, in_specs=[far if at in far_in else v...]
where the time goes in v6:
time: 338 us; the launch traced here: 333 us
  Pallas kernels  312 us (92%)
  local copies, waits for them, and re-layouts  10.6 us (3%)
  other arithmetic  7.04 us (2%)
    pallas_call x2, Pallas kernels, run_kernel(): pl.pallas_call(body, out_shape=outs, in_specs=[far if at in far_in else v...  312 us

profile of v6, /device:TPU:0, one launch (start us, length us, event | category | flops | bytes accessed | tf_op | source)
XLA Modules:
  0.0 333.1 jit_solution(1234892688770298482)
XLA Ops:
  0.7 0.7 copy-done
  1.3 1.0 fusion.1
  2.3 0.4 rev.6
  4.2 0.7 fusion.4.facts_in.facts_home
  4.9 1.9 copy.43
  6.8 172.5 %forward.1 = (bf16[1024,1024]{1,0:T(8,128)(2,1)}, bf16[1024,1024]{1,0:T(8,128)(2,1)}, bf16[1024,256]{1,0:T(8,128)(2,1)}, bf16[1536,256]{1,0:T(8,128)(2,1)}, bf16...) custom-call(bf16[256,1024]{1,0:T(8,128)(2,1)} %bitcast.52, ...), custom_call_target="tpu_custom_call" | custom-call | tf_op jit(solution)/shard_map/forward/pallas_call | solution.py:1855
  179.3 139.2 %cotangent.1 = (bf16[256,1024]{1,0:T(8,128)(2,1)}, bf16[128,1024]{1,0:T(8,128)(2,1)}, bf16[256,1024]{1,0:T(8,128)(2,1)}, bf16[1024,256]{1,0:T(8,128)(2,1)}, f32[...) custom-call(f32[256,1024]{1,0:T(8,128)} %get-tuple-element.54.far_mi, ...), custom_call_target="tpu_custom_call" | custom-call | tf_op jit(solution)/shard_map/cotangent/pallas_call | solution.py:1855
  318.6 2.4 add_bitcast_fusion
  321.1 1.0 add_bitcast_fusion.2
  322.0 0.5 slice.40
  322.5 0.1 slice_reduce_fusion
  322.7 1.2 divide_sqrt_fusion
  323.8 1.5 copy.42
  325.4 0.8 copy.39
  326.2 0.8 bitcast_convert_fusion
  327.1 0.7 add_bitcast_fusion.4
  327.8 0.3 rev.7
  328.1 0.3 fusion
  328.4 0.7 dynamic_slice.7
  329.0 0.6 constant_dynamic-slice_fusion
  329.7 0.8 copy.50
  330.5 0.8 copy.51
  331.3 0.8 copy.52
  332.1 0.6 copy.53
  (31 shorter events, 0.4 us)
Async XLA Ops:
  0.6 0.7 copy-start
  318.6 2.5 copy-start.6
  318.6 2.5 copy-start.7
  318.6 3.4 %copy-start.11 = (f32[16,1024]{1,0:T(8,128)S(1)}, f32[16,1024]{1,0:T(8,128)}, u32[]{:S(2)}) copy-start(f32[16,1024]{1,0:T(8,128)} %get-tuple-element.82) | copy-start | bytes 196612
  318.6 5.2 %copy-start.1 = (bf16[1024,256]{1,0:T(8,128)(2,1)S(1)}, bf16[1024,256]{1,0:T(8,128)(2,1)}, u32[]{:S(2)}) copy-start(bf16[1024,256]{1,0:T(8,128)(2,1)} %get-tuple-element.85) | copy-start | bytes 1572868
  321.0 4.3 %copy-start.5 = (bf16[4,3,32,512]{3,2,1,0:T(8,128)(2,1)S(1)}, bf16[4,3,32,512]{3,2,1,0:T(8,128)(2,1)}, u32[]{:S(2)}) copy-start(bf16[4,3,32,512]{3,2,1,0:T(8,128)(2,1)} %get-tuple-element.91) | copy-start | bytes 1179652
  321.1 5.2 %copy-start.8 = (bf16[128,1024]{1,0:T(8,128)(2,1)S(1)}, bf16[128,1024]{1,0:T(8,128)(2,1)}, u32[]{:S(2)}) copy-start(bf16[128,1024]{1,0:T(8,128)(2,1)} %get-tuple-element.81) | copy-start | bytes 786436
  322.0 5.0 %copy-start.9 = (bf16[2,128,256]{2,1,0:T(8,128)(2,1)S(1)}, bf16[2,128,256]{2,1,0:T(8,128)(2,1)}, u32[]{:S(2)}) copy-start(bf16[2,128,256]{2,1,0:T(8,128)(2,1)} %get-tuple-element.87) | copy-start | bytes 393220
  323.8 4.3 %copy-start.12 = (s32[512]{0:T(512)S(1)}, s32[512]{0:T(512)}, u32[]{:S(2)}) copy-start(s32[512]{0:T(512)} %param.22) | copy-start | bytes 6148
  323.8 5.8 %copy-start.4 = (bf16[256,1024]{1,0:T(8,128)(2,1)S(1)}, bf16[256,1024]{1,0:T(8,128)(2,1)}, u32[]{:S(2)}) copy-start(bf16[256,1024]{1,0:T(8,128)(2,1)} %get-tuple-element.80) | copy-start | bytes 1572868
  325.4 5.1 %copy-start.3 = (bf16[256,1024]{1,0:T(8,128)(2,1)S(1)}, bf16[256,1024]{1,0:T(8,128)(2,1)}, u32[]{:S(2)}) copy-start(bf16[256,1024]{1,0:T(8,128)(2,1)} %get-tuple-element.83) | copy-start | bytes 1572868
  325.4 5.8 %copy-start.2 = (f32[128,1024]{1,0:T(8,128)S(1)}, f32[128,1024]{1,0:T(8,128)}, u32[]{:S(2)}) copy-start(f32[128,1024]{1,0:T(8,128)} %get-tuple-element.84) | copy-start | bytes 1572868
  326.2 5.8 %copy-start.10 = (f32[128,128]{1,0:T(8,128)S(1)}, f32[128,128]{1,0:T(8,128)}, u32[]{:S(2)}) copy-start(f32[128,128]{1,0:T(8,128)} %get-tuple-element.126) | copy-start | bytes 196612

commit v7 on v6

--- a/solution.py
+++ b/solution.py
@@ -785,6 +785,13 @@
         for moved in (self.near_far, self.near_own, self.far):
             self.links.sent(moved)
 
+    def split(self):
+        self.near_far.wait_recv()
+        summed = self.part(2)[...].astype(jnp.float32) + self.near_in[0].astype(jnp.float32)
+        self.near_own.wait_recv()
+        own = self.part(0)[...].astype(jnp.float32) + self.near_in[1].astype(jnp.float32)
+        return summed.astype(jnp.bfloat16), own
+
     def finish(self):
         self.near_own.wait_recv()
         self.far.wait_recv()
@@ -857,7 +864,7 @@
     far_normed, far_snormed, far_queries, far_keys, far_values, far_state_qkv, far_lse, far_mixed,
     far_wst, far_wtok, far_wout, far_gates, far_x, far_s0, far_s1,
     far_gate_values, far_gstate_here, far_wup_grad, far_wdn_grad,
-    smixed_rows, s2_ref, facts, block_out, middle_grad, branch_rows, small_sums,
+    smixed_rows, s2_ref, facts, feed_far, feed_own, result_own, middle_grad, branch_rows, small_sums,
     normed, snormed, queries, keys, values, state_qkv, lse_ref, mixed,
     wst, wtok, wout, gates, x_ref, s0_ref, s1_ref,
     smixed, tiles, initial_all, normed_send, gstate_send, s0_send, gate_values, wup, wdn, middle,
@@ -1046,6 +1053,12 @@
         return RowSum(links, here, *rs[block], rows).fill(
             lambda which: dot(hidden[rows_at(block * window + which * rows, rows), :], wdn[...], NT)
         )
+
+    def store_feed(block, summed):
+        at = slice(block * rows, (block + 1) * rows)
+        feed_far[block], own = summed.split()
+        feed_own[at, :] = own.astype(jnp.bfloat16)
+        result_own[at, :] = middle[at, :] + own
 
     def start_gout(block):
         at = slice(block * rows, (block + 1) * rows)
@@ -1159,23 +1172,15 @@
     gather_g1 = start_gout(1)
     sums[1].sent()
     feed_1 = feed_sum(1)
-    feed_0.forward()
+    store_feed(0, feed_0)
     back_0 = feed_back(0, gather_g0)
     back_0.forward()
     back_1 = feed_back(1, gather_g1)
-    feed_1.forward()
+    store_feed(1, feed_1)
     keep_down = weight_grad(grad_stage, gout, hidden, far_wdn_grad, local_sems.at[1])
     back_1.forward()
     keep_up = weight_grad(hidden, middle_normed, up_grad, far_wup_grad, local_sems.at[2])
-    feed_total, result_total, gain_total = 0.0, 0.0, 0.0
-    for block, feed_here in ((0, feed_0), (1, feed_1)):
-        at = slice(block * rows, (block + 1) * rows)
-        feed = feed_here.finish()
-        result = middle[at, :] + feed
-        block_out[at, :] = result.astype(jnp.bfloat16)
-        share = row_mask(facts, block * window + rank * rows, rows)
-        feed_total = feed_total + jnp.sum(feed * feed * share, axis=0, keepdims=True)
-        result_total = result_total + jnp.sum(result * result * share, axis=0, keepdims=True)
+    gain_total = 0.0
     for block, back_here in ((1, back_1), (0, back_0)):
         at = slice(block * rows, (block + 1) * rows)
         straight, gain = rms_back(middle[at, :], gains_ref[1:2, :], back_here.finish())
@@ -1184,8 +1189,7 @@
         branch_rows[at, :] = total.astype(jnp.bfloat16)
         gain_total = gain_total + gain
     small_sums[...] = jnp.concatenate(
-        [gain_total, result_total, branch_total, feed_total]
-        + [jnp.zeros((4, gain_total.shape[1]), jnp.float32)],
+        [gain_total, branch_total, jnp.zeros((6, gain_total.shape[1]), jnp.float32)],
         axis=0,
     )
     gstate_turn.arrived()
@@ -1368,7 +1372,8 @@
     far_middle_grad, far_branch_rows, gstate_ref, far_x, s0_ref, s1_ref, far_gate_values, gains_ref, facts, facts_home,
     small_sums,
     far_normed, far_snormed, far_queries, far_keys, far_values, far_state_qkv, far_lse, far_mixed,
-    far_smixed, far_wst, far_wtok, far_wout, far_gates, far_wup_grad, far_wdn_grad, far_block_out, far_state_out,
+    far_smixed, far_wst, far_wtok, far_wout, far_gates, far_wup_grad, far_wdn_grad, far_feed, far_feed_own, far_result_own,
+    far_state_out,
     block_home, state_home, tokens_home, past_home, carried_grad, initial_grad, totals,
     up_home, down_home, wst_home, wtok_home, wout_home, gates_home,
     gates, wout, queries, keys, state_qkv, values, lse_ref, mixed, wst, wtok,
@@ -1379,6 +1384,7 @@
     wst_first, wtok_first, wout_first, gates_first, wst_last, wtok_last, wout_last, gates_last,
     up_first, down_first, up_last, down_last, up_held, down_held, ring_in, level_in, ring_send, level_send,
     late_in, late_level_in, late_send, late_level_send, gate_pair_in,
+    feed_in, feed_own,
     *rest,
 ):
     rs = [rest[0:4], rest[4:8], rest[8:12]]
@@ -1416,6 +1422,7 @@
         (far_wst, wst),
         (far_wtok, wtok),
         (far_x, tokens_send),
+        (far_feed_own, feed_own),
         (far_smixed.at[pl.ds(0, rows), own_half], smixed_pair.at[pair_rows(0)]),
         (far_smixed.at[pl.ds(rows, rows), own_half], smixed_pair.at[pair_rows(1)]),
     ):
@@ -1633,8 +1640,16 @@
     down_sum = FarPlaneSum(
         links, here, far_wdn_grad, down_first, down_last, down_held, held_sems.at[pl.ds(2, 2)]
     ).start()
-    bring_gates = pltpu.make_async_copy(far_gate_values.at[pl.ds(0, rows)], gate_values, local_sems.at[0])
-    bring_gates.start()
+    bring_result = [
+        pltpu.make_async_copy(
+            far_result_own.at[pl.ds(block * rows, rows)],
+            gate_values.at[:, pl.ds(block * size, size)],
+            local_sems.at[6 + block],
+        )
+        for block in range(2)
+    ]
+    for moved in bring_result:
+        moved.start()
     for ref in (tile_grads, key_grad, value_grad, skey_grad, svalue_grad):
         ref[...] = jnp.zeros(ref.shape, ref.dtype)
     bias_tiles(facts, tiles, heads, 3 * TILE, LOG2E)
@@ -1643,13 +1658,30 @@
         moved.wait()
     mix_back(1, branch_1)
     branch_0 = RowGather(links, here, branch_grad, 0, rows).start()
-    block_turn = home(far_block_out, block_home)
+    feed_moves = [links.copy(far_feed.at[block], feed_in.at[block], mates[2]) for block in range(2)]
     state_turn = home(far_state_out, state_home)
     token_back(1)
     for moved in moves_1:
         moved.wait_recv()
     state_back(1)
     gather_cot(1)
+    result_total, feed_total = 0.0, 0.0
+    for block in range(2):
+        at = slice(block * rows, (block + 1) * rows)
+        feed_moves[block].wait_recv()
+        bring_result[block].wait()
+        came = feed_in[block].astype(jnp.float32)
+        feed = feed_own[at, :].astype(jnp.float32) + came
+        result = gate_values[:, block * size : (block + 1) * size] + came
+        feed_in[block] = result.astype(jnp.bfloat16)
+        share = row_mask(facts, block * window + rank * rows, rows)
+        feed_total = feed_total + jnp.sum(feed * feed * share, axis=0, keepdims=True)
+        result_total = result_total + jnp.sum(result * result * share, axis=0, keepdims=True)
+    block_turns = [
+        home(feed_in.at[block], block_home.at[pl.ds(block * rows, rows)]) for block in range(2)
+    ]
+    bring_gates = pltpu.make_async_copy(far_gate_values.at[pl.ds(0, rows)], gate_values, local_sems.at[0])
+    bring_gates.start()
     up_sum.forward()
     state_sum_1 = state_sum(1)
     token_sum_1 = token_sum(1)
@@ -1675,7 +1707,9 @@
             ring_send[at : at + 1, :] = jnp.zeros((1, size), jnp.float32)
             ring_send[at : at + 1, 0:span] = jnp.where(rank == owner, total, 0.0)
     ring_send[1:2, :] = small_sums[0:1, :]
-    ring_send[3:6, :] = small_sums[1:4, :]
+    ring_send[3:4, :] = result_total
+    ring_send[4:5, :] = small_sums[1:2, :]
+    ring_send[5:6, :] = feed_total
     counted = jnp.zeros((1, 1), jnp.float32)
     for block in range(2):
         valid_rows = row_mask(facts, block * window + rank * rows, rows)
@@ -1842,7 +1876,7 @@
         for step in range(4):
             totals[row : row + 1, step * 256 : (step + 1) * 256] = late[first + step : first + step + 1, :]
     gate_moves.arrived()
-    for turn in (block_turn, state_turn, past_turn, turn_1, turn_0):
+    for turn in (*block_turns, state_turn, past_turn, turn_1, turn_0):
         turn.arrived()
     for settle in (up_settle, down_settle, wout_settle, wst_settle, wtok_settle):
         settle.arrived()
@@ -1919,7 +1953,7 @@
     (
         normed, snormed, queries, keys, values, sqkv, lse, mixed, wst_all, wtok_all, wout_all, gates_all,
         x, s0, s1, gate_values, gstate, wup_grad, wdn_grad, smixed_rows, s2, facts,
-        block_out, middle_grad, branch_rows, small_sums,
+        feed_far, feed_own, result_own, middle_grad, branch_rows, small_sums,
     ) = run_kernel(
         forward_kernel,
         [shape(*of) for of in kept]
@@ -1931,7 +1965,9 @@
             shape((2 * rows, size), low),
             shape((rows, size), low),
             shape((8, 2 * window), full),
+            shape((2, rows, size), low),
             shape((2 * rows, size), low),
+            shape((2 * rows, size), full),
             shape((2 * rows, size), full),
             shape((2 * rows, size), low),
             shape((8, size), full),
@@ -2048,19 +2084,21 @@
             vmem((8, size // 4), full),
             vmem((8, size // 4), full),
             vmem((3, rows, 2 * width), low),
+            vmem((2, rows, size), low),
+            vmem((2 * rows, size), low),
         ]
         + rs * 3
         + sems(128)
-        + [pltpu.SemaphoreType.DMA((8,)), pltpu.SemaphoreType.DMA((4,)), pltpu.SemaphoreType.DMA((15,))],
+        + [pltpu.SemaphoreType.DMA((8,)), pltpu.SemaphoreType.DMA((4,)), pltpu.SemaphoreType.DMA((16,))],
         1,
         "cotangent",
         [
             middle_grad, branch_rows, gstate, x, s0, s1, gate_values, norm_gains, facts, facts_in,
             small_sums,
             normed, snormed, queries, keys, values, sqkv, lse, mixed, smixed_rows,
-            wst_all, wtok_all, wout_all, gates_all, wup_grad, wdn_grad, block_out, s2,
+            wst_all, wtok_all, wout_all, gates_all, wup_grad, wdn_grad, feed_far, feed_own, result_own, s2,
         ],
-        far_in=(0, 1, 3, 6, *range(11, 28)),
+        far_in=(0, 1, 3, 6, *range(11, 30)),
         far_out=(0, 1, 2, 3, 7, 8, 9, 10, 11, 12),
     )
     both = lambda pair: pair[0].astype(full) + pair[1].astype(full)

time: 338 us -> 337 us (level)
  no operation moved by 1% of the time
where the time goes in v7:
time: 337 us; the launch traced here: 331 us
  Pallas kernels  309 us (92%)
  local copies, waits for them, and re-layouts  10.6 us (3%)
  other arithmetic  7.04 us (2%)
    pallas_call x2, Pallas kernels, run_kernel(): pl.pallas_call(body, out_shape=outs, in_specs=[far if at in far_in else v...  309 us

profile of v7, /device:TPU:0, one launch (start us, length us, event | category | flops | bytes accessed | tf_op | source)
XLA Modules:
  0.0 330.8 jit_solution(16064313570905024207)
XLA Ops:
  0.7 0.7 copy-done
  1.3 1.0 fusion.1
  2.3 0.4 rev.6
  4.2 0.7 fusion.4.facts_in.facts_home
  4.9 1.9 copy.43
  6.8 165.6 %forward.1 = (bf16[1024,1024]{1,0:T(8,128)(2,1)}, bf16[1024,1024]{1,0:T(8,128)(2,1)}, bf16[1024,256]{1,0:T(8,128)(2,1)}, bf16[1536,256]{1,0:T(8,128)(2,1)}, bf16...) custom-call(bf16[256,1024]{1,0:T(8,128)(2,1)} %bitcast.52, ...), custom_call_target="tpu_custom_call" | custom-call | tf_op jit(solution)/shard_map/forward/pallas_call | solution.py:1889
  172.4 143.8 %cotangent.1 = (bf16[256,1024]{1,0:T(8,128)(2,1)}, bf16[128,1024]{1,0:T(8,128)(2,1)}, bf16[256,1024]{1,0:T(8,128)(2,1)}, bf16[1024,256]{1,0:T(8,128)(2,1)}, f32[...) custom-call(f32[256,1024]{1,0:T(8,128)} %get-tuple-element.56.far_mi, ...), custom_call_target="tpu_custom_call" | custom-call | tf_op jit(solution)/shard_map/cotangent/pallas_call | solution.py:1889
  316.3 2.4 add_bitcast_fusion
  318.7 1.0 add_bitcast_fusion.2
  319.7 0.5 slice.40
  320.2 0.1 slice_reduce_fusion
  320.3 1.2 divide_sqrt_fusion
  321.5 1.5 copy.42
  323.1 0.8 copy.39
  323.9 0.8 bitcast_convert_fusion
  324.7 0.7 add_bitcast_fusion.4
  325.5 0.3 rev.7
  325.8 0.3 fusion
  326.1 0.7 dynamic_slice.7
  326.7 0.6 constant_dynamic-slice_fusion
  327.4 0.8 copy.50
  328.2 0.8 copy.51
  329.0 0.8 copy.52
  329.7 0.6 copy.53
  (31 shorter events, 0.4 us)
Async XLA Ops:
  0.6 0.7 copy-start
  316.2 2.5 copy-start.6
  316.3 2.5 copy-start.7
  316.3 3.4 %copy-start.11 = (f32[16,1024]{1,0:T(8,128)S(1)}, f32[16,1024]{1,0:T(8,128)}, u32[]{:S(2)}) copy-start(f32[16,1024]{1,0:T(8,128)} %get-tuple-element.86) | copy-start | bytes 196612
  316.3 5.2 %copy-start.1 = (bf16[1024,256]{1,0:T(8,128)(2,1)S(1)}, bf16[1024,256]{1,0:T(8,128)(2,1)}, u32[]{:S(2)}) copy-start(bf16[1024,256]{1,0:T(8,128)(2,1)} %get-tuple-element.89) | copy-start | bytes 1572868
  318.7 4.3 %copy-start.5 = (bf16[4,3,32,512]{3,2,1,0:T(8,128)(2,1)S(1)}, bf16[4,3,32,512]{3,2,1,0:T(8,128)(2,1)}, u32[]{:S(2)}) copy-start(bf16[4,3,32,512]{3,2,1,0:T(8,128)(2,1)} %get-tuple-element.95) | copy-start | bytes 1179652
  318.7 5.2 %copy-start.8 = (bf16[128,1024]{1,0:T(8,128)(2,1)S(1)}, bf16[128,1024]{1,0:T(8,128)(2,1)}, u32[]{:S(2)}) copy-start(bf16[128,1024]{1,0:T(8,128)(2,1)} %get-tuple-element.85) | copy-start | bytes 786436
  319.7 5.0 %copy-start.9 = (bf16[2,128,256]{2,1,0:T(8,128)(2,1)S(1)}, bf16[2,128,256]{2,1,0:T(8,128)(2,1)}, u32[]{:S(2)}) copy-start(bf16[2,128,256]{2,1,0:T(8,128)(2,1)} %get-tuple-element.91) | copy-start | bytes 393220
  321.5 4.3 %copy-start.12 = (s32[512]{0:T(512)S(1)}, s32[512]{0:T(512)}, u32[]{:S(2)}) copy-start(s32[512]{0:T(512)} %param.22) | copy-start | bytes 6148
  321.5 5.8 %copy-start.4 = (bf16[256,1024]{1,0:T(8,128)(2,1)S(1)}, bf16[256,1024]{1,0:T(8,128)(2,1)}, u32[]{:S(2)}) copy-start(bf16[256,1024]{1,0:T(8,128)(2,1)} %get-tuple-element.84) | copy-start | bytes 1572868
  323.0 5.1 %copy-start.3 = (bf16[256,1024]{1,0:T(8,128)(2,1)S(1)}, bf16[256,1024]{1,0:T(8,128)(2,1)}, u32[]{:S(2)}) copy-start(bf16[256,1024]{1,0:T(8,128)(2,1)} %get-tuple-element.87) | copy-start | bytes 1572868
  323.1 5.8 %copy-start.2 = (f32[128,1024]{1,0:T(8,128)S(1)}, f32[128,1024]{1,0:T(8,128)}, u32[]{:S(2)}) copy-start(f32[128,1024]{1,0:T(8,128)} %get-tuple-element.88) | copy-start | bytes 1572868
  323.9 5.8 %copy-start.10 = (f32[128,128]{1,0:T(8,128)S(1)}, f32[128,128]{1,0:T(8,128)}, u32[]{:S(2)}) copy-start(f32[128,128]{1,0:T(8,128)} %get-tuple-element.130) | copy-start | bytes 196612

commit v8 on v7

--- a/solution.py
+++ b/solution.py
@@ -1917,9 +1917,9 @@
     model_rows = token_qkv.shape[0]
     low, full = jnp.bfloat16, jnp.float32
 
-    one_hot = (bucket_ids[:, None] == jnp.arange(bias_table.shape[0])[None, :]).astype(full)
-    per_offset = jnp.dot(one_hot, bias_table, precision=HIGHEST)
-    lines = jnp.pad(per_offset[::-1].T, ((0, 0), (1, window - 1)), constant_values=NEGATIVE)
+    line_ids = jnp.pad(bucket_ids[::-1], (1, window - 1), constant_values=-1)[None, :]
+    one_hot = (jnp.arange(bias_table.shape[0])[:, None] == line_ids).astype(full)
+    lines = jnp.dot(bias_table.T, one_hot, precision=HIGHEST) + jnp.where(line_ids < 0, NEGATIVE, 0.0)
     numbers = jnp.stack([valid_count[0], fresh_start[0]]).astype(full)
     facts_in = jnp.concatenate(
         [
@@ -2104,13 +2104,16 @@
     both = lambda pair: pair[0].astype(full) + pair[1].astype(full)
     gates_out = jnp.sum(gates_home.astype(full).reshape(2, 2, 3, rows // 4, 2 * width), axis=0)
     gates_out = jnp.transpose(gates_out, (2, 1, 0, 3)).reshape(rows // 4, 3, size)
-    line_sums = totals[8 : 8 + levels * heads, 1 : window + 1][:, ::-1]
-    table_all = jnp.dot(one_hot.T, line_sums.T, precision=HIGHEST)
-    table_rows = table_all.shape[0] // dp_size
-    table_out = lax.dynamic_slice(table_all, (dp_at * table_rows, level * heads), (table_rows, heads))
+    table_rows = bias_table.shape[0] // dp_size
+    own_ids = dp_at * table_rows + jnp.arange(table_rows)
+    own_lines = lax.dynamic_slice(totals, (8 + level * heads, 0), (heads, 2 * window))
+    table_out = jnp.dot(
+        (own_ids[:, None] == line_ids).astype(full), own_lines.T, precision=HIGHEST
+    )
     share = size // (dp_size * levels)
     gains_out = lax.dynamic_slice(totals, (0, (dp_at * levels + level) * share), (3, share))
-    rms_stats = jnp.sqrt(jnp.sum(totals[3:6], axis=1) / totals[6, 0])
+    stat_sums = jnp.sum(totals[3:7], axis=1)
+    rms_stats = jnp.sqrt(stat_sums[:3] / (stat_sums[3] / size))
     return (
         block_home.reshape(1, blocks, rows, size),
         state_home.astype(full)[None],

time: 337 us -> 338 us (level)
  no operation moved by 1% of the time
where the time goes in v8:
time: 338 us; the launch traced here: 332 us
  Pallas kernels  310 us (92%)
  local copies, waits for them, and re-layouts  10.2 us (3%)
  other arithmetic  7.26 us (2%)
    pallas_call x2, Pallas kernels, run_kernel(): pl.pallas_call(body, out_shape=outs, in_specs=[far if at in far_in else v...  310 us

profile of v8, /device:TPU:0, one launch (start us, length us, event | category | flops | bytes accessed | tf_op | source)
XLA Modules:
  0.0 331.9 jit_solution(8943144509411373854)
XLA Ops:
  0.7 0.8 rev.3
  1.4 0.1 pad.4
  1.6 0.2 fusion
  3.1 0.1 pad.6.clone
  3.2 0.1 pad.7.clone
  3.3 0.7 maximum_maximum_fusion.facts_in.facts_home
  4.0 1.9 copy.43
  5.9 165.6 %forward.1 = (bf16[1024,1024]{1,0:T(8,128)(2,1)}, bf16[1024,1024]{1,0:T(8,128)(2,1)}, bf16[1024,256]{1,0:T(8,128)(2,1)}, bf16[1536,256]{1,0:T(8,128)(2,1)}, bf16...) custom-call(bf16[256,1024]{1,0:T(8,128)(2,1)} %bitcast.52, ...), custom_call_target="tpu_custom_call" | custom-call | tf_op jit(solution)/shard_map/forward/pallas_call | solution.py:1889
  171.5 144.1 %cotangent.1 = (bf16[256,1024]{1,0:T(8,128)(2,1)}, bf16[128,1024]{1,0:T(8,128)(2,1)}, bf16[256,1024]{1,0:T(8,128)(2,1)}, bf16[1024,256]{1,0:T(8,128)(2,1)}, f32[...) custom-call(f32[256,1024]{1,0:T(8,128)} %get-tuple-element.56.far_mi, ...), custom_call_target="tpu_custom_call" | custom-call | tf_op jit(solution)/shard_map/cotangent/pallas_call | solution.py:1889
  315.6 2.4 add_bitcast_fusion
  318.0 1.0 add_bitcast_fusion.2
  319.0 0.9 slice_reduce_fusion
  319.9 0.6 slice.41
  321.2 0.5 divide_sqrt_fusion
  321.7 1.5 copy.42
  323.3 0.8 copy.39
  324.1 0.8 bitcast_convert_fusion
  324.9 0.7 add_bitcast_fusion.4
  325.6 1.3 constant_dynamic-slice_fusion
  326.9 1.5 fusion.2
  328.4 0.8 copy.50
  329.2 0.8 copy.51
  330.0 0.8 copy.52
  330.8 0.6 copy.53
  (27 shorter events, 0.3 us)
Async XLA Ops:
  0.6 0.9 copy-start
  315.5 2.5 copy-start.6
  315.6 2.5 copy-start.7
  315.6 6.1 %copy-start.1 = (bf16[1024,256]{1,0:T(8,128)(2,1)S(1)}, bf16[1024,256]{1,0:T(8,128)(2,1)}, u32[]{:S(2)}) copy-start(bf16[1024,256]{1,0:T(8,128)(2,1)} %get-tuple-element.89) | copy-start | bytes 1572868
  318.0 5.2 %copy-start.5 = (bf16[4,3,32,512]{3,2,1,0:T(8,128)(2,1)S(1)}, bf16[4,3,32,512]{3,2,1,0:T(8,128)(2,1)}, u32[]{:S(2)}) copy-start(bf16[4,3,32,512]{3,2,1,0:T(8,128)(2,1)} %get-tuple-element.95) | copy-start | bytes 1179652
  318.0 6.0 %copy-start.8 = (bf16[128,1024]{1,0:T(8,128)(2,1)S(1)}, bf16[128,1024]{1,0:T(8,128)(2,1)}, u32[]{:S(2)}) copy-start(bf16[128,1024]{1,0:T(8,128)(2,1)} %get-tuple-element.85) | copy-start | bytes 786436
  319.0 5.9 %copy-start.9 = (bf16[2,128,256]{2,1,0:T(8,128)(2,1)S(1)}, bf16[2,128,256]{2,1,0:T(8,128)(2,1)}, u32[]{:S(2)}) copy-start(bf16[2,128,256]{2,1,0:T(8,128)(2,1)} %get-tuple-element.91) | copy-start | bytes 393220
  321.7 6.8 %copy-start.4 = (bf16[256,1024]{1,0:T(8,128)(2,1)S(1)}, bf16[256,1024]{1,0:T(8,128)(2,1)}, u32[]{:S(2)}) copy-start(bf16[256,1024]{1,0:T(8,128)(2,1)} %get-tuple-element.84) | copy-start | bytes 1572868
  323.2 6.0 %copy-start.3 = (bf16[256,1024]{1,0:T(8,128)(2,1)S(1)}, bf16[256,1024]{1,0:T(8,128)(2,1)}, u32[]{:S(2)}) copy-start(bf16[256,1024]{1,0:T(8,128)(2,1)} %get-tuple-element.87) | copy-start | bytes 1572868
  323.3 6.8 %copy-start.2 = (f32[128,1024]{1,0:T(8,128)S(1)}, f32[128,1024]{1,0:T(8,128)}, u32[]{:S(2)}) copy-start(f32[128,1024]{1,0:T(8,128)} %get-tuple-element.88) | copy-start | bytes 1572868
  324.1 6.8 %copy-start.10 = (f32[128,128]{1,0:T(8,128)S(1)}, f32[128,128]{1,0:T(8,128)}, u32[]{:S(2)}) copy-start(f32[128,128]{1,0:T(8,128)} %get-tuple-element.130) | copy-start | bytes 196612
